TPU v7x, 32 devices: a whole 2x2x4 slice. The times are simulated.
32 devices in a mesh: tm: 16 (over z, x, core), chan: 2 (over y).
Axes of the slice: x: 2, y: 2, z: 4, core: 2. Of those that a mesh axis runs over, the one named last changes fastest.
Arguments:
- raw_traces: bfloat16 [1280, 65536], P('chan', 'tm'), may hold values from -120 to 120
- fir_taps: bfloat16 [128], replicated, may hold values from -0.5 to 0.5
- sources: int32 [512], replicated, may hold values from 0 to 1279, as said below
- dead_flags: int32 [1280], P('chan'), may hold values 0 or 1
Outputs:
- correlations: float32 [512, 8, 1280], P('tm', None, 'chan')
Inputs may be any that keep to these rules, and one draw needn't show every extreme that they name: `sources`: 512 distinct channel indices; no group of 640 channels that share c // 640 holds more than 384 of them, and one group holds exactly 384.
All inputs are finite; a program needn't handle non-finite values. No bound on the sum of `dead_flags` on one device may be relied on, other than what follows from the above.
Results may differ from a plain program's by a relative error of at most 0.013.
Values may be sent and summed in bfloat16 or wider, within the bound.
No kernel may reach another device: no remote copies, remote signals or barrier semaphores. Data moves between devices by JAX's collectives and lax.ppermute only.
A program may use at most 64 MiB of HBM per device.

v0:
```python
import math

import jax
import jax.numpy as jnp
from jax import lax
from jax.sharding import PartitionSpec as P

VS = 512
TD = 256
NWIN = 4
NLAG = 8
HW = 32
TAPS = 128
DECIM = 4


def from_behind(value, axis, steps):
    count = lax.axis_size(axis)
    initial, last = (max(0, -steps), min(count, count - steps))
    return lax.ppermute(value, axis, [(source, source + steps) for source in range(initial, last)])


def fir_rows(fir_taps, out_block):
    width = TAPS + DECIM * out_block
    padded_taps = jnp.concatenate(
        [
            jnp.zeros((1,), jnp.bfloat16),
            fir_taps,
            jnp.zeros((width + DECIM - TAPS - 1,), jnp.bfloat16),
        ]
    )
    return jnp.tile(padded_taps, out_block)[: out_block * width].reshape(out_block, width)


def dft_table():
    time_index = jnp.arange(TD)[:, None]
    freq_index = jnp.arange(TD // 2)[None, :]
    phase = time_index * freq_index % TD
    angles = 2.0 * math.pi / TD * phase.astype(jnp.float32)
    return jnp.concatenate([jnp.cos(angles), -jnp.sin(angles)], axis=1).astype(jnp.bfloat16)


def lag_tables():
    lag_shift = jnp.arange(NLAG) - NLAG // 2
    freq_index = jnp.arange(TD // 2)
    phase = lag_shift[:, None] * freq_index[None, :] % TD
    angles = 2.0 * math.pi / TD * phase.astype(jnp.float32)
    return (jnp.cos(angles), jnp.sin(angles))


def band_matrix():
    bin_index = jnp.arange(TD // 2)
    return (jnp.abs(bin_index[:, None] - bin_index[None, :]) <= HW).astype(jnp.float32)


def whiten(spectrum, alive):
    half_bins = TD // 2
    real_part = spectrum[..., :half_bins]
    imag_part = spectrum[..., half_bins:]
    amplitude = jnp.sqrt(real_part * real_part + imag_part * imag_part)
    mean_level = jnp.einsum(
        "cwf,fg->cwg", amplitude, band_matrix(), precision=lax.Precision.HIGHEST
    ) / (2 * HW + 1)
    factor = alive / (mean_level + 1e-06)
    return (spectrum * jnp.concatenate([factor, factor], axis=-1)).astype(jnp.bfloat16)


def rotate(source, gain_scale):
    half_bins = TD // 2
    real_src = source[..., :half_bins].astype(jnp.float32)[:, None]
    imag_src = source[..., half_bins:].astype(jnp.float32)[:, None]
    cos_lag, sin_lag = lag_tables()
    cos_lag = cos_lag[None, :, None, :]
    sin_lag = sin_lag[None, :, None, :]
    real_out = (real_src * cos_lag + imag_src * sin_lag) * gain_scale
    imag_out = (imag_src * cos_lag - real_src * sin_lag) * gain_scale
    return jnp.concatenate([real_out, imag_out], axis=-1).astype(jnp.bfloat16)


def local(raw_traces, fir_taps, sources, dead_flags):
    chan_rows = raw_traces.shape[0]
    time_parts = lax.axis_size("tm")
    chan_parts = lax.axis_size("chan")
    group_index = lax.axis_index("chan")
    history = from_behind(raw_traces[:, raw_traces.shape[1] - TAPS :], "tm", 1)
    out_block = min(128, raw_traces.shape[1] // DECIM)
    sample_block = DECIM * out_block
    grouped = raw_traces.reshape(chan_rows, -1, sample_block)
    before = jnp.concatenate([history[:, None, :], grouped[:, :-1, sample_block - TAPS :]], axis=1)
    window = jnp.concatenate([before, grouped], axis=2).reshape(-1, TAPS + sample_block)
    dec = jnp.dot(window, fir_rows(fir_taps, out_block).T, preferred_element_type=jnp.float32)
    dec = dec.astype(jnp.bfloat16).reshape(chan_rows, -1)
    spectrum = jnp.dot(
        dec.reshape(-1, TD), dft_table(), preferred_element_type=jnp.float32
    ).reshape(chan_rows, -1, TD)
    alive = (1 - dead_flags).astype(jnp.float32)[:, None, None]
    whitened = whiten(spectrum, alive)
    white_flat = whitened.reshape(chan_rows, -1)
    first_chan = group_index * chan_rows
    most_rows = min(2 * VS // chan_parts, VS * 3 // 4)
    group = sources // chan_rows
    same_group = group[:, None] == group[None, :]
    earlier = jnp.arange(VS)[None, :] < jnp.arange(VS)[:, None]
    slot_rank = jnp.sum((same_group & earlier).astype(jnp.int32), axis=1)
    slot_owner = (
        (slot_rank[None, :] == jnp.arange(most_rows)[:, None]) & (group == group_index)[None, :]
    ).astype(jnp.bfloat16)
    chan_match = (sources[:, None] - first_chan == jnp.arange(chan_rows)[None, :]).astype(
        jnp.bfloat16
    )
    selector = jnp.dot(slot_owner, chan_match, preferred_element_type=jnp.float32).astype(
        jnp.bfloat16
    )
    src_panel = jnp.dot(selector, white_flat, preferred_element_type=jnp.float32).astype(
        jnp.bfloat16
    )
    gathered = lax.all_gather(src_panel, "chan", axis=0, tiled=True)
    row_pick = (
        (group * most_rows + slot_rank)[:, None] == jnp.arange(chan_parts * most_rows)[None, :]
    ).astype(jnp.bfloat16)
    source = jnp.dot(row_pick, gathered, preferred_element_type=jnp.float32).astype(jnp.bfloat16)
    gain_scale = 1.0 / math.sqrt(time_parts * NWIN * TD)
    lagged = rotate(source.reshape(VS, -1, TD), gain_scale).reshape(VS * NLAG, -1)
    stacked = lax.psum_scatter(
        lax.dot_general(
            lagged, white_flat, (((1,), (1,)), ((), ())), preferred_element_type=jnp.float32
        ).astype(jnp.bfloat16),
        "tm",
        scatter_dimension=0,
        tiled=True,
    ).astype(jnp.float32)
    return stacked.reshape(-1, NLAG, chan_rows)


def solution(mesh):
    return jax.shard_map(
        local,
        mesh=mesh,
        in_specs=(P("chan", "tm"), P(), P(), P("chan")),
        out_specs=P("tm", None, "chan"),
        check_vma=False,
    )
```

profile of v0, /device:TPU:0, one launch (start us, length us, event | category | flops | bytes accessed | tf_op | source)
XLA Modules:
  0.0 191.5 jit_solution(3498819078673920567)
XLA Ops:
  6.5 0.9 slice.21
  7.5 2.4 %collective-permute-start = (bf16[640,128]{1,0:T(8,128)(2,1)S(1)}, bf16[640,128]{1,0:T(8,128)(2,1)S(1)}, u32[]{:S(2)}, u32[]{:S(2)}) collective-permute-start(bf16[640,128]{1,0:T(8,128)(2,1)S(1)} %slice.21), channel_id=1, source_target_pairs={{0,2},{2,4},{4,6},{6,8},{8,10},{10,12},{12,14},{14,16},{16,18},{18... | collective-permute-start | bytes 491528 | tf_op jit(solution)/shard_map/ppermute | solution.py:20
  9.8 0.5 negate_convert_fusion
  10.4 0.7 broadcast_compare_fusion
  11.1 0.7 broadcast_subtract_fusion
  11.8 0.7 subtract_convert_fusion
  12.5 0.7 pad_maximum_fusion
  13.2 8.9 %concatenate.27 = bf16[5120,512]{1,0:T(8,128)(2,1)} reshape(bf16[640,4096]{1,0:T(8,128)(2,1)} %param.4) | data formatting | bytes 10485760 | tf_op jit(solution)/shard_map/concatenate | solution.py:90
  22.2 0.4 tile.10
  22.5 0.1 reshape.99
  22.7 6.2 %copy.15 = bf16[80,8,8,512]{3,2,1,0:T(8,128)(2,1)S(1)} copy(bf16[80,8,8,512]{3,1,2,0:T(8,128)(2,1)} %bitcast.24) | data formatting | bytes 10485760
  28.9 0.2 slice.28
  29.0 0.2 convert_reduce_fusion
  29.3 0.3 copy.11
  29.6 0.7 maximum_bitcast_fusion.1
  30.3 2.1 %fusion.4 = bf16[5120,128]{1,0:T(8,128)(2,1)S(1)} fusion(bf16[128,640]{1,0:T(8,128)(2,1)S(1)} %reshape.99, bf16[5120,512]{1,0:T(8,128)(2,1)S(1)} %bitcast.28, bf16[5120,128]{1,0:T(8,128)(2,1)S(1)} %maximum_bitcast_fusion.1), kind=kOutput, calls=%fused_computation.8 | convolution fusion | flops 852623360 | bytes 8028160 | tf_op jit(solution)/shard_map/dot_general | solution.py:91
  32.4 0.9 dot_general.25
  33.3 0.5 fusion.15
  33.8 1.4 fusion.11
  35.2 0.3 fusion.7
  35.5 2.2 %convolution_convert_fusion.1 = bf16[384,1024]{1,0:T(8,128)(2,1)} fusion(bf16[640,1024]{0,1:T(8,128)(2,1)S(1)} %bitcast.29, s32[512]{0:T(512)S(1)} %broadcast_subtract_fusion, s32[512]{0:T(512)S(1)} %convert_reduce_fusion, pred[512]{0:T(512)(128)(4,1)S(1)} %get-tuple-element.5), kind=kOutput, calls=%fused_computation.17 | convolution fusion | flops 756334592 | bytes 2101760 | tf_op jit(solution)/shard_map/dot_general | solution.py:114
  37.8 0.2 reduce-scatter.2.cloned.1.call-start
  38.1 29.6 %all-gather.2.cloned.1.call-done = bf16[768,1024]{1,0:T(8,128)(2,1)} async-done(((bf16[384,1024]{1,0:T(8,128)(2,1)}), bf16[768,1024]{1,0:T(8,128)(2,1)}) %all-gather.2.cloned.1.call-update) | async-done | bytes 1572880 | tf_op jit(solution)/shard_map/all_gather | solution.py:117
  67.7 2.4 %fusion.9 = bf16[512,1024]{1,0:T(8,128)(2,1)S(1)} fusion(bf16[768,1024]{1,0:T(8,128)(2,1)} %all-gather.2.cloned.1.call-done, s32[512]{0:T(512)S(1)} %multiply_add_fusion), kind=kOutput, calls=%fused_computation.13 | convolution fusion | flops 806223872 | bytes 2623488 | tf_op jit(solution)/shard_map/dot_general | solution.py:121
  70.1 0.8 reshape.101
  70.9 0.3 slice_convert_fusion.1
  71.2 5.5 %multiply_convert_fusion.1 = (bf16[512,8,4,128]{3,2,1,0:T(4,128)(2,1)S(1)}, bf16[512,8,4,128]{3,2,1,0:T(4,128)(2,1)S(1)}) fusion(f32[8,128]{1,0:T(8,128)S(1)} %get-tuple-element.12, f32[512,4,128]{2,1,0:T(4,128)S(1)} %get-tuple-element.10, f32[8,128]{1,0:T(8,128)S(1)} %get-tuple-element.11, f32[512,4,128]{2,1,0:T(4,128)S(1)} %get-tuple-element.9), kind=kLoop, calls=%fused_computation.2 | loop fusion | flops 20971520 | bytes 10493952 | tf_op jit(solution)/shard_map/convert.1
  76.7 6.6 %maximum_bitcast_fusion = bf16[512,8,4,256]{3,2,1,0:T(4,128)(2,1)} fusion(bf16[512,8,4,128]{3,2,1,0:T(4,128)(2,1)S(1)} %get-tuple-element.8, bf16[512,8,4,128]{3,2,1,0:T(4,128)(2,1)S(1)} %get-tuple-element.7), kind=kLoop, calls=%fused_computation | loop fusion | flops 16777216 | bytes 16777216
  83.3 9.4 %copy.16 = bf16[512,8,4,256]{3,1,2,0:T(8,128)(2,1)} copy(bf16[512,8,4,256]{3,2,1,0:T(4,128)(2,1)} %maximum_bitcast_fusion) | data formatting | bytes 16777216
  92.7 11.5 %convolution_convert_fusion = bf16[4096,640]{1,0:T(8,128)(2,1)} fusion(bf16[4096,1024]{1,0:T(8,128)(2,1)} %bitcast.25, bf16[640,1024]{0,1:T(8,128)(2,1)S(1)} %bitcast.30), kind=kOutput, calls=%fused_computation.7 | convolution fusion | flops 5371330560 | bytes 14942208 | tf_op jit(solution)/shard_map/dot_general | solution.py:125
  104.2 78.6 %reduce-scatter.2.cloned.1.call-done = bf16[256,640]{1,0:T(8,128)(2,1)} async-done(((bf16[4096,640]{1,0:T(8,128)(2,1)}), bf16[256,640]{1,0:T(8,128)(2,1)}) %reduce-scatter.2.cloned.1.call-update) | async-done | bytes 327696 | tf_op jit(solution)/shard_map/reduce_scatter | solution.py:124
  182.8 1.9 bitcast_convert_fusion
  (15 shorter events, 0.2 us)
Async XLA Ops:
  6.5 61.2 %all-gather.2.cloned.1.call-start = ((), (), s32[]{:S(2)}) async-start(), calls=%async_computation.1 | async-start | bytes 2359296 | tf_op jit(solution)/shard_map/all_gather | solution.py:117
  7.5 21.8 %collective-permute-start = (bf16[640,128]{1,0:T(8,128)(2,1)S(1)}, bf16[640,128]{1,0:T(8,128)(2,1)S(1)}, u32[]{:S(2)}, u32[]{:S(2)}) collective-permute-start(bf16[640,128]{1,0:T(8,128)(2,1)S(1)} %slice.21), channel_id=1, source_target_pairs={{0,2},{2,4},{4,6},{6,8},{8,10},{10,12},{12,14},{14,16},{16,18},{18... | collective-permute-start | bytes 491528 | tf_op jit(solution)/shard_map/ppermute | solution.py:20
  22.7 7.6 %slice-start = ((s8[5242880]{0:T(1024)(128)(4,1)}), s8[4194304]{0:T(1024)(128)(4,1)S(1)}, s32[]{:S(2)}) async-start(s8[5242880]{0:T(1024)(128)(4,1)} %bitcast.27), calls=%async_computation.3 | async-start | bytes 8388608
  22.7 7.6 %slice-start.1 = ((s8[5242880]{0:T(1024)(128)(4,1)}), s8[1048576]{0:T(1024)(128)(4,1)S(1)}, s32[]{:S(2)}) async-start(s8[5242880]{0:T(1024)(128)(4,1)} %bitcast.27), calls=%async_computation.4 | async-start | bytes 2097152
  37.8 145.1 %reduce-scatter.2.cloned.1.call-start = ((), (), s32[]{:S(2)}) async-start(), calls=%async_computation.2 | async-start | bytes 5570560 | tf_op jit(solution)/shard_map/reduce_scatter | solution.py:124
Sparse Core Ops, SparseCore 0:
  37.9 29.7 all-gather.1
  104.3 78.4 reduce-scatter.1
where the time goes:
time: 192 us
  waiting for transfers between devices  108 us (56%)
  local copies, waits for them, and re-layouts  28 us (15%)
  matrix products  20.2 us (11%)
  other arithmetic  19 us (10%)
  between operations  13.6 us (7%)
  starting transfers between devices  2.59 us (1%)
    reduce_scatter x1, waiting for transfers between devices, local(): lax.psum_scatter(lax.dot_general(lagged, white_flat, (((1,), (1,)), ((),...  78.6 us
    all_gather x1, waiting for transfers between devices, local(): gathered = lax.all_gather(src_panel, 'chan', axis=0, tiled=True)  29.6 us
    unnamed x6, local copies, waits for them, and re-layouts  15.5 us
    dot_general x1, matrix products, local(): lax.dot_general(lagged, white_flat, (((1,), (1,)), ((), ())), preferred_e...  11.5 us
    concatenate x1, local copies, waits for them, and re-layouts, local(): jnp.concatenate([before, grouped], axis=2).reshape(-1, TAPS + sample_block)  8.93 us
    unnamed x2, other arithmetic  6.63 us
    another operation x2, other arithmetic  6.01 us
  transfers between devices with their start and end apart: 3, of which 2 were waited for; matrix products, arithmetic and copies ran while one was open for 10% of the time, Pallas kernels for 0%

commit v1 on v0

v1 whole, which is shorter than its diff:
```python
import functools
import math

import jax
import jax.numpy as jnp
import numpy as np
from jax import lax
from jax.experimental import pallas as pl
from jax.experimental.pallas import tpu as pltpu
from jax.sharding import PartitionSpec as P

VS = 512
TD = 256
HALF = TD // 2
NLAG = 8
HW = 32
TAPS = 128
DECIM = 4
SPAN = DECIM * TD
VMEM_LIMIT = 50 * 1024 * 1024
CHUNKS = (8, 8, 8, 8)
ROW_BLOCK = 320

VMEM = pl.BlockSpec(memory_space=pltpu.VMEM)
ANY = pl.BlockSpec(memory_space=pl.ANY)


def params():
    return pltpu.CompilerParams(vmem_limit_bytes=VMEM_LIMIT)


def cost(flops, nbytes):
    return pl.CostEstimate(flops=int(flops), bytes_accessed=int(nbytes), transcendentals=0)


def swap(value, axis, bit):
    return lax.ppermute(value, axis, [(i, i ^ bit) for i in range(lax.axis_size(axis))])


def dft_table():
    phase = np.arange(TD)[:, None] * np.arange(HALF)[None, :] % TD
    angles = np.float32(2.0 * math.pi / TD) * phase.astype(np.float32)
    return np.concatenate([np.cos(angles), -np.sin(angles)], axis=1).astype(jnp.bfloat16)


def lag_tables(gain):
    phase = (np.arange(NLAG) - NLAG // 2)[:, None] * np.arange(HALF)[None, :] % TD
    angles = 2.0 * math.pi / TD * phase.astype(np.float64)
    return (gain * np.cos(angles)).astype(np.float32), (gain * np.sin(angles)).astype(np.float32)


def band_table():
    bins = np.arange(HALF)
    band = (np.abs(bins[:, None] - bins[None, :]) <= HW).astype(np.float32)
    return np.concatenate([band, band], axis=0).astype(jnp.bfloat16)


def fir_base(fir_taps):
    rows = TAPS // DECIM
    width = 2 * TAPS
    padded = jnp.concatenate(
        [jnp.zeros((1,), jnp.bfloat16), fir_taps, jnp.zeros((width + DECIM - TAPS - 1,), jnp.bfloat16)]
    )
    return jnp.tile(padded, rows)[: rows * width].reshape(rows, width)


def nt_dot(left, right):
    return lax.dot_general(left, right, (((1,), (1,)), ((), ())), preferred_element_type=jnp.float32)


def fill_fir(base_ref, fir_ref):
    rows = TAPS // DECIM
    fir_ref[...] = jnp.zeros_like(fir_ref)
    for i in range(TD // rows):
        fir_ref[rows * i : rows * (i + 1), TAPS * i : TAPS * (i + 2)] = base_ref[...]


def whiten_rows(samples, fir_ref, table_ref, band_ref, alive):
    dec = nt_dot(samples, fir_ref[...]).astype(jnp.bfloat16)
    spectrum = jnp.dot(dec, table_ref[...], preferred_element_type=jnp.float32)
    real_part = spectrum[:, :HALF]
    imag_part = spectrum[:, HALF:]
    amplitude = jnp.sqrt(real_part * real_part + imag_part * imag_part)
    high = amplitude.astype(jnp.bfloat16)
    low = (amplitude - high.astype(jnp.float32)).astype(jnp.bfloat16)
    total = jnp.dot(
        jnp.concatenate([high, low], axis=1), band_ref[...], preferred_element_type=jnp.float32
    )
    factor = alive / (total * (1.0 / (2 * HW + 1)) + 1e-06)
    return jnp.concatenate([real_part * factor, imag_part * factor], axis=1).astype(jnp.bfloat16)


def late_kernel(row_block, raw_ref, base_ref, table_ref, band_ref, alive_ref, out_ref, fir_ref, held_ref, sems):
    windows = out_ref.shape[1] // TD
    rows = raw_ref.shape[0]
    first = SPAN - TAPS
    copies = []
    for w in range(windows):
        start = 0 if w == 0 else TAPS + w * SPAN
        stop = TAPS + (w + 1) * SPAN
        copy = pltpu.make_async_copy(
            raw_ref.at[:, first + start : first + stop], held_ref.at[:, start:stop], sems.at[w]
        )
        copy.start()
        copies.append(copy)
    fill_fir(base_ref, fir_ref)
    for w in range(windows):
        copies[w].wait()
        for r in range(0, rows, row_block):
            part = pl.ds(r, row_block)
            out_ref[part, w * TD : (w + 1) * TD] = whiten_rows(
                held_ref[part, w * SPAN : (w + 1) * SPAN + TAPS],
                fir_ref, table_ref, band_ref, alive_ref[part, :],
            )


def first_kernel(
    row_block, sizes, raw_ref, hist_ref, base_ref, table_ref, band_ref, alive_ref, late_ref, sel_ref, *refs
):
    panels = refs[: 2 * len(sizes)]
    white_ref, fir_ref, held_ref, sem = refs[2 * len(sizes) :]
    rows = raw_ref.shape[0]
    copy = pltpu.make_async_copy(raw_ref.at[:, :SPAN], held_ref, sem)
    copy.start()
    fill_fir(base_ref, fir_ref)
    white_ref[:, TD:] = late_ref[...]
    copy.wait()
    for r in range(0, rows, row_block):
        part = pl.ds(r, row_block)
        samples = jnp.concatenate([hist_ref[part, :], held_ref[part, :]], axis=1)
        white_ref[part, :TD] = whiten_rows(samples, fir_ref, table_ref, band_ref, alive_ref[part, :])
    row = 0
    for panel in panels:
        count = panel.shape[0]
        panel[...] = jnp.dot(
            sel_ref[row : row + count, :], white_ref[...], preferred_element_type=jnp.float32
        ).astype(jnp.bfloat16)
        row += count


def main_kernel(own_ref, own_in_ref, sib_ref, sib_in_ref, white_ref, white_sib_ref, cos_ref, sin_ref, keep_ref, send_ref, lag_ref):
    count, depth = own_ref.shape
    cos_lag = cos_ref[...][None]
    sin_lag = sin_ref[...][None]
    for side, (a_ref, b_ref) in enumerate(((own_ref, own_in_ref), (sib_ref, sib_in_ref))):
        for w in range(0, depth, TD):
            parts = []
            for k in (w, w + HALF):
                parts.append(a_ref[:, k : k + HALF].astype(jnp.float32) + b_ref[:, k : k + HALF].astype(jnp.float32))
            real_src, imag_src = (part[:, None, :] for part in parts)
            real_out = real_src * cos_lag + imag_src * sin_lag
            imag_out = imag_src * cos_lag - real_src * sin_lag
            k = side * depth + w
            lag_ref[:, k : k + HALF] = real_out.reshape(count * NLAG, HALF).astype(jnp.bfloat16)
            lag_ref[:, k + HALF : k + TD] = imag_out.reshape(count * NLAG, HALF).astype(jnp.bfloat16)
    white = jnp.concatenate([white_ref[...], white_sib_ref[...]], axis=1)
    half = keep_ref.shape[0]
    send_ref[...] = nt_dot(lag_ref[half:, :], white).astype(jnp.bfloat16)
    keep_ref[...] = nt_dot(lag_ref[:half, :], white)


def add_kernel(keep_ref, recv_ref, kept_ref, send_ref):
    half = kept_ref.shape[0]
    kept_ref[...] = keep_ref[:half, :] + recv_ref[:half, :].astype(jnp.float32)
    send_ref[...] = (keep_ref[half:, :] + recv_ref[half:, :].astype(jnp.float32)).astype(jnp.bfloat16)


def last_kernel(*refs):
    out_ref = refs[-1]
    row = 0
    for keep_ref, recv_ref in zip(refs[:-1:2], refs[1:-1:2]):
        count = keep_ref.shape[0]
        out_ref[row : row + count, :] = keep_ref[...] + recv_ref[...].astype(jnp.float32)
        row += count


def local(raw_traces, fir_taps, sources, dead_flags):
    rows, samples = raw_traces.shape
    windows = samples // SPAN
    depth = windows * TD
    late = windows - 1
    time_parts = lax.axis_size("tm")
    chan_parts = lax.axis_size("chan")
    me = lax.axis_index("tm")
    per_dest = VS // time_parts
    bits = [1 << i for i in range(1, time_parts.bit_length() - 1)]
    scale = per_dest / sum(CHUNKS)
    sizes = [int(size * scale) for size in CHUNKS]

    history = lax.ppermute(
        raw_traces[:, samples - TAPS :], "tm", [(i, i + 1) for i in range(time_parts - 1)]
    )

    relative, offset = [], []
    begin = 0
    for size in sizes:
        for core in (0, 1):
            for code in range(time_parts // 2):
                rel = core
                for place, bit in enumerate(bits):
                    rel += bit * (code >> (len(bits) - 1 - place) & 1)
                relative += [rel] * size
                offset += list(range(begin, begin + size))
        begin += size
    wanted = per_dest * jnp.bitwise_xor(me, np.array(relative, np.int32)) + np.array(offset, np.int32)
    ordered = jnp.sum(jnp.where(wanted[:, None] == jnp.arange(VS)[None, :], sources[None, :], 0), axis=1)
    place = ordered - lax.axis_index("chan") * rows
    selector = (place[:, None] == jnp.arange(rows)[None, :]).astype(jnp.bfloat16)

    alive = jnp.broadcast_to((1 - dead_flags).astype(jnp.float32)[:, None], (rows, HALF))
    base = fir_base(fir_taps)
    table = jnp.asarray(dft_table())
    band = jnp.asarray(band_table())
    row_block = ROW_BLOCK if rows % ROW_BLOCK == 0 else rows
    fir_scratch = pltpu.VMEM((TD, SPAN + TAPS), jnp.bfloat16)
    fir_flops = 2 * rows * TD * (SPAN + TAPS + TD + HALF)

    late_white = pl.pallas_call(
        functools.partial(late_kernel, row_block),
        out_shape=jax.ShapeDtypeStruct((rows, late * TD), jnp.bfloat16),
        in_specs=[ANY] + [VMEM] * 4,
        out_specs=VMEM,
        scratch_shapes=[
            fir_scratch,
            pltpu.VMEM((rows, late * SPAN + TAPS), jnp.bfloat16),
            pltpu.SemaphoreType.DMA((late,)),
        ],
        compiler_params=params(),
        cost_estimate=cost(fir_flops * late, 2 * rows * samples),
        name="late_windows",
    )(raw_traces, base, table, band, alive)

    panel_shapes = []
    for size in sizes:
        panel_shapes += [jax.ShapeDtypeStruct((size * time_parts // 2, depth), jnp.bfloat16)] * 2
    *panels, white = pl.pallas_call(
        functools.partial(first_kernel, row_block, sizes),
        out_shape=panel_shapes + [jax.ShapeDtypeStruct((rows, depth), jnp.bfloat16)],
        in_specs=[ANY] + [VMEM] * 7,
        out_specs=[VMEM] * (len(panel_shapes) + 1),
        scratch_shapes=[fir_scratch, pltpu.VMEM((rows, SPAN), jnp.bfloat16), pltpu.SemaphoreType.DMA],
        compiler_params=params(),
        cost_estimate=cost(fir_flops + 2 * VS * rows * depth, 2 * (rows * SPAN + (rows + VS) * depth)),
        name="first_window",
    )(raw_traces, history, base, table, band, alive, late_white, selector)

    def across(panel):
        if chan_parts == 2:
            return swap(panel, "chan", 1)
        return lax.psum(panel, "chan") - panel

    cos_lag, sin_lag = (jnp.asarray(t) for t in lag_tables(1.0 / math.sqrt(time_parts * depth)))
    white_sib = None
    finals = []
    for q, size in enumerate(sizes):
        own, other = panels[2 * q : 2 * q + 2]
        own_in = across(own)
        sib = swap(other, "tm", 1)
        sib_in = across(sib)
        if white_sib is None:
            white_sib = swap(white, "tm", 1)
        count = own.shape[0]
        half = count * NLAG // 2
        keep, send = pl.pallas_call(
            main_kernel,
            out_shape=[
                jax.ShapeDtypeStruct((half, rows), jnp.float32),
                jax.ShapeDtypeStruct((half, rows), jnp.bfloat16),
            ],
            in_specs=[VMEM] * 8,
            out_specs=[VMEM] * 2,
            scratch_shapes=[pltpu.VMEM((count * NLAG, 2 * depth), jnp.bfloat16)],
            compiler_params=params(),
            cost_estimate=cost(2 * 2 * half * 2 * depth * rows, 4 * rows * depth + 6 * half * rows),
            name=f"product_{q}",
        )(own, own_in, sib, sib_in, white, white_sib, cos_lag, sin_lag)
        for bit in bits[:-1]:
            recv = swap(send, "tm", bit)
            half = keep.shape[0] // 2
            keep, send = pl.pallas_call(
                add_kernel,
                out_shape=[
                    jax.ShapeDtypeStruct((half, rows), jnp.float32),
                    jax.ShapeDtypeStruct((half, rows), jnp.bfloat16),
                ],
                in_specs=[VMEM] * 2,
                out_specs=[VMEM] * 2,
                compiler_params=params(),
                cost_estimate=cost(2 * half * rows, 18 * half * rows),
                name=f"add_{q}_{bit}",
            )(keep, recv)
        finals += [keep, swap(send, "tm", bits[-1])]
    stacked = pl.pallas_call(
        last_kernel,
        out_shape=jax.ShapeDtypeStruct((per_dest * NLAG, rows), jnp.float32),
        in_specs=[VMEM] * len(finals),
        out_specs=VMEM,
        compiler_params=params(),
        cost_estimate=cost(per_dest * NLAG * rows, 10 * per_dest * NLAG * rows),
        name="last_sum",
    )(*finals)
    return stacked.reshape(per_dest, NLAG, rows)


def solution(mesh):
    return jax.shard_map(
        local,
        mesh=mesh,
        in_specs=(P("chan", "tm"), P(), P(), P("chan")),
        out_specs=P("tm", None, "chan"),
        check_vma=False,
    )
```

time: 192 us -> 87.3 us (0.45)
  waiting for transfers between devices: 108 us -> 20.2 us
  starting transfers between devices: 2.59 us -> 33.8 us
  Pallas kernels: 0 us -> 26.2 us
  local copies, waits for them, and re-layouts: 28 us -> 3.19 us
  matrix products: 20.2 us -> 0 us
  other arithmetic: 19 us -> 3.24 us
  between operations: 13.6 us -> 0.23 us
    reduce_scatter x1 -> x0, waiting for transfers between devices: 78.6 us -> none  [local(): lax.psum_scatter(lax.dot_general(lagged, white_flat, (((1,), (1,)), ((),...]
    ppermute x1 -> x26, starting transfers between devices: 2.37 us -> 33.8 us  [the longest x25 31.4 us: swap(): lax.ppermute(value, axis, [(i, i ^ bit) for i in range(lax.axis_size(axis...]
    all_gather x1 -> x0, waiting for transfers between devices: 29.6 us -> none  [local(): gathered = lax.all_gather(src_panel, 'chan', axis=0, tiled=True)]
    pallas_call x0 -> x15, Pallas kernels: none -> 26.2 us  [the longest x4 14.6 us: local(): pl.pallas_call(main_kernel, out_shape=[jax.ShapeDtypeStruct((half, rows),...]
    ppermute x1 -> x26, waiting for transfers between devices: 0.01 us -> 20.2 us  [the longest x25 20.2 us: swap(): lax.ppermute(value, axis, [(i, i ^ bit) for i in range(lax.axis_size(axis...]
    dot_general x6 -> x0, matrix products: 20.2 us -> none  [the longest x1 11.5 us: local(): lax.dot_general(lagged, white_flat, (((1,), (1,)), ((), ())), preferred_e...]
    unnamed x6 -> x12, local copies, waits for them, and re-layouts: 15.5 us -> 1.91 us
    concatenate x1 -> x0, local copies, waits for them, and re-layouts: 8.93 us -> none  [local(): jnp.concatenate([before, grouped], axis=2).reshape(-1, TAPS + sample_block)]
  transfers between devices with their start and end apart: 3 -> 26, of which waited for: 2 -> 10; matrix products, arithmetic and copies ran while one was open for 10% -> 4% of each run, Pallas kernels for 0% -> 24%
where the time goes in v1:
time: 87.3 us; the launch traced here: 86.9 us
  starting transfers between devices  33.8 us (39%)
  Pallas kernels  26.2 us (30%)
  waiting for transfers between devices  20.2 us (23%)
  other arithmetic  3.24 us (4%)
  local copies, waits for them, and re-layouts  3.19 us (4%)
    ppermute x25, starting transfers between devices, swap(): lax.ppermute(value, axis, [(i, i ^ bit) for i in range(lax.axis_size(axis...  31.4 us
    ppermute x25, waiting for transfers between devices, swap(): lax.ppermute(value, axis, [(i, i ^ bit) for i in range(lax.axis_size(axis...  20.2 us
    pallas_call x4, Pallas kernels, local(): pl.pallas_call(main_kernel, out_shape=[jax.ShapeDtypeStruct((half, rows),...  14.6 us
    pallas_call x1, Pallas kernels, local(): pl.pallas_call(functools.partial(late_kernel, row_block), out_shape=jax.S...  6.01 us
    pallas_call x1, Pallas kernels, local(): pl.pallas_call(functools.partial(first_kernel, row_block, sizes), out_sha...  4.31 us
    ppermute x1, starting transfers between devices, local(): lax.ppermute(raw_traces[:, samples - TAPS:], 'tm', [(i, i + 1) for i in r...  2.37 us
    unnamed x12, local copies, waits for them, and re-layouts  1.91 us
  transfers between devices with their start and end apart: 26, of which 10 were waited for; matrix products, arithmetic and copies ran while one was open for 4% of the time, Pallas kernels for 24%

profile of v1, /device:TPU:0, one launch (start us, length us, event | category | flops | bytes accessed | tf_op | source)
XLA Modules:
  0.0 86.9 jit_solution(13730740884444021690)
XLA Ops:
  0.0 1.0 %slice.6 = bf16[640,128]{1,0:T(8,128)(2,1)S(1)} slice(bf16[640,4096]{1,0:T(8,128)(2,1)} %raw_ref.3), slice={[0:640], [3968:4096]} | slice | bytes 327680 | tf_op jit(solution)/shard_map/slice | solution.py:191
  1.0 2.4 %collective-permute-start = (bf16[640,128]{1,0:T(8,128)(2,1)S(1)}, bf16[640,128]{1,0:T(8,128)(2,1)S(1)}, u32[]{:S(2)}, u32[]{:S(2)}) collective-permute-start(bf16[640,128]{1,0:T(8,128)(2,1)S(1)} %slice.6), channel_id=1, source_target_pairs={{0,2},{2,4},{4,6},{6,8},{8,10},{10,12},{12,14},{14,16},{16,18},{18... | collective-permute-start | bytes 491528 | tf_op jit(solution)/shard_map/ppermute | solution.py:190
  4.7 0.9 %select_reduce_fusion = s32[512]{0:T(512)S(1)} fusion(s32[512]{0:T(512)} %param.12, s32[512]{0:T(512)S(1)} %multiply_add_fusion), kind=kLoop, calls=%fused_computation.2 | loop fusion | flops 785920 | bytes 6144 | tf_op jit(solution)/shard_map/reduce_sum | solution.py:206
  7.0 6.0 %late_windows.1.late_ref = bf16[640,768]{1,0:T(8,128)(2,1)S(1)} custom-call(bf16[640,4096]{1,0:T(8,128)(2,1)} %raw_ref.3, bf16[32,256]{1,0:T(8,128)(2,1)S(1)} %reshape.13.base_ref, bf16[256,256]{1,0:T(8,128)(2,1)S(1)} %copy-done, bf16[256,128]{1,0:T(8,128)(2,1)S(1)} %copy-done.1, f32[640,128]{1,0:T(8,128)S(1)} %broadcast_in_dim.17.alive_ref), custom_call_target="tpu_custom_call" | custom-call | flops 1509949440 | bytes 5242880 | tf_op jit(solution)/shard_map/late_windows/pallas_call | solution.py:218
  13.0 4.3 %first_window.1 = (bf16[64,1024]{1,0:T(8,128)(2,1)S(1)}, bf16[64,1024]{1,0:T(8,128)(2,1)S(1)}, bf16[64,1024]{1,0:T(8,128)(2,1)S(1)}, bf16[64,1024]{1,0:T(8,128)(...) custom-call(bf16[640,4096]{1,0:T(8,128)(2,1)} %raw_ref.3, ...), custom_call_target="tpu_custom_call" | custom-call | flops 1174405120 | bytes 3670016 | tf_op jit(solution)/shard_map/first_window/pallas_call | solution.py:236
  17.4 2.7 %collective-permute-start.4 = (bf16[640,1024]{1,0:T(8,128)(2,1)}, bf16[640,1024]{1,0:T(8,128)(2,1)S(1)}, u32[]{:S(2)}, u32[]{:S(2)}) collective-permute-start(bf16[640,1024]{1,0:T(8,128)(2,1)} %get-tuple-element.40.white_ref), channel_id=1, source_target_pairs={{0,2},{2,0},{4,6},{6,4},{8,10},{10,8},{12,14},{14,12},{16,18},{18,... | collective-permute-start | bytes 3932168 | tf_op jit(solution)/shard_map/ppermute | solution.py:37
  20.1 1.5 %collective-permute-start.20 = (bf16[64,1024]{1,0:T(8,128)(2,1)S(1)}, bf16[64,1024]{1,0:T(8,128)(2,1)S(1)}, u32[]{:S(2)}, u32[]{:S(2)}) collective-permute-start(bf16[64,1024]{1,0:T(8,128)(2,1)S(1)} %get-tuple-element.63.own_ref), channel_id=1, source_target_pairs={{0,1},{1,0},{2,3},{3,2},{4,5},{5,4},{6,7},{7,6},{8,9},{9,8},{10,11... | collective-permute-start | bytes 393224 | tf_op jit(solution)/shard_map/ppermute | solution.py:37
  22.7 1.5 %collective-permute-start.22 = (bf16[64,1024]{1,0:T(8,128)(2,1)S(1)}, bf16[64,1024]{1,0:T(8,128)(2,1)S(1)}, u32[]{:S(2)}, u32[]{:S(2)}) collective-permute-start(bf16[64,1024]{1,0:T(8,128)(2,1)S(1)} %collective-permute-done.21.sib_ref), channel_id=1, source_target_pairs={{0,1},{1,0},{2,3},{3,2},{4,5},{5,4},{6,7},{7,6},{8,9},{9,8},{10,11... | collective-permute-start | bytes 393224 | tf_op jit(solution)/shard_map/ppermute | solution.py:37
  24.3 2.1 %collective-permute-done.20.own_in_ref = bf16[64,1024]{1,0:T(8,128)(2,1)S(1)} collective-permute-done((bf16[64,1024]{1,0:T(8,128)(2,1)S(1)}, bf16[64,1024]{1,0:T(8,128)(2,1)S(1)}, u32[]{:S(2)}, u32[]{:S(2)}) %collective-permute-start.20) | collective-permute-done | bytes 131104 | tf_op jit(solution)/shard_map/ppermute | solution.py:37
  26.4 1.5 %collective-permute-start.14 = (bf16[64,1024]{1,0:T(8,128)(2,1)S(1)}, bf16[64,1024]{1,0:T(8,128)(2,1)S(1)}, u32[]{:S(2)}, u32[]{:S(2)}) collective-permute-start(bf16[64,1024]{1,0:T(8,128)(2,1)S(1)} %get-tuple-element.55.own_ref), channel_id=1, source_target_pairs={{0,1},{1,0},{2,3},{3,2},{4,5},{5,4},{6,7},{7,6},{8,9},{9,8},{10,11... | collective-permute-start | bytes 393224 | tf_op jit(solution)/shard_map/ppermute | solution.py:37
  29.2 1.5 %collective-permute-start.8 = (bf16[64,1024]{1,0:T(8,128)(2,1)S(1)}, bf16[64,1024]{1,0:T(8,128)(2,1)S(1)}, u32[]{:S(2)}, u32[]{:S(2)}) collective-permute-start(bf16[64,1024]{1,0:T(8,128)(2,1)S(1)} %get-tuple-element.47.own_ref), channel_id=1, source_target_pairs={{0,1},{1,0},{2,3},{3,2},{4,5},{5,4},{6,7},{7,6},{8,9},{9,8},{10,11... | collective-permute-start | bytes 393224 | tf_op jit(solution)/shard_map/ppermute | solution.py:37
  31.8 1.3 %copy-done.2 = bf16[640,1024]{1,0:T(8,128)(2,1)S(1)} copy-done((bf16[640,1024]{1,0:T(8,128)(2,1)S(1)}, bf16[640,1024]{1,0:T(8,128)(2,1)}, u32[]{:S(2)}) %copy-start.2) | copy-done | bytes 1310744
  33.1 3.6 %product_3.1 = (f32[256,640]{1,0:T(8,128)S(1)}, bf16[256,640]{1,0:T(8,128)(2,1)S(1)}) custom-call(bf16[64,1024]{1,0:T(8,128)(2,1)S(1)} %get-tuple-element.63.own_ref, bf16[64,1024]{1,0:T(8,128)(2,1)S(1)} %collective-permute-done.20.own_in_ref, bf16[64,1024]{1,0:T(8,128)(2,1)S(1)} %collective-permute-done.21.sib_ref, ...), custom_call_target="tpu_custom_call" | custom-call | flops 1342177280 | bytes 3604480 | tf_op jit(solution)/shard_map/product_3/pallas_call | solution.py:264
  36.8 1.0 %collective-permute-start.1 = (bf16[64,1024]{1,0:T(8,128)(2,1)S(1)}, bf16[64,1024]{1,0:T(8,128)(2,1)S(1)}, u32[]{:S(2)}, u32[]{:S(2)}) collective-permute-start(bf16[64,1024]{1,0:T(8,128)(2,1)S(1)} %get-tuple-element.38.own_ref), channel_id=1, source_target_pairs={{0,1},{1,0},{2,3},{3,2},{4,5},{5,4},{6,7},{7,6},{8,9},{9,8},{10,11... | collective-permute-start | bytes 393224 | tf_op jit(solution)/shard_map/ppermute | solution.py:37
  37.8 1.1 %collective-permute-start.3 = (bf16[64,1024]{1,0:T(8,128)(2,1)S(1)}, bf16[64,1024]{1,0:T(8,128)(2,1)S(1)}, u32[]{:S(2)}, u32[]{:S(2)}) collective-permute-start(bf16[64,1024]{1,0:T(8,128)(2,1)S(1)} %collective-permute-done.2.sib_ref), channel_id=1, source_target_pairs={{0,1},{1,0},{2,3},{3,2},{4,5},{5,4},{6,7},{7,6},{8,9},{9,8},{10,11... | collective-permute-start | bytes 393224 | tf_op jit(solution)/shard_map/ppermute | solution.py:37
  38.9 1.5 %collective-permute-start.23 = (bf16[256,640]{1,0:T(8,128)(2,1)S(1)}, bf16[256,640]{1,0:T(8,128)(2,1)S(1)}, u32[]{:S(2)}, u32[]{:S(2)}) collective-permute-start(bf16[256,640]{1,0:T(8,128)(2,1)S(1)} %get-tuple-element.66), channel_id=1, source_target_pairs={{0,4},{2,6},{4,0},{6,2},{8,12},{10,14},{12,8},{14,10},{16,20},{18,... | collective-permute-start | bytes 983048 | tf_op jit(solution)/shard_map/ppermute | solution.py:37
  40.4 3.6 %product_2.1 = (f32[256,640]{1,0:T(8,128)S(1)}, bf16[256,640]{1,0:T(8,128)(2,1)S(1)}) custom-call(bf16[64,1024]{1,0:T(8,128)(2,1)S(1)} %get-tuple-element.55.own_ref, bf16[64,1024]{1,0:T(8,128)(2,1)S(1)} %collective-permute-done.14.own_in_ref, bf16[64,1024]{1,0:T(8,128)(2,1)S(1)} %collective-permute-done.15.sib_ref, ...), custom_call_target="tpu_custom_call" | custom-call | flops 1342177280 | bytes 3604480 | tf_op jit(solution)/shard_map/product_2/pallas_call | solution.py:264
  44.6 3.6 %product_1.1 = (f32[256,640]{1,0:T(8,128)S(1)}, bf16[256,640]{1,0:T(8,128)(2,1)S(1)}) custom-call(bf16[64,1024]{1,0:T(8,128)(2,1)S(1)} %get-tuple-element.47.own_ref, bf16[64,1024]{1,0:T(8,128)(2,1)S(1)} %collective-permute-done.8.own_in_ref, bf16[64,1024]{1,0:T(8,128)(2,1)S(1)} %collective-permute-done.9.sib_ref, ...), custom_call_target="tpu_custom_call" | custom-call | flops 1342177280 | bytes 3604480 | tf_op jit(solution)/shard_map/product_1/pallas_call | solution.py:264
  48.2 1.6 %collective-permute-start.11 = (bf16[256,640]{1,0:T(8,128)(2,1)S(1)}, bf16[256,640]{1,0:T(8,128)(2,1)S(1)}, u32[]{:S(2)}, u32[]{:S(2)}) collective-permute-start(bf16[256,640]{1,0:T(8,128)(2,1)S(1)} %get-tuple-element.50), channel_id=1, source_target_pairs={{0,4},{2,6},{4,0},{6,2},{8,12},{10,14},{12,8},{14,10},{16,20},{18,... | collective-permute-start | bytes 983048 | tf_op jit(solution)/shard_map/ppermute | solution.py:37
  49.8 3.8 %product_0.1 = (f32[256,640]{1,0:T(8,128)S(1)}, bf16[256,640]{1,0:T(8,128)(2,1)S(1)}) custom-call(bf16[64,1024]{1,0:T(8,128)(2,1)S(1)} %get-tuple-element.38.own_ref, bf16[64,1024]{1,0:T(8,128)(2,1)S(1)} %collective-permute-done.1.own_in_ref, bf16[64,1024]{1,0:T(8,128)(2,1)S(1)} %collective-permute-done.2.sib_ref, ...), custom_call_target="tpu_custom_call" | custom-call | flops 1342177280 | bytes 3604480 | tf_op jit(solution)/shard_map/product_0/pallas_call | solution.py:264
  54.2 1.6 %collective-permute-start.24 = (bf16[128,640]{1,0:T(8,128)(2,1)S(1)}, bf16[128,640]{1,0:T(8,128)(2,1)S(1)}, u32[]{:S(2)}, u32[]{:S(2)}) collective-permute-start(bf16[128,640]{1,0:T(8,128)(2,1)S(1)} %get-tuple-element.68), channel_id=1, source_target_pairs={{0,8},{2,10},{4,12},{6,14},{8,0},{10,2},{12,4},{14,6},{16,24},{18,... | collective-permute-start | bytes 491528 | tf_op jit(solution)/shard_map/ppermute | solution.py:37
  56.2 1.6 %collective-permute-start.18 = (bf16[128,640]{1,0:T(8,128)(2,1)S(1)}, bf16[128,640]{1,0:T(8,128)(2,1)S(1)}, u32[]{:S(2)}, u32[]{:S(2)}) collective-permute-start(bf16[128,640]{1,0:T(8,128)(2,1)S(1)} %get-tuple-element.60), channel_id=1, source_target_pairs={{0,8},{2,10},{4,12},{6,14},{8,0},{10,2},{12,4},{14,6},{16,24},{18,... | collective-permute-start | bytes 491528 | tf_op jit(solution)/shard_map/ppermute | solution.py:37
  57.8 5.3 %collective-permute-done.11.recv_ref = bf16[256,640]{1,0:T(8,128)(2,1)S(1)} collective-permute-done((bf16[256,640]{1,0:T(8,128)(2,1)S(1)}, bf16[256,640]{1,0:T(8,128)(2,1)S(1)}, u32[]{:S(2)}, u32[]{:S(2)}) %collective-permute-start.11) | collective-permute-done | bytes 327712 | tf_op jit(solution)/shard_map/ppermute | solution.py:37
  63.2 1.6 %collective-permute-start.12 = (bf16[128,640]{1,0:T(8,128)(2,1)S(1)}, bf16[128,640]{1,0:T(8,128)(2,1)S(1)}, u32[]{:S(2)}, u32[]{:S(2)}) collective-permute-start(bf16[128,640]{1,0:T(8,128)(2,1)S(1)} %get-tuple-element.52), channel_id=1, source_target_pairs={{0,8},{2,10},{4,12},{6,14},{8,0},{10,2},{12,4},{14,6},{16,24},{18,... | collective-permute-start | bytes 491528 | tf_op jit(solution)/shard_map/ppermute | solution.py:37
  64.8 3.3 %collective-permute-done.5.recv_ref = bf16[256,640]{1,0:T(8,128)(2,1)S(1)} collective-permute-done((bf16[256,640]{1,0:T(8,128)(2,1)S(1)}, bf16[256,640]{1,0:T(8,128)(2,1)S(1)}, u32[]{:S(2)}, u32[]{:S(2)}) %collective-permute-start.5) | collective-permute-done | bytes 327712 | tf_op jit(solution)/shard_map/ppermute | solution.py:37
  68.2 1.6 %collective-permute-start.6 = (bf16[128,640]{1,0:T(8,128)(2,1)S(1)}, bf16[128,640]{1,0:T(8,128)(2,1)S(1)}, u32[]{:S(2)}, u32[]{:S(2)}) collective-permute-start(bf16[128,640]{1,0:T(8,128)(2,1)S(1)} %get-tuple-element.44), channel_id=1, source_target_pairs={{0,8},{2,10},{4,12},{6,14},{8,0},{10,2},{12,4},{14,6},{16,24},{18,... | collective-permute-start | bytes 491528 | tf_op jit(solution)/shard_map/ppermute | solution.py:37
  69.9 2.7 %collective-permute-start.25 = (bf16[64,640]{1,0:T(8,128)(2,1)S(1)}, bf16[64,640]{1,0:T(8,128)(2,1)S(1)}, u32[]{:S(2)}, u32[]{:S(2)}) collective-permute-start(bf16[64,640]{1,0:T(8,128)(2,1)S(1)} %get-tuple-element.70), channel_id=1, source_target_pairs={{0,16},{2,18},{4,20},{6,22},{8,24},{10,26},{12,28},{14,30},{16,0},... | collective-permute-start | bytes 245768 | tf_op jit(solution)/shard_map/ppermute | solution.py:37
  73.1 2.7 %collective-permute-start.13 = (bf16[64,640]{1,0:T(8,128)(2,1)S(1)}, bf16[64,640]{1,0:T(8,128)(2,1)S(1)}, u32[]{:S(2)}, u32[]{:S(2)}) collective-permute-start(bf16[64,640]{1,0:T(8,128)(2,1)S(1)} %get-tuple-element.54), channel_id=1, source_target_pairs={{0,16},{2,18},{4,20},{6,22},{8,24},{10,26},{12,28},{14,30},{16,0},... | collective-permute-start | bytes 245768 | tf_op jit(solution)/shard_map/ppermute | solution.py:37
  75.8 2.4 %collective-permute-start.7 = (bf16[64,640]{1,0:T(8,128)(2,1)S(1)}, bf16[64,640]{1,0:T(8,128)(2,1)S(1)}, u32[]{:S(2)}, u32[]{:S(2)}) collective-permute-start(bf16[64,640]{1,0:T(8,128)(2,1)S(1)} %get-tuple-element.46), channel_id=1, source_target_pairs={{0,16},{2,18},{4,20},{6,22},{8,24},{10,26},{12,28},{14,30},{16,0},... | collective-permute-start | bytes 245768 | tf_op jit(solution)/shard_map/ppermute | solution.py:37
  78.1 3.7 %collective-permute-done.25.refs_7_ = bf16[64,640]{1,0:T(8,128)(2,1)S(1)} collective-permute-done((bf16[64,640]{1,0:T(8,128)(2,1)S(1)}, bf16[64,640]{1,0:T(8,128)(2,1)S(1)}, u32[]{:S(2)}, u32[]{:S(2)}) %collective-permute-start.25) | collective-permute-done | bytes 81952 | tf_op jit(solution)/shard_map/ppermute | solution.py:37
  81.8 1.8 %collective-permute-done.19.refs_5_ = bf16[64,640]{1,0:T(8,128)(2,1)S(1)} collective-permute-done((bf16[64,640]{1,0:T(8,128)(2,1)S(1)}, bf16[64,640]{1,0:T(8,128)(2,1)S(1)}, u32[]{:S(2)}, u32[]{:S(2)}) %collective-permute-start.19) | collective-permute-done | bytes 81952 | tf_op jit(solution)/shard_map/ppermute | solution.py:37
  83.6 1.5 %collective-permute-done.13.refs_3_ = bf16[64,640]{1,0:T(8,128)(2,1)S(1)} collective-permute-done((bf16[64,640]{1,0:T(8,128)(2,1)S(1)}, bf16[64,640]{1,0:T(8,128)(2,1)S(1)}, u32[]{:S(2)}, u32[]{:S(2)}) %collective-permute-start.13) | collective-permute-done | bytes 81952 | tf_op jit(solution)/shard_map/ppermute | solution.py:37
  (60 shorter events, 10.1 us)
Async XLA Ops:
  0.0 7.0 %copy-start = (bf16[256,256]{1,0:T(8,128)(2,1)S(1)}, bf16[256,256]{1,0:T(8,128)(2,1)}, u32[]{:S(2)}) copy-start(bf16[256,256]{1,0:T(8,128)(2,1)} %constant.34.clone.table_ref) | copy-start | bytes 393220
  0.0 7.0 %copy-start.1 = (bf16[256,128]{1,0:T(8,128)(2,1)S(1)}, bf16[256,128]{1,0:T(8,128)(2,1)}, u32[]{:S(2)}) copy-start(bf16[256,128]{1,0:T(8,128)(2,1)} %constant.35.clone.band_ref) | copy-start | bytes 196612
  1.0 12.1 %collective-permute-start = (bf16[640,128]{1,0:T(8,128)(2,1)S(1)}, bf16[640,128]{1,0:T(8,128)(2,1)S(1)}, u32[]{:S(2)}, u32[]{:S(2)}) collective-permute-start(bf16[640,128]{1,0:T(8,128)(2,1)S(1)} %slice.6), channel_id=1, source_target_pairs={{0,2},{2,4},{4,6},{6,8},{8,10},{10,12},{12,14},{14,16},{16,18},{18... | collective-permute-start | bytes 491528 | tf_op jit(solution)/shard_map/ppermute | solution.py:190
  13.0 18.8 %copy-start.3 = (f32[8,128]{1,0:T(8,128)S(1)}, f32[8,128]{1,0:T(8,128)}, u32[]{:S(2)}) copy-start(f32[8,128]{1,0:T(8,128)} %constant.36.clone.cos_ref) | copy-start | bytes 12292
  13.0 18.8 %copy-start.4 = (f32[8,128]{1,0:T(8,128)S(1)}, f32[8,128]{1,0:T(8,128)}, u32[]{:S(2)}) copy-start(f32[8,128]{1,0:T(8,128)} %constant.37.clone.sin_ref) | copy-start | bytes 12292
  17.4 13.4 %collective-permute-start.4 = (bf16[640,1024]{1,0:T(8,128)(2,1)}, bf16[640,1024]{1,0:T(8,128)(2,1)S(1)}, u32[]{:S(2)}, u32[]{:S(2)}) collective-permute-start(bf16[640,1024]{1,0:T(8,128)(2,1)} %get-tuple-element.40.white_ref), channel_id=1, source_target_pairs={{0,2},{2,0},{4,6},{6,4},{8,10},{10,8},{12,14},{14,12},{16,18},{18,... | collective-permute-start | bytes 3932168 | tf_op jit(solution)/shard_map/ppermute | solution.py:37
  20.0 2.7 %collective-permute-start.21 = (bf16[64,1024]{1,0:T(8,128)(2,1)S(1)}, bf16[64,1024]{1,0:T(8,128)(2,1)S(1)}, u32[]{:S(2)}, u32[]{:S(2)}) collective-permute-start(bf16[64,1024]{1,0:T(8,128)(2,1)S(1)} %get-tuple-element.64), channel_id=1, source_target_pairs={{0,2},{2,0},{4,6},{6,4},{8,10},{10,8},{12,14},{14,12},{16,18},{18,... | collective-permute-start | bytes 393224 | tf_op jit(solution)/shard_map/ppermute | solution.py:37
  20.1 6.3 %collective-permute-start.20 = (bf16[64,1024]{1,0:T(8,128)(2,1)S(1)}, bf16[64,1024]{1,0:T(8,128)(2,1)S(1)}, u32[]{:S(2)}, u32[]{:S(2)}) collective-permute-start(bf16[64,1024]{1,0:T(8,128)(2,1)S(1)} %get-tuple-element.63.own_ref), channel_id=1, source_target_pairs={{0,1},{1,0},{2,3},{3,2},{4,5},{5,4},{6,7},{7,6},{8,9},{9,8},{10,11... | collective-permute-start | bytes 393224 | tf_op jit(solution)/shard_map/ppermute | solution.py:37
  21.6 6.3 %collective-permute-start.15 = (bf16[64,1024]{1,0:T(8,128)(2,1)S(1)}, bf16[64,1024]{1,0:T(8,128)(2,1)S(1)}, u32[]{:S(2)}, u32[]{:S(2)}) collective-permute-start(bf16[64,1024]{1,0:T(8,128)(2,1)S(1)} %get-tuple-element.56), channel_id=1, source_target_pairs={{0,2},{2,0},{4,6},{6,4},{8,10},{10,8},{12,14},{14,12},{16,18},{18,... | collective-permute-start | bytes 393224 | tf_op jit(solution)/shard_map/ppermute | solution.py:37
  21.8 6.1 %collective-permute-start.9 = (bf16[64,1024]{1,0:T(8,128)(2,1)S(1)}, bf16[64,1024]{1,0:T(8,128)(2,1)S(1)}, u32[]{:S(2)}, u32[]{:S(2)}) collective-permute-start(bf16[64,1024]{1,0:T(8,128)(2,1)S(1)} %get-tuple-element.48), channel_id=1, source_target_pairs={{0,2},{2,0},{4,6},{6,4},{8,10},{10,8},{12,14},{14,12},{16,18},{18,... | collective-permute-start | bytes 393224 | tf_op jit(solution)/shard_map/ppermute | solution.py:37
  22.7 6.5 %collective-permute-start.22 = (bf16[64,1024]{1,0:T(8,128)(2,1)S(1)}, bf16[64,1024]{1,0:T(8,128)(2,1)S(1)}, u32[]{:S(2)}, u32[]{:S(2)}) collective-permute-start(bf16[64,1024]{1,0:T(8,128)(2,1)S(1)} %collective-permute-done.21.sib_ref), channel_id=1, source_target_pairs={{0,1},{1,0},{2,3},{3,2},{4,5},{5,4},{6,7},{7,6},{8,9},{9,8},{10,11... | collective-permute-start | bytes 393224 | tf_op jit(solution)/shard_map/ppermute | solution.py:37
  26.4 10.4 %collective-permute-start.14 = (bf16[64,1024]{1,0:T(8,128)(2,1)S(1)}, bf16[64,1024]{1,0:T(8,128)(2,1)S(1)}, u32[]{:S(2)}, u32[]{:S(2)}) collective-permute-start(bf16[64,1024]{1,0:T(8,128)(2,1)S(1)} %get-tuple-element.55.own_ref), channel_id=1, source_target_pairs={{0,1},{1,0},{2,3},{3,2},{4,5},{5,4},{6,7},{7,6},{8,9},{9,8},{10,11... | collective-permute-start | bytes 393224 | tf_op jit(solution)/shard_map/ppermute | solution.py:37
  27.9 9.9 %collective-permute-start.2 = (bf16[64,1024]{1,0:T(8,128)(2,1)S(1)}, bf16[64,1024]{1,0:T(8,128)(2,1)S(1)}, u32[]{:S(2)}, u32[]{:S(2)}) collective-permute-start(bf16[64,1024]{1,0:T(8,128)(2,1)S(1)} %get-tuple-element.39), channel_id=1, source_target_pairs={{0,2},{2,0},{4,6},{6,4},{8,10},{10,8},{12,14},{14,12},{16,18},{18,... | collective-permute-start | bytes 393224 | tf_op jit(solution)/shard_map/ppermute | solution.py:37
  27.9 10.9 %collective-permute-start.16 = (bf16[64,1024]{1,0:T(8,128)(2,1)S(1)}, bf16[64,1024]{1,0:T(8,128)(2,1)S(1)}, u32[]{:S(2)}, u32[]{:S(2)}) collective-permute-start(bf16[64,1024]{1,0:T(8,128)(2,1)S(1)} %collective-permute-done.15.sib_ref), channel_id=1, source_target_pairs={{0,1},{1,0},{2,3},{3,2},{4,5},{5,4},{6,7},{7,6},{8,9},{9,8},{10,11... | collective-permute-start | bytes 393224 | tf_op jit(solution)/shard_map/ppermute | solution.py:37
  29.2 14.8 %collective-permute-start.8 = (bf16[64,1024]{1,0:T(8,128)(2,1)S(1)}, bf16[64,1024]{1,0:T(8,128)(2,1)S(1)}, u32[]{:S(2)}, u32[]{:S(2)}) collective-permute-start(bf16[64,1024]{1,0:T(8,128)(2,1)S(1)} %get-tuple-element.47.own_ref), channel_id=1, source_target_pairs={{0,1},{1,0},{2,3},{3,2},{4,5},{5,4},{6,7},{7,6},{8,9},{9,8},{10,11... | collective-permute-start | bytes 393224 | tf_op jit(solution)/shard_map/ppermute | solution.py:37
  30.7 1.1 %copy-start.5 = (bf16[640,1024]{1,0:T(8,128)(2,1)}, bf16[640,1024]{1,0:T(8,128)(2,1)S(1)}, u32[]{:S(2)}) copy-start(bf16[640,1024]{1,0:T(8,128)(2,1)S(1)} %collective-permute-done.4.white_sib_ref) | copy-start | bytes 3932164
  30.7 13.9 %collective-permute-start.10 = (bf16[64,1024]{1,0:T(8,128)(2,1)S(1)}, bf16[64,1024]{1,0:T(8,128)(2,1)S(1)}, u32[]{:S(2)}, u32[]{:S(2)}) collective-permute-start(bf16[64,1024]{1,0:T(8,128)(2,1)S(1)} %collective-permute-done.9.sib_ref), channel_id=1, source_target_pairs={{0,1},{1,0},{2,3},{3,2},{4,5},{5,4},{6,7},{7,6},{8,9},{9,8},{10,11... | collective-permute-start | bytes 393224 | tf_op jit(solution)/shard_map/ppermute | solution.py:37
  31.8 1.3 %copy-start.2 = (bf16[640,1024]{1,0:T(8,128)(2,1)S(1)}, bf16[640,1024]{1,0:T(8,128)(2,1)}, u32[]{:S(2)}) copy-start(bf16[640,1024]{1,0:T(8,128)(2,1)} %get-tuple-element.40.white_ref) | copy-start | bytes 3932164
  36.8 13.1 %collective-permute-start.1 = (bf16[64,1024]{1,0:T(8,128)(2,1)S(1)}, bf16[64,1024]{1,0:T(8,128)(2,1)S(1)}, u32[]{:S(2)}, u32[]{:S(2)}) collective-permute-start(bf16[64,1024]{1,0:T(8,128)(2,1)S(1)} %get-tuple-element.38.own_ref), channel_id=1, source_target_pairs={{0,1},{1,0},{2,3},{3,2},{4,5},{5,4},{6,7},{7,6},{8,9},{9,8},{10,11... | collective-permute-start | bytes 393224 | tf_op jit(solution)/shard_map/ppermute | solution.py:37
  37.8 12.0 %collective-permute-start.3 = (bf16[64,1024]{1,0:T(8,128)(2,1)S(1)}, bf16[64,1024]{1,0:T(8,128)(2,1)S(1)}, u32[]{:S(2)}, u32[]{:S(2)}) collective-permute-start(bf16[64,1024]{1,0:T(8,128)(2,1)S(1)} %collective-permute-done.2.sib_ref), channel_id=1, source_target_pairs={{0,1},{1,0},{2,3},{3,2},{4,5},{5,4},{6,7},{7,6},{8,9},{9,8},{10,11... | collective-permute-start | bytes 393224 | tf_op jit(solution)/shard_map/ppermute | solution.py:37
  38.9 15.3 %collective-permute-start.23 = (bf16[256,640]{1,0:T(8,128)(2,1)S(1)}, bf16[256,640]{1,0:T(8,128)(2,1)S(1)}, u32[]{:S(2)}, u32[]{:S(2)}) collective-permute-start(bf16[256,640]{1,0:T(8,128)(2,1)S(1)} %get-tuple-element.66), channel_id=1, source_target_pairs={{0,4},{2,6},{4,0},{6,2},{8,12},{10,14},{12,8},{14,10},{16,20},{18,... | collective-permute-start | bytes 983048 | tf_op jit(solution)/shard_map/ppermute | solution.py:37
  44.0 12.1 %collective-permute-start.17 = (bf16[256,640]{1,0:T(8,128)(2,1)S(1)}, bf16[256,640]{1,0:T(8,128)(2,1)S(1)}, u32[]{:S(2)}, u32[]{:S(2)}) collective-permute-start(bf16[256,640]{1,0:T(8,128)(2,1)S(1)} %get-tuple-element.58), channel_id=1, source_target_pairs={{0,4},{2,6},{4,0},{6,2},{8,12},{10,14},{12,8},{14,10},{16,20},{18,... | collective-permute-start | bytes 983048 | tf_op jit(solution)/shard_map/ppermute | solution.py:37
  48.2 14.9 %collective-permute-start.11 = (bf16[256,640]{1,0:T(8,128)(2,1)S(1)}, bf16[256,640]{1,0:T(8,128)(2,1)S(1)}, u32[]{:S(2)}, u32[]{:S(2)}) collective-permute-start(bf16[256,640]{1,0:T(8,128)(2,1)S(1)} %get-tuple-element.50), channel_id=1, source_target_pairs={{0,4},{2,6},{4,0},{6,2},{8,12},{10,14},{12,8},{14,10},{16,20},{18,... | collective-permute-start | bytes 983048 | tf_op jit(solution)/shard_map/ppermute | solution.py:37
  53.6 14.5 %collective-permute-start.5 = (bf16[256,640]{1,0:T(8,128)(2,1)S(1)}, bf16[256,640]{1,0:T(8,128)(2,1)S(1)}, u32[]{:S(2)}, u32[]{:S(2)}) collective-permute-start(bf16[256,640]{1,0:T(8,128)(2,1)S(1)} %get-tuple-element.42), channel_id=1, source_target_pairs={{0,4},{2,6},{4,0},{6,2},{8,12},{10,14},{12,8},{14,10},{16,20},{18,... | collective-permute-start | bytes 983048 | tf_op jit(solution)/shard_map/ppermute | solution.py:37
  54.2 15.7 %collective-permute-start.24 = (bf16[128,640]{1,0:T(8,128)(2,1)S(1)}, bf16[128,640]{1,0:T(8,128)(2,1)S(1)}, u32[]{:S(2)}, u32[]{:S(2)}) collective-permute-start(bf16[128,640]{1,0:T(8,128)(2,1)S(1)} %get-tuple-element.68), channel_id=1, source_target_pairs={{0,8},{2,10},{4,12},{6,14},{8,0},{10,2},{12,4},{14,6},{16,24},{18,... | collective-permute-start | bytes 491528 | tf_op jit(solution)/shard_map/ppermute | solution.py:37
  56.2 16.4 %collective-permute-start.18 = (bf16[128,640]{1,0:T(8,128)(2,1)S(1)}, bf16[128,640]{1,0:T(8,128)(2,1)S(1)}, u32[]{:S(2)}, u32[]{:S(2)}) collective-permute-start(bf16[128,640]{1,0:T(8,128)(2,1)S(1)} %get-tuple-element.60), channel_id=1, source_target_pairs={{0,8},{2,10},{4,12},{6,14},{8,0},{10,2},{12,4},{14,6},{16,24},{18,... | collective-permute-start | bytes 491528 | tf_op jit(solution)/shard_map/ppermute | solution.py:37
  63.2 9.8 %collective-permute-start.12 = (bf16[128,640]{1,0:T(8,128)(2,1)S(1)}, bf16[128,640]{1,0:T(8,128)(2,1)S(1)}, u32[]{:S(2)}, u32[]{:S(2)}) collective-permute-start(bf16[128,640]{1,0:T(8,128)(2,1)S(1)} %get-tuple-element.52), channel_id=1, source_target_pairs={{0,8},{2,10},{4,12},{6,14},{8,0},{10,2},{12,4},{14,6},{16,24},{18,... | collective-permute-start | bytes 491528 | tf_op jit(solution)/shard_map/ppermute | solution.py:37
  68.2 7.5 %collective-permute-start.6 = (bf16[128,640]{1,0:T(8,128)(2,1)S(1)}, bf16[128,640]{1,0:T(8,128)(2,1)S(1)}, u32[]{:S(2)}, u32[]{:S(2)}) collective-permute-start(bf16[128,640]{1,0:T(8,128)(2,1)S(1)} %get-tuple-element.44), channel_id=1, source_target_pairs={{0,8},{2,10},{4,12},{6,14},{8,0},{10,2},{12,4},{14,6},{16,24},{18,... | collective-permute-start | bytes 491528 | tf_op jit(solution)/shard_map/ppermute | solution.py:37
  69.9 11.9 %collective-permute-start.25 = (bf16[64,640]{1,0:T(8,128)(2,1)S(1)}, bf16[64,640]{1,0:T(8,128)(2,1)S(1)}, u32[]{:S(2)}, u32[]{:S(2)}) collective-permute-start(bf16[64,640]{1,0:T(8,128)(2,1)S(1)} %get-tuple-element.70), channel_id=1, source_target_pairs={{0,16},{2,18},{4,20},{6,22},{8,24},{10,26},{12,28},{14,30},{16,0},... | collective-permute-start | bytes 245768 | tf_op jit(solution)/shard_map/ppermute | solution.py:37
  72.6 11.0 %collective-permute-start.19 = (bf16[64,640]{1,0:T(8,128)(2,1)S(1)}, bf16[64,640]{1,0:T(8,128)(2,1)S(1)}, u32[]{:S(2)}, u32[]{:S(2)}) collective-permute-start(bf16[64,640]{1,0:T(8,128)(2,1)S(1)} %get-tuple-element.62), channel_id=1, source_target_pairs={{0,16},{2,18},{4,20},{6,22},{8,24},{10,26},{12,28},{14,30},{16,0},... | collective-permute-start | bytes 245768 | tf_op jit(solution)/shard_map/ppermute | solution.py:37
  73.1 12.0 %collective-permute-start.13 = (bf16[64,640]{1,0:T(8,128)(2,1)S(1)}, bf16[64,640]{1,0:T(8,128)(2,1)S(1)}, u32[]{:S(2)}, u32[]{:S(2)}) collective-permute-start(bf16[64,640]{1,0:T(8,128)(2,1)S(1)} %get-tuple-element.54), channel_id=1, source_target_pairs={{0,16},{2,18},{4,20},{6,22},{8,24},{10,26},{12,28},{14,30},{16,0},... | collective-permute-start | bytes 245768 | tf_op jit(solution)/shard_map/ppermute | solution.py:37
  75.8 10.2 %collective-permute-start.7 = (bf16[64,640]{1,0:T(8,128)(2,1)S(1)}, bf16[64,640]{1,0:T(8,128)(2,1)S(1)}, u32[]{:S(2)}, u32[]{:S(2)}) collective-permute-start(bf16[64,640]{1,0:T(8,128)(2,1)S(1)} %get-tuple-element.46), channel_id=1, source_target_pairs={{0,16},{2,18},{4,20},{6,22},{8,24},{10,26},{12,28},{14,30},{16,0},... | collective-permute-start | bytes 245768 | tf_op jit(solution)/shard_map/ppermute | solution.py:37

commit v2 on v0

v2 whole, which is shorter than its diff:
```python
import functools
import math

import jax
import jax.numpy as jnp
import numpy as np
from jax import lax
from jax.experimental import pallas as pl
from jax.experimental.pallas import tpu as pltpu
from jax.sharding import PartitionSpec as P

VS = 512
TD = 256
HALF = TD // 2
NLAG = 8
HW = 32
TAPS = 128
DECIM = 4
SPAN = DECIM * TD
VMEM_LIMIT = 20 * 1024 * 1024
BLOCK = 320
CHUNKS = (2, 8, 8, 8, 6)
FIRST = (1, 1, 0, 1, 0)
SECOND = ((2,), (4,), (0, 1), (3,))
THIRD = ((2,), (0,), (3,), (1,))
PLAN = (
    ('split', 0, (), ()),
    ('merge', 0, (1, 2, 3, 4), ()),
    ('product', 0, (), ()),
    ('product', 1, (), (('y', 1),)),
    ('product', 2, (), (('y', 2), ('first', 0))),
    ('product', 3, (), (('y', 3),)),
    ('second', 2, (), (('first', 1),)),
    ('product', 4, (), (('y', 4),)),
    ('second', 0, (), (('first', 2),)),
    ('third', 0, (), (('second', 2),)),
    ('second', 3, (), (('first', 3),)),
    ('third', 1, (), (('second', 0),)),
    ('second', 1, (), (('first', 4),)),
    ('sum', 0, (), (('third', 0),)),
    ('third', 2, (), (('second', 3),)),
    ('sum', 1, (), (('third', 1),)),
    ('third', 3, (), (('second', 1),)),
    ('sum', 2, (), (('third', 2),)),
)
BASE_COST = 0.05
COSTS = {'split_0': 8, 'merge_0': 1, 'product_0': 0.265, 'product_1': 0.558, 'product_2': 0.604, 'product_3': 0.385, 'second_2': 0.186, 'product_4': 0.345, 'second_0': 0.23, 'third_0': 0.266, 'second_3': 0.245, 'third_1': 0.266, 'second_1': 0.186, 'sum_0': 0.047, 'third_2': 0.271, 'sum_1': 0.111, 'third_3': 0.368, 'sum_2': 0.293}

VMEM = pl.BlockSpec(memory_space=pltpu.VMEM)
ANY = pl.BlockSpec(memory_space=pl.ANY)


def params(limit=VMEM_LIMIT):
    return pltpu.CompilerParams(vmem_limit_bytes=limit)


def cost(flops, nbytes):
    return pl.CostEstimate(flops=int(flops), bytes_accessed=int(nbytes), transcendentals=0)


def swap(value, axis, bit):
    return lax.ppermute(value, axis, [(i, i ^ bit) for i in range(lax.axis_size(axis))])


def dft_table():
    phase = np.arange(TD)[:, None] * np.arange(HALF)[None, :] % TD
    angles = np.float32(2.0 * math.pi / TD) * phase.astype(np.float32)
    return np.concatenate([np.cos(angles), -np.sin(angles)], axis=1).astype(jnp.bfloat16)


def lag_tables(gain):
    phase = (np.arange(NLAG) - NLAG // 2)[:, None] * np.arange(HALF)[None, :] % TD
    angles = 2.0 * math.pi / TD * phase.astype(np.float64)
    return (gain * np.cos(angles)).astype(np.float32), (gain * np.sin(angles)).astype(np.float32)


def band_table():
    bins = np.arange(HALF)
    band = (np.abs(bins[:, None] - bins[None, :]) <= HW).astype(np.float32)
    return np.concatenate([band, band], axis=0).astype(jnp.bfloat16)


def nt_dot(left, right):
    return lax.dot_general(left, right, (((1,), (1,)), ((), ())), preferred_element_type=jnp.float32)


def history_kernel(raw_ref, out_ref, sem):
    samples = raw_ref.shape[1]
    copy = pltpu.make_async_copy(raw_ref.at[:, samples - TAPS :], out_ref, sem)
    copy.start()
    copy.wait()


def fill_fir(taps_ref, fir_ref):
    rows = TAPS // DECIM
    taps = jnp.broadcast_to(taps_ref[...].astype(jnp.float32), (rows, TAPS))
    padded = jnp.concatenate([taps, jnp.zeros_like(taps)], axis=1)
    base = pltpu.roll(padded, 1, 1, stride=DECIM, stride_axis=0).astype(jnp.bfloat16)
    fir_ref[...] = jnp.zeros_like(fir_ref)
    for i in range(TD // rows):
        fir_ref[rows * i : rows * (i + 1), TAPS * i : TAPS * (i + 2)] = base


def fill_alive(dead_ref, alive_ref):
    alive = 1.0 - dead_ref[...].astype(jnp.float32)
    for i in range(0, alive_ref.shape[0], HALF):
        alive_ref[i : i + HALF, :] = jnp.broadcast_to(alive[:, i : i + HALF], (HALF, HALF)).T


def fill_selector(sizes, orders, sources_ref, select_ref):
    rows = select_ref.shape[1]
    me = lax.axis_index("tm")
    first_chan = lax.axis_index("chan") * rows
    per_dest = sum(sizes)
    codes = 1 << len(orders[0])
    channels = sources_ref[...].astype(jnp.float32)
    begin, row = 0, 0
    for size, bits in zip(sizes, orders):
        count = 2 * codes * size
        index = lax.broadcasted_iota(jnp.int32, (count, VS), 0)
        scale = (1 << 16) // size + 1
        piece = lax.shift_right_logical(index * scale, 16)
        relative = lax.shift_right_logical(piece, len(bits))
        for place, bit in enumerate(bits):
            relative = relative + bit * (lax.shift_right_logical(piece, len(bits) - 1 - place) & 1)
        wanted = per_dest * jnp.bitwise_xor(relative, me) + begin + (index - size * piece)
        match = wanted == lax.broadcasted_iota(jnp.int32, (count, VS), 1)
        chosen = jnp.sum(jnp.where(match, channels, 0.0), axis=1, keepdims=True)
        place = chosen.astype(jnp.int32) - first_chan
        hit = place == lax.broadcasted_iota(jnp.int32, (count, rows), 1)
        select_ref[row : row + count, :] = jnp.where(hit, 1.0, 0.0).astype(jnp.bfloat16)
        begin += size
        row += count


def whiten(dec, table_ref, band_ref, alive):
    spectrum = jnp.dot(dec, table_ref[...], preferred_element_type=jnp.float32)
    real_part = spectrum[:, :HALF]
    imag_part = spectrum[:, HALF:]
    amplitude = jnp.sqrt(real_part * real_part + imag_part * imag_part)
    high = amplitude.astype(jnp.bfloat16)
    low = (amplitude - high.astype(jnp.float32)).astype(jnp.bfloat16)
    total = jnp.dot(
        jnp.concatenate([high, low], axis=1), band_ref[...], preferred_element_type=jnp.float32
    )
    factor = alive / (total * (1.0 / (2 * HW + 1)) + 1e-06)
    return jnp.concatenate([real_part * factor, imag_part * factor], axis=1).astype(jnp.bfloat16)


def late_kernel(
    sizes, orders, raw_ref, taps_ref, dead_ref, sources_ref, table_ref, band_ref,
    out_ref, fir_ref, alive_ref, select_ref,
):
    windows, rows, _ = out_ref.shape
    fill_fir(taps_ref, fir_ref)
    fill_alive(dead_ref, alive_ref)
    fill_selector(sizes, orders, sources_ref, select_ref)
    samples = jnp.concatenate(
        [raw_ref[:, w * SPAN - TAPS : (w + 1) * SPAN] for w in range(1, windows + 1)], axis=0
    )
    dec = nt_dot(samples, fir_ref[...]).astype(jnp.bfloat16)
    alive = jnp.concatenate([alive_ref[...]] * windows, axis=0)
    out_ref[...] = whiten(dec, table_ref, band_ref, alive).reshape(out_ref.shape)


def pick(select, white):
    return jnp.dot(select, white, preferred_element_type=jnp.float32).astype(jnp.bfloat16)


def first_kernel(
    raw_ref, hist_ref, fir_ref, table_ref, band_ref, alive_ref, late_ref, select_ref,
    panel_ref, white_ref,
):
    white_ref[1:] = late_ref[...]
    samples = jnp.concatenate([hist_ref[...], raw_ref[:, :SPAN]], axis=1)
    dec = nt_dot(samples, fir_ref[...]).astype(jnp.bfloat16)
    white_ref[0] = whiten(dec, table_ref, band_ref, alive_ref[...])
    select = select_ref[: panel_ref.shape[1]]
    for w in range(white_ref.shape[0]):
        panel_ref[w] = pick(select, white_ref[w])


def panels_kernel(skip, counts, select_ref, white_ref, own_ref, other_ref):
    for w in range(white_ref.shape[0]):
        chosen = pick(select_ref[skip:], white_ref[w])
        row, place = 0, 0
        for count in counts:
            own_ref[w, place : place + count] = chosen[row : row + count]
            other_ref[w, place : place + count] = chosen[row + count : row + 2 * count]
            row += 2 * count
            place += count


def merge_kernel(own_ref, sib_ref, *panel_refs):
    row = 0
    for panel_ref in panel_refs:
        count = panel_ref.shape[2]
        panel_ref[0] = own_ref[:, row : row + count]
        panel_ref[1] = sib_ref[:, row : row + count]
        row += count


def split_kernel(panel_ref, recv_ref, keep_ref, send_ref):
    count = keep_ref.shape[1]
    keep_ref[...] = panel_ref[:, :count] + recv_ref[:, :count]
    send_ref[...] = panel_ref[:, count:] + recv_ref[:, count:]


def product_kernel(sources, white_ref, white_sib_ref, cos_ref, sin_ref, keep_ref, send_ref, lag_ref):
    windows = white_ref.shape[0]
    half = keep_ref.shape[0]
    cos_lag = cos_ref[...][None]
    sin_lag = sin_ref[...][None]
    for side in range(2):
        for w in range(windows):
            source = sources(side, w)
            count = source.shape[0]
            real_src = source[:, None, :HALF]
            imag_src = source[:, None, HALF:]
            real_out = real_src * cos_lag + imag_src * sin_lag
            imag_out = imag_src * cos_lag - real_src * sin_lag
            k = (side * windows + w) * TD
            lag_ref[:, k : k + HALF] = real_out.reshape(count * NLAG, HALF).astype(jnp.bfloat16)
            lag_ref[:, k + HALF : k + TD] = imag_out.reshape(count * NLAG, HALF).astype(jnp.bfloat16)
    white = jnp.concatenate(
        [ref[w] for ref in (white_ref, white_sib_ref) for w in range(windows)], axis=1
    )
    blocks = -(-half // BLOCK)
    size = half // blocks
    for row in range(0, half, size):
        send_ref[row : row + size] = nt_dot(lag_ref[half + row : half + row + size], white).astype(jnp.bfloat16)
    for row in range(0, half, size):
        keep_ref[row : row + size] = nt_dot(lag_ref[row : row + size], white)


def taken_kernel(own_ref, sib_ref, *refs):
    product_kernel(lambda side, w: (own_ref, sib_ref)[side][w].astype(jnp.float32), *refs)


def summed_kernel(panel_ref, recv_ref, *refs):
    def sources(side, w):
        return panel_ref[side, w].astype(jnp.float32) + recv_ref[side, w].astype(jnp.float32)

    product_kernel(sources, *refs)


def halves_kernel(pieces, *refs):
    *parts, kept_ref, send_ref = refs
    place = 0
    for keep_ref, recv_ref, counts in zip(parts[::2], parts[1::2], pieces):
        row = 0
        for count in counts:
            half = count // 2
            for out_ref, begin in ((kept_ref, row), (send_ref, row + half)):
                rows = slice(begin, begin + half)
                value = keep_ref[rows, :] + recv_ref[rows, :].astype(jnp.float32)
                out_ref[place : place + half, :] = value.astype(out_ref.dtype)
            row += count
            place += half


def total_kernel(keep_ref, recv_ref, out_ref):
    out_ref[...] = keep_ref[...] + recv_ref[...].astype(jnp.float32)


def last_kernel(pieces, *refs):
    *parts, out_ref = refs
    parts = iter(parts)
    for summed, places in pieces:
        keep_ref = next(parts)
        recv_ref = None if summed else next(parts)
        row = 0
        for begin, count in places:
            rows = slice(row, row + count)
            value = keep_ref[rows, :]
            if not summed:
                value = value + recv_ref[rows, :].astype(jnp.float32)
            out_ref[begin : begin + count, :] = value
            row += count


class Chain:
    def __init__(self):
        self.last = None

    def __call__(self, name, kernel, args, outs, scratch=(), gates=(), waits=(), limit=VMEM_LIMIT, first=VMEM):
        args, gates = list(args), list(gates)
        order = [*waits] if self.last is None else [*waits, self.last]
        taken, passed = len(args), len(args) + len(gates) + len(order)

        def body(*refs):
            written = refs[passed : passed + len(outs)]
            kernel(*refs[:taken], *written, *refs[passed + len(outs) + len(gates) :])

        results = pl.pallas_call(
            body,
            out_shape=[*outs, *(jax.ShapeDtypeStruct(g.shape, g.dtype) for g in gates)],
            in_specs=[first] + [VMEM] * (taken - 1) + [ANY] * (len(gates) + len(order)),
            out_specs=[VMEM] * len(outs) + [ANY] * len(gates),
            input_output_aliases={taken + i: len(outs) + i for i in range(len(gates))},
            scratch_shapes=list(scratch),
            compiler_params=params(limit),
            cost_estimate=cost(1e9 * COSTS.get(name, BASE_COST), 1e4),
            name=name,
        )(*args, *gates, *order)
        self.last = results[0]
        return results


def local(raw_traces, fir_taps, sources, dead_flags):
    rows, samples = raw_traces.shape
    windows = samples // SPAN
    late = windows - 1
    time_parts = lax.axis_size("tm")
    chan_parts = lax.axis_size("chan")
    per_dest = VS // time_parts
    codes = time_parts // 2
    bits = [1 << i for i in range(1, time_parts.bit_length() - 1)]
    sizes, firsts, seconds, thirds, plan = CHUNKS, FIRST, SECOND, THIRD, PLAN
    if per_dest != sum(CHUNKS) or len(bits) != 3:
        sizes, firsts = (per_dest // 2,) * 2, (0, 0)
        seconds = thirds = ((0,), (1,))
        plan = [("split", 0, (), ()), ("merge", 0, (), ()), ("product", 0, (1,), ()), ("product", 1, (), ())]
        final = "third" + "+" * (len(bits) - 3)
        plan += [(name, q, (), ()) for name in ("second", *(final[:5 + i] for i in range(len(final) - 4))) for q in (0, 1)]
    final = "third" + "+" * (len(bits) - 3)
    orders = [[bits[first], *bits[:first], *bits[first + 1 :]] for first in firsts]
    counts = [size * codes for size in sizes]
    bf16, f32 = jnp.bfloat16, jnp.float32
    shape = jax.ShapeDtypeStruct
    chain = Chain()

    (tail,) = chain(
        "history", history_kernel, [pltpu.with_memory_space_constraint(raw_traces, pltpu.HBM)], [shape((rows, TAPS), bf16)], [pltpu.SemaphoreType.DMA],
        first=ANY,
    )
    history = lax.ppermute(tail, "tm", [(i, i + 1) for i in range(time_parts - 1)])

    table = jnp.asarray(dft_table())
    band = jnp.asarray(band_table())
    late_white, fir, alive, select = chain(
        "late",
        functools.partial(late_kernel, sizes, orders),
        [raw_traces, fir_taps.reshape(1, -1), dead_flags.reshape(1, -1), sources.reshape(1, -1), table, band],
        [
            shape((late, rows, TD), bf16),
            shape((TD, SPAN + TAPS), bf16),
            shape((rows, HALF), f32),
            shape((VS, rows), bf16),
        ],
    )
    panel, white = chain(
        "first",
        first_kernel,
        [raw_traces, history, fir, table, band, alive, late_white, select],
        [shape((windows, 2 * counts[0], TD), bf16), shape((windows, rows, TD), bf16)],
    )
    rest = shape((windows, sum(counts[1:]), TD), bf16)
    own, other = chain(
        "panels", functools.partial(panels_kernel, 2 * counts[0], counts[1:]), [select, white], [rest, rest]
    )
    white_sib = swap(white, "tm", 1)
    sib = swap(other, "tm", 1)
    tables = [jnp.asarray(t) for t in lag_tables(1.0 / math.sqrt(time_parts * windows * TD))]
    spectra = [white, white_sib, *tables]

    def across(panel):
        if chan_parts == 2:
            return swap(panel, "chan", 1)
        return lax.psum(panel, "chan") - panel

    panels = {0: panel}
    arrived = {}
    state, pieces, moved = {}, {}, {}
    for kind, q, leaving, waits in plan:
        name = f"{kind}_{q}"
        gates = [panels[g] for g in leaving if g in panels]
        held = [moved[key] for key in waits if key in moved]
        call = functools.partial(chain, name, gates=gates, waits=held)
        if kind == "split":
            half = shape((windows, counts[0], TD), bf16)
            keep, send, *let = call(split_kernel, [panel, across(panel)], [half, half])
            taken = [keep, swap(send, "tm", 1)]
        elif kind == "merge":
            made = call(merge_kernel, [own, sib], [shape((2, windows, c, TD), bf16) for c in counts[1:]])
            panels.update(enumerate(made, 1))
            let = []
        elif kind == "product":
            half = counts[q] * NLAG // 2
            args = taken if q == 0 else [panels[q], arrived[q]]
            keep, send, *let = call(
                summed_kernel if q else taken_kernel, [*args, *spectra],
                [shape((half, rows), f32), shape((half, rows), bf16)],
                [pltpu.VMEM((2 * half, 2 * windows * TD), bf16)],
            )
            moved["first", q] = swap(send, "tm", orders[q][0])
            state["first", q] = keep, moved["first", q]
            pieces["first", q] = [half]
        elif kind == "sum":
            keep, recv = state["third", q]
            total, *let = call(total_kernel, [keep, recv], [shape(keep.shape, f32)])
            state["third", q] = total, None
        else:
            before, groups = {"second": ("first", seconds), "third": ("second", thirds)}.get(kind, (kind[:-1], thirds))
            members = [(before, member) for member in groups[q]]
            if before.startswith("third"):
                members = [(before, q)]
            split = [pieces[m] for m in members]
            half = sum(map(sum, split)) // 2
            keep, send, *let = call(
                functools.partial(halves_kernel, split), [x for m in members for x in state[m]],
                [shape((half, rows), f32), shape((half, rows), bf16)],
            )
            pieces[kind, q] = [count // 2 for part in split for count in part]
            chunk = groups[q][0] if kind == "second" else seconds[groups[q][0]][0]
            stage = 1 if kind == "second" else 2 + kind.count("+")
            moved[kind, q] = swap(send, "tm", orders[chunk][stage])
            state[kind, q] = keep, moved[kind, q]
        panels.update(zip(leaving, let))
        for g in leaving:
            moved["y", g] = arrived[g] = across(panels[g])

    starts = [sum(sizes[:q]) * NLAG for q in range(len(sizes))]
    args, places = [], []
    for q, group in enumerate(thirds):
        args += [x for x in state[final, q] if x is not None]
        chunks = [chunk for member in group for chunk in seconds[member]]
        places.append((state[final, q][1] is None, [(starts[chunk], sizes[chunk] * NLAG) for chunk in chunks]))
    (stacked,) = chain(
        "last", functools.partial(last_kernel, places), args, [shape((per_dest * NLAG, rows), f32)]
    )
    return stacked.reshape(per_dest, NLAG, rows)


def solution(mesh):
    return jax.shard_map(
        local,
        mesh=mesh,
        in_specs=(P("chan", "tm"), P(), P(), P("chan")),
        out_specs=P("tm", None, "chan"),
        check_vma=False,
    )
```

time: 192 us -> 69.4 us (0.36)
  waiting for transfers between devices: 108 us -> 18.7 us
  starting transfers between devices: 2.59 us -> 31.5 us
  local copies, waits for them, and re-layouts: 28 us -> 0.86 us
  matrix products: 20.2 us -> 0 us
  other arithmetic: 19 us -> 0 us
  Pallas kernels: 0 us -> 17.9 us
  between operations: 13.6 us -> 0.27 us
    reduce_scatter x1 -> x0, waiting for transfers between devices: 78.6 us -> none  [local(): lax.psum_scatter(lax.dot_general(lagged, white_flat, (((1,), (1,)), ((),...]
    all_gather x1 -> x0, waiting for transfers between devices: 29.6 us -> none  [local(): gathered = lax.all_gather(src_panel, 'chan', axis=0, tiled=True)]
    ppermute x1 -> x22, starting transfers between devices: 2.37 us -> 31.5 us  [the longest x21 29 us: swap(): lax.ppermute(value, axis, [(i, i ^ bit) for i in range(lax.axis_size(axis...]
    dot_general x6 -> x0, matrix products: 20.2 us -> none  [the longest x1 11.5 us: local(): lax.dot_general(lagged, white_flat, (((1,), (1,)), ((), ())), preferred_e...]
    ppermute x1 -> x22, waiting for transfers between devices: 0.01 us -> 18.7 us  [the longest x21 18.7 us: swap(): lax.ppermute(value, axis, [(i, i ^ bit) for i in range(lax.axis_size(axis...]
    pallas_call x0 -> x23, Pallas kernels: none -> 17.9 us  [__call__(): pl.pallas_call(body, out_shape=[*outs, *(jax.ShapeDtypeStruct(g.shape, g....]
    unnamed x6 -> x16, local copies, waits for them, and re-layouts: 15.5 us -> 0.86 us
    concatenate x1 -> x0, local copies, waits for them, and re-layouts: 8.93 us -> none  [local(): jnp.concatenate([before, grouped], axis=2).reshape(-1, TAPS + sample_block)]
  transfers between devices with their start and end apart: 3 -> 22, of which waited for: 2 -> 10; matrix products, arithmetic and copies ran while one was open for 10% -> 0% of each run, Pallas kernels for 0% -> 21%
where the time goes in v2:
time: 69.4 us; the launch traced here: 69.3 us
  starting transfers between devices  31.5 us (45%)
  waiting for transfers between devices  18.7 us (27%)
  Pallas kernels  17.9 us (26%)
  local copies, waits for them, and re-layouts  0.86 us (1%)
    ppermute x21, starting transfers between devices, swap(): lax.ppermute(value, axis, [(i, i ^ bit) for i in range(lax.axis_size(axis...  29 us
    ppermute x21, waiting for transfers between devices, swap(): lax.ppermute(value, axis, [(i, i ^ bit) for i in range(lax.axis_size(axis...  18.7 us
    pallas_call x23, Pallas kernels, __call__(): pl.pallas_call(body, out_shape=[*outs, *(jax.ShapeDtypeStruct(g.shape, g....  17.9 us
    ppermute x1, starting transfers between devices, local(): lax.ppermute(tail, 'tm', [(i, i + 1) for i in range(time_parts - 1)])  2.51 us
  transfers between devices with their start and end apart: 22, of which 10 were waited for; matrix products, arithmetic and copies ran while one was open for 0% of the time, Pallas kernels for 21%

profile of v2, /device:TPU:0, one launch (start us, length us, event | category | flops | bytes accessed | tf_op | source)
XLA Modules:
  0.0 69.3 jit_solution(16289433567070699809)
XLA Ops:
  0.0 1.1 %history.1.refs_6_ = bf16[640,128]{1,0:T(8,128)(2,1)S(1)} custom-call(bf16[640,4096]{1,0:T(8,128)(2,1)} %refs_0_.5), custom_call_target="tpu_custom_call" | custom-call | flops 50000000 | bytes 10000 | tf_op jit(solution)/shard_map/history/pallas_call | solution.py:295
  1.1 2.5 %collective-permute-start = (bf16[640,128]{1,0:T(8,128)(2,1)S(1)}, bf16[640,128]{1,0:T(8,128)(2,1)S(1)}, u32[]{:S(2)}, u32[]{:S(2)}) collective-permute-start(bf16[640,128]{1,0:T(8,128)(2,1)S(1)} %history.1.refs_6_), channel_id=1, source_target_pairs={{0,2},{2,4},{4,6},{6,8},{8,10},{10,12},{12,14},{14,16},{16,18},{18... | collective-permute-start | bytes 491528 | tf_op jit(solution)/shard_map/ppermute | solution.py:337
  4.5 3.0 %late.1 = (bf16[3,640,256]{2,1,0:T(8,128)(2,1)S(1)}, bf16[256,1152]{1,0:T(8,128)(2,1)S(1)}, f32[640,128]{1,0:T(8,128)S(1)}, bf16[512,640]{1,0:T(8,128)(2,1)S(1)}) custom-call(bf16[640,4096]{1,0:T(8,128)(2,1)S(1)} %copy-done, bf16[1,128]{1,0:T(2,128)(2,1)S(1)} %bitcast.4, s32[1,640]{1,0:T(1,128)S(1)} %reshape.13.refs_2_, s32[1,512]{1,0:T(1,128)S(1)} %bitcast.3, ...), custom_call_target="tpu_custom_call" | custom-call | flops 50000000 | bytes 10000 | tf_op jit(solution)/shard_map/late/pallas_call | solution.py:295
  7.5 1.7 %first.1 = (bf16[4,32,256]{2,1,0:T(8,128)(2,1)S(1)}, bf16[4,640,256]{2,1,0:T(8,128)(2,1)S(1)}) custom-call(bf16[640,4096]{1,0:T(8,128)(2,1)S(1)} %copy-done, bf16[640,128]{1,0:T(8,128)(2,1)S(1)} %collective-permute-done.refs_1_, bf16[256,1152]{1,0:T(8,128)(2,1)S(1)} %get-tuple-element.45.refs_2_, bf16[256,256]{1,0:T(8,128)(2,1)S(1)} %copy-done.1, ...), custom_call_target="tpu_custom_call" | custom-call | flops 50000000 | bytes 10000 | tf_op jit(solution)/shard_map/first/pallas_call | solution.py:295
  9.2 2.6 %collective-permute-start.3 = (bf16[4,640,256]{2,1,0:T(8,128)(2,1)S(1)}, bf16[4,640,256]{2,1,0:T(8,128)(2,1)S(1)}, u32[]{:S(2)}, u32[]{:S(2)}) collective-permute-start(bf16[4,640,256]{2,1,0:T(8,128)(2,1)S(1)} %get-tuple-element.50.refs_1_.refs_2_), channel_id=1, source_target_pairs={{0,2},{2,0},{4,6},{6,4},{8,10},{10,8},{12,14},{14,12},{16,18},{18,... | collective-permute-start | bytes 3932168 | tf_op jit(solution)/shard_map/ppermute | solution.py:62
  11.8 1.5 %collective-permute-start.1 = (bf16[4,32,256]{2,1,0:T(8,128)(2,1)S(1)}, bf16[4,32,256]{2,1,0:T(8,128)(2,1)S(1)}, u32[]{:S(2)}, u32[]{:S(2)}) collective-permute-start(bf16[4,32,256]{2,1,0:T(8,128)(2,1)S(1)} %get-tuple-element.49.refs_2_.refs_0_), channel_id=1, source_target_pairs={{0,1},{1,0},{2,3},{3,2},{4,5},{5,4},{6,7},{7,6},{8,9},{9,8},{10,11... | collective-permute-start | bytes 196616 | tf_op jit(solution)/shard_map/ppermute | solution.py:62
  13.4 0.9 %panels.1 = (bf16[4,240,256]{2,1,0:T(8,128)(2,1)S(1)}, bf16[4,240,256]{2,1,0:T(8,128)(2,1)S(1)}) custom-call(bf16[512,640]{1,0:T(8,128)(2,1)S(1)} %get-tuple-element.48.refs_7_.refs_0_, bf16[4,640,256]{2,1,0:T(8,128)(2,1)S(1)} %get-tuple-element.50.refs_1_.refs_2_, bf16[4,32,256]{2,1,0:T(8,128)(2,1)S(1)} %get-tuple-element.49.refs_2_.refs_0_), custom_call_target="tpu_custom_call" | custom-call | flops 50000000 | bytes 10000 | tf_op jit(solution)/shard_map/panels/pallas_call | solution.py:295
  14.4 1.7 %collective-permute-done.1.refs_1_ = bf16[4,32,256]{2,1,0:T(8,128)(2,1)S(1)} collective-permute-done((bf16[4,32,256]{2,1,0:T(8,128)(2,1)S(1)}, bf16[4,32,256]{2,1,0:T(8,128)(2,1)S(1)}, u32[]{:S(2)}, u32[]{:S(2)}) %collective-permute-start.1) | collective-permute-done | bytes 65568 | tf_op jit(solution)/shard_map/ppermute | solution.py:62
  16.3 1.5 %collective-permute-start.6 = (bf16[2,4,64,256]{3,2,1,0:T(8,128)(2,1)S(1)}, bf16[2,4,64,256]{3,2,1,0:T(8,128)(2,1)S(1)}, u32[]{:S(2)}, u32[]{:S(2)}) collective-permute-start(bf16[2,4,64,256]{3,2,1,0:T(8,128)(2,1)S(1)} %get-tuple-element.55.refs_6_.refs_0_), channel_id=1, source_target_pairs={{0,1},{1,0},{2,3},{3,2},{4,5},{5,4},{6,7},{7,6},{8,9},{9,8},{10,11... | collective-permute-start | bytes 786440 | tf_op jit(solution)/shard_map/ppermute | solution.py:62
  18.4 1.5 %collective-permute-start.8 = (bf16[2,4,64,256]{3,2,1,0:T(8,128)(2,1)S(1)}, bf16[2,4,64,256]{3,2,1,0:T(8,128)(2,1)S(1)}, u32[]{:S(2)}, u32[]{:S(2)}) collective-permute-start(bf16[2,4,64,256]{3,2,1,0:T(8,128)(2,1)S(1)} %get-tuple-element.60.refs_0_), channel_id=1, source_target_pairs={{0,1},{1,0},{2,3},{3,2},{4,5},{5,4},{6,7},{7,6},{8,9},{9,8},{10,11... | collective-permute-start | bytes 786440 | tf_op jit(solution)/shard_map/ppermute | solution.py:62
  19.9 1.7 %product_0.1 = (f32[64,640]{1,0:T(8,128)S(1)}, bf16[64,640]{1,0:T(8,128)(2,1)S(1)}) custom-call(bf16[4,16,256]{2,1,0:T(8,128)(2,1)S(1)} %get-tuple-element.52.refs_2_.refs_0_, bf16[4,16,256]{2,1,0:T(8,128)(2,1)S(1)} %collective-permute-done.2.refs_1_, bf16[4,640,256]{2,1,0:T(8,128)(2,1)S(1)} %get-tuple-element.50.refs_1_.refs_2_, ...), custom_call_target="tpu_custom_call" | custom-call | flops 265000000 | bytes 10000 | tf_op jit(solution)/shard_map/product_0/pallas_call | solution.py:295
  21.6 2.0 %collective-permute-start.5 = (bf16[64,640]{1,0:T(8,128)(2,1)S(1)}, bf16[64,640]{1,0:T(8,128)(2,1)S(1)}, u32[]{:S(2)}, u32[]{:S(2)}) collective-permute-start(bf16[64,640]{1,0:T(8,128)(2,1)S(1)} %get-tuple-element.57), channel_id=1, source_target_pairs={{0,8},{2,10},{4,12},{6,14},{8,0},{10,2},{12,4},{14,6},{16,24},{18,... | collective-permute-start | bytes 245768 | tf_op jit(solution)/shard_map/ppermute | solution.py:62
  23.6 1.9 %collective-permute-done.6.refs_1_.refs_6_ = bf16[2,4,64,256]{3,2,1,0:T(8,128)(2,1)S(1)} collective-permute-done((bf16[2,4,64,256]{3,2,1,0:T(8,128)(2,1)S(1)}, bf16[2,4,64,256]{3,2,1,0:T(8,128)(2,1)S(1)}, u32[]{:S(2)}, u32[]{:S(2)}) %collective-permute-start.6) | collective-permute-done | bytes 262176 | tf_op jit(solution)/shard_map/ppermute | solution.py:62
  25.5 2.0 %product_1.1 = (f32[256,640]{1,0:T(8,128)S(1)}, bf16[256,640]{1,0:T(8,128)(2,1)S(1)}) custom-call(bf16[2,4,64,256]{3,2,1,0:T(8,128)(2,1)S(1)} %get-tuple-element.55.refs_6_.refs_0_, bf16[2,4,64,256]{3,2,1,0:T(8,128)(2,1)S(1)} %collective-permute-done.6.refs_1_.refs_6_, bf16[4,640,256]{2,1,0:T(8,128)(2,1)S(1)} %get-tuple-element.50.refs_1_.refs_2_, ...), custom_call_target="tpu_custom_call" | custom-call | flops 558000000 | bytes 10000 | tf_op jit(solution)/shard_map/product_1/pallas_call | solution.py:295
  27.6 1.9 %collective-permute-start.7 = (bf16[256,640]{1,0:T(8,128)(2,1)S(1)}, bf16[256,640]{1,0:T(8,128)(2,1)S(1)}, u32[]{:S(2)}, u32[]{:S(2)}) collective-permute-start(bf16[256,640]{1,0:T(8,128)(2,1)S(1)} %get-tuple-element.59), channel_id=1, source_target_pairs={{0,8},{2,10},{4,12},{6,14},{8,0},{10,2},{12,4},{14,6},{16,24},{18,... | collective-permute-start | bytes 983048 | tf_op jit(solution)/shard_map/ppermute | solution.py:62
  29.5 1.6 %collective-permute-done.9.refs_1_.refs_6_ = bf16[2,4,64,256]{3,2,1,0:T(8,128)(2,1)S(1)} collective-permute-done((bf16[2,4,64,256]{3,2,1,0:T(8,128)(2,1)S(1)}, bf16[2,4,64,256]{3,2,1,0:T(8,128)(2,1)S(1)}, u32[]{:S(2)}, u32[]{:S(2)}) %collective-permute-start.9) | collective-permute-done | bytes 262176 | tf_op jit(solution)/shard_map/ppermute | solution.py:62
  31.1 2.0 %product_2.1 = (f32[256,640]{1,0:T(8,128)S(1)}, bf16[256,640]{1,0:T(8,128)(2,1)S(1)}) custom-call(bf16[2,4,64,256]{3,2,1,0:T(8,128)(2,1)S(1)} %get-tuple-element.61.refs_0_, bf16[2,4,64,256]{3,2,1,0:T(8,128)(2,1)S(1)} %collective-permute-done.9.refs_1_.refs_6_, bf16[4,640,256]{2,1,0:T(8,128)(2,1)S(1)} %get-tuple-element.50.refs_1_.refs_2_, ...), custom_call_target="tpu_custom_call" | custom-call | flops 604000000 | bytes 10000 | tf_op jit(solution)/shard_map/product_2/pallas_call | solution.py:295
  33.2 1.6 %collective-permute-start.11 = (bf16[256,640]{1,0:T(8,128)(2,1)S(1)}, bf16[256,640]{1,0:T(8,128)(2,1)S(1)}, u32[]{:S(2)}, u32[]{:S(2)}) collective-permute-start(bf16[256,640]{1,0:T(8,128)(2,1)S(1)} %get-tuple-element.66), channel_id=1, source_target_pairs={{0,4},{2,6},{4,0},{6,2},{8,12},{10,14},{12,8},{14,10},{16,20},{18,... | collective-permute-start | bytes 983048 | tf_op jit(solution)/shard_map/ppermute | solution.py:62
  34.8 1.5 %collective-permute-start.12 = (bf16[2,4,48,256]{3,2,1,0:T(8,128)(2,1)S(1)}, bf16[2,4,48,256]{3,2,1,0:T(8,128)(2,1)S(1)}, u32[]{:S(2)}, u32[]{:S(2)}) collective-permute-start(bf16[2,4,48,256]{3,2,1,0:T(8,128)(2,1)S(1)} %get-tuple-element.67.refs_0_), channel_id=1, source_target_pairs={{0,1},{1,0},{2,3},{3,2},{4,5},{5,4},{6,7},{7,6},{8,9},{9,8},{10,11... | collective-permute-start | bytes 589832 | tf_op jit(solution)/shard_map/ppermute | solution.py:62
  36.3 2.0 %product_3.1 = (f32[256,640]{1,0:T(8,128)S(1)}, bf16[256,640]{1,0:T(8,128)(2,1)S(1)}) custom-call(bf16[2,4,64,256]{3,2,1,0:T(8,128)(2,1)S(1)} %get-tuple-element.60.refs_0_, bf16[2,4,64,256]{3,2,1,0:T(8,128)(2,1)S(1)} %collective-permute-done.8.refs_1_.refs_6_, bf16[4,640,256]{2,1,0:T(8,128)(2,1)S(1)} %get-tuple-element.50.refs_1_.refs_2_, ...), custom_call_target="tpu_custom_call" | custom-call | flops 385000000 | bytes 10000 | tf_op jit(solution)/shard_map/product_3/pallas_call | solution.py:295
  38.4 1.9 %collective-permute-start.16 = (bf16[256,640]{1,0:T(8,128)(2,1)S(1)}, bf16[256,640]{1,0:T(8,128)(2,1)S(1)}, u32[]{:S(2)}, u32[]{:S(2)}) collective-permute-start(bf16[256,640]{1,0:T(8,128)(2,1)S(1)} %get-tuple-element.74), channel_id=1, source_target_pairs={{0,8},{2,10},{4,12},{6,14},{8,0},{10,2},{12,4},{14,6},{16,24},{18,... | collective-permute-start | bytes 983048 | tf_op jit(solution)/shard_map/ppermute | solution.py:62
  40.4 1.8 %collective-permute-start.10 = (bf16[160,640]{1,0:T(8,128)(2,1)S(1)}, bf16[160,640]{1,0:T(8,128)(2,1)S(1)}, u32[]{:S(2)}, u32[]{:S(2)}) collective-permute-start(bf16[160,640]{1,0:T(8,128)(2,1)S(1)} %get-tuple-element.65), channel_id=1, source_target_pairs={{0,4},{2,6},{4,0},{6,2},{8,12},{10,14},{12,8},{14,10},{16,20},{18,... | collective-permute-start | bytes 614408 | tf_op jit(solution)/shard_map/ppermute | solution.py:62
  42.1 1.9 %product_4.1 = (f32[192,640]{1,0:T(8,128)S(1)}, bf16[192,640]{1,0:T(8,128)(2,1)S(1)}) custom-call(bf16[2,4,48,256]{3,2,1,0:T(8,128)(2,1)S(1)} %get-tuple-element.67.refs_0_, bf16[2,4,48,256]{3,2,1,0:T(8,128)(2,1)S(1)} %collective-permute-done.12.refs_1_.refs_6_, bf16[4,640,256]{2,1,0:T(8,128)(2,1)S(1)} %get-tuple-element.50.refs_1_.refs_2_, ...), custom_call_target="tpu_custom_call" | custom-call | flops 345000000 | bytes 10000 | tf_op jit(solution)/shard_map/product_4/pallas_call | solution.py:295
  45.4 2.3 %collective-permute-done.10.refs_1_.refs_2_ = bf16[160,640]{1,0:T(8,128)(2,1)S(1)} collective-permute-done((bf16[160,640]{1,0:T(8,128)(2,1)S(1)}, bf16[160,640]{1,0:T(8,128)(2,1)S(1)}, u32[]{:S(2)}, u32[]{:S(2)}) %collective-permute-start.10) | collective-permute-done | bytes 204832 | tf_op jit(solution)/shard_map/ppermute | solution.py:62
  48.8 1.6 %collective-permute-start.18 = (bf16[128,640]{1,0:T(8,128)(2,1)S(1)}, bf16[128,640]{1,0:T(8,128)(2,1)S(1)}, u32[]{:S(2)}, u32[]{:S(2)}) collective-permute-start(bf16[128,640]{1,0:T(8,128)(2,1)S(1)} %get-tuple-element.79), channel_id=1, source_target_pairs={{0,4},{2,6},{4,0},{6,2},{8,12},{10,14},{12,8},{14,10},{16,20},{18,... | collective-permute-start | bytes 491528 | tf_op jit(solution)/shard_map/ppermute | solution.py:62
  50.4 3.4 %collective-permute-start.13 = (bf16[80,640]{1,0:T(8,128)(2,1)S(1)}, bf16[80,640]{1,0:T(8,128)(2,1)S(1)}, u32[]{:S(2)}, u32[]{:S(2)}) collective-permute-start(bf16[80,640]{1,0:T(8,128)(2,1)S(1)} %get-tuple-element.71), channel_id=1, source_target_pairs={{0,16},{2,18},{4,20},{6,22},{8,24},{10,26},{12,28},{14,30},{16,0},... | collective-permute-start | bytes 307208 | tf_op jit(solution)/shard_map/ppermute | solution.py:62
  54.0 2.9 %collective-permute-start.17 = (bf16[64,640]{1,0:T(8,128)(2,1)S(1)}, bf16[64,640]{1,0:T(8,128)(2,1)S(1)}, u32[]{:S(2)}, u32[]{:S(2)}) collective-permute-start(bf16[64,640]{1,0:T(8,128)(2,1)S(1)} %get-tuple-element.78), channel_id=1, source_target_pairs={{0,16},{2,18},{4,20},{6,22},{8,24},{10,26},{12,28},{14,30},{16,0},... | collective-permute-start | bytes 245768 | tf_op jit(solution)/shard_map/ppermute | solution.py:62
  56.9 4.3 %collective-permute-done.13.refs_1_.refs_2_ = bf16[80,640]{1,0:T(8,128)(2,1)S(1)} collective-permute-done((bf16[80,640]{1,0:T(8,128)(2,1)S(1)}, bf16[80,640]{1,0:T(8,128)(2,1)S(1)}, u32[]{:S(2)}, u32[]{:S(2)}) %collective-permute-start.13) | collective-permute-done | bytes 102432 | tf_op jit(solution)/shard_map/ppermute | solution.py:62
  61.3 1.8 %collective-permute-done.17.refs_1_.refs_2_ = bf16[64,640]{1,0:T(8,128)(2,1)S(1)} collective-permute-done((bf16[64,640]{1,0:T(8,128)(2,1)S(1)}, bf16[64,640]{1,0:T(8,128)(2,1)S(1)}, u32[]{:S(2)}, u32[]{:S(2)}) %collective-permute-start.17) | collective-permute-done | bytes 81952 | tf_op jit(solution)/shard_map/ppermute | solution.py:62
  63.2 1.2 %collective-permute-start.21 = (bf16[48,640]{1,0:T(8,128)(2,1)S(1)}, bf16[48,640]{1,0:T(8,128)(2,1)S(1)}, u32[]{:S(2)}, u32[]{:S(2)}) collective-permute-start(bf16[48,640]{1,0:T(8,128)(2,1)S(1)} %get-tuple-element.84), channel_id=1, source_target_pairs={{0,16},{2,18},{4,20},{6,22},{8,24},{10,26},{12,28},{14,30},{16,0},... | collective-permute-start | bytes 184328 | tf_op jit(solution)/shard_map/ppermute | solution.py:62
  64.4 2.7 %collective-permute-done.19.refs_1_.refs_2_ = bf16[64,640]{1,0:T(8,128)(2,1)S(1)} collective-permute-done((bf16[64,640]{1,0:T(8,128)(2,1)S(1)}, bf16[64,640]{1,0:T(8,128)(2,1)S(1)}, u32[]{:S(2)}, u32[]{:S(2)}) %collective-permute-start.19) | collective-permute-done | bytes 81952 | tf_op jit(solution)/shard_map/ppermute | solution.py:62
  67.1 1.3 %collective-permute-done.21.refs_4_ = bf16[48,640]{1,0:T(8,128)(2,1)S(1)} collective-permute-done((bf16[48,640]{1,0:T(8,128)(2,1)S(1)}, bf16[48,640]{1,0:T(8,128)(2,1)S(1)}, u32[]{:S(2)}, u32[]{:S(2)}) %collective-permute-start.21) | collective-permute-done | bytes 61472 | tf_op jit(solution)/shard_map/ppermute | solution.py:62
  (52 shorter events, 5.5 us)
Async XLA Ops:
  0.0 3.6 %copy-start.1 = (bf16[256,256]{1,0:T(8,128)(2,1)S(1)}, bf16[256,256]{1,0:T(8,128)(2,1)}, u32[]{:S(2)}) copy-start(bf16[256,256]{1,0:T(8,128)(2,1)} %constant.8.clone.refs_4_.refs_3_) | copy-start | bytes 393220
  0.0 3.6 %copy-start.7 = (s32[640]{0:T(1024)S(1)}, s32[640]{0:T(1024)}, u32[]{:S(2)}) copy-start(s32[640]{0:T(1024)} %param.11) | copy-start | bytes 7684
  0.0 3.6 %copy-start.6 = (bf16[128]{0:T(256)(128)(2,1)S(1)}, bf16[128]{0:T(256)(128)(2,1)}, u32[]{:S(2)}) copy-start(bf16[128]{0:T(256)(128)(2,1)} %param.9) | copy-start | bytes 772
  0.0 3.7 %copy-start = (bf16[640,4096]{1,0:T(8,128)(2,1)S(1)}, bf16[640,4096]{1,0:T(8,128)(2,1)}, u32[]{:S(2)}) copy-start(bf16[640,4096]{1,0:T(8,128)(2,1)} %refs_0_.5) | copy-start | bytes 15728644
  0.0 3.7 %copy-start.5 = (s32[512]{0:T(512)S(1)}, s32[512]{0:T(512)}, u32[]{:S(2)}) copy-start(s32[512]{0:T(512)} %param.10) | copy-start | bytes 6148
  1.1 6.4 %collective-permute-start = (bf16[640,128]{1,0:T(8,128)(2,1)S(1)}, bf16[640,128]{1,0:T(8,128)(2,1)S(1)}, u32[]{:S(2)}, u32[]{:S(2)}) collective-permute-start(bf16[640,128]{1,0:T(8,128)(2,1)S(1)} %history.1.refs_6_), channel_id=1, source_target_pairs={{0,2},{2,4},{4,6},{6,8},{8,10},{10,12},{12,14},{14,16},{16,18},{18... | collective-permute-start | bytes 491528 | tf_op jit(solution)/shard_map/ppermute | solution.py:337
  3.7 0.8 %copy-start.2 = (bf16[256,128]{1,0:T(8,128)(2,1)S(1)}, bf16[256,128]{1,0:T(8,128)(2,1)}, u32[]{:S(2)}) copy-start(bf16[256,128]{1,0:T(8,128)(2,1)} %constant.9.clone.refs_5_.refs_4_) | copy-start | bytes 196612
  9.2 10.6 %collective-permute-start.3 = (bf16[4,640,256]{2,1,0:T(8,128)(2,1)S(1)}, bf16[4,640,256]{2,1,0:T(8,128)(2,1)S(1)}, u32[]{:S(2)}, u32[]{:S(2)}) collective-permute-start(bf16[4,640,256]{2,1,0:T(8,128)(2,1)S(1)} %get-tuple-element.50.refs_1_.refs_2_), channel_id=1, source_target_pairs={{0,2},{2,0},{4,6},{6,4},{8,10},{10,8},{12,14},{14,12},{16,18},{18,... | collective-permute-start | bytes 3932168 | tf_op jit(solution)/shard_map/ppermute | solution.py:62
  11.8 4.3 %collective-permute-start.1 = (bf16[4,32,256]{2,1,0:T(8,128)(2,1)S(1)}, bf16[4,32,256]{2,1,0:T(8,128)(2,1)S(1)}, u32[]{:S(2)}, u32[]{:S(2)}) collective-permute-start(bf16[4,32,256]{2,1,0:T(8,128)(2,1)S(1)} %get-tuple-element.49.refs_2_.refs_0_), channel_id=1, source_target_pairs={{0,1},{1,0},{2,3},{3,2},{4,5},{5,4},{6,7},{7,6},{8,9},{9,8},{10,11... | collective-permute-start | bytes 196616 | tf_op jit(solution)/shard_map/ppermute | solution.py:62
  14.3 1.9 %collective-permute-start.4 = (bf16[4,240,256]{2,1,0:T(8,128)(2,1)S(1)}, bf16[4,240,256]{2,1,0:T(8,128)(2,1)S(1)}, u32[]{:S(2)}, u32[]{:S(2)}) collective-permute-start(bf16[4,240,256]{2,1,0:T(8,128)(2,1)S(1)} %get-tuple-element.54), channel_id=1, source_target_pairs={{0,2},{2,0},{4,6},{6,4},{8,10},{10,8},{12,14},{14,12},{16,18},{18,... | collective-permute-start | bytes 1474568 | tf_op jit(solution)/shard_map/ppermute | solution.py:62
  16.2 3.6 %copy-start.3 = (f32[8,128]{1,0:T(8,128)S(1)}, f32[8,128]{1,0:T(8,128)}, u32[]{:S(2)}) copy-start(f32[8,128]{1,0:T(8,128)} %constant.10.clone.refs_4_) | copy-start | bytes 12292
  16.2 3.6 %copy-start.4 = (f32[8,128]{1,0:T(8,128)S(1)}, f32[8,128]{1,0:T(8,128)}, u32[]{:S(2)}) copy-start(f32[8,128]{1,0:T(8,128)} %constant.11.clone.refs_5_) | copy-start | bytes 12292
  16.3 9.2 %collective-permute-start.6 = (bf16[2,4,64,256]{3,2,1,0:T(8,128)(2,1)S(1)}, bf16[2,4,64,256]{3,2,1,0:T(8,128)(2,1)S(1)}, u32[]{:S(2)}, u32[]{:S(2)}) collective-permute-start(bf16[2,4,64,256]{3,2,1,0:T(8,128)(2,1)S(1)} %get-tuple-element.55.refs_6_.refs_0_), channel_id=1, source_target_pairs={{0,1},{1,0},{2,3},{3,2},{4,5},{5,4},{6,7},{7,6},{8,9},{9,8},{10,11... | collective-permute-start | bytes 786440 | tf_op jit(solution)/shard_map/ppermute | solution.py:62
  17.8 13.3 %collective-permute-start.9 = (bf16[2,4,64,256]{3,2,1,0:T(8,128)(2,1)S(1)}, bf16[2,4,64,256]{3,2,1,0:T(8,128)(2,1)S(1)}, u32[]{:S(2)}, u32[]{:S(2)}) collective-permute-start(bf16[2,4,64,256]{3,2,1,0:T(8,128)(2,1)S(1)} %get-tuple-element.61.refs_0_), channel_id=1, source_target_pairs={{0,1},{1,0},{2,3},{3,2},{4,5},{5,4},{6,7},{7,6},{8,9},{9,8},{10,11... | collective-permute-start | bytes 786440 | tf_op jit(solution)/shard_map/ppermute | solution.py:62
  18.4 1.5 %collective-permute-start.2 = (bf16[4,16,256]{2,1,0:T(8,128)(2,1)S(1)}, bf16[4,16,256]{2,1,0:T(8,128)(2,1)S(1)}, u32[]{:S(2)}, u32[]{:S(2)}) collective-permute-start(bf16[4,16,256]{2,1,0:T(8,128)(2,1)S(1)} %get-tuple-element.53), channel_id=1, source_target_pairs={{0,2},{2,0},{4,6},{6,4},{8,10},{10,8},{12,14},{14,12},{16,18},{18,... | collective-permute-start | bytes 98312 | tf_op jit(solution)/shard_map/ppermute | solution.py:62
  18.4 17.9 %collective-permute-start.8 = (bf16[2,4,64,256]{3,2,1,0:T(8,128)(2,1)S(1)}, bf16[2,4,64,256]{3,2,1,0:T(8,128)(2,1)S(1)}, u32[]{:S(2)}, u32[]{:S(2)}) collective-permute-start(bf16[2,4,64,256]{3,2,1,0:T(8,128)(2,1)S(1)} %get-tuple-element.60.refs_0_), channel_id=1, source_target_pairs={{0,1},{1,0},{2,3},{3,2},{4,5},{5,4},{6,7},{7,6},{8,9},{9,8},{10,11... | collective-permute-start | bytes 786440 | tf_op jit(solution)/shard_map/ppermute | solution.py:62
  21.6 9.5 %collective-permute-start.5 = (bf16[64,640]{1,0:T(8,128)(2,1)S(1)}, bf16[64,640]{1,0:T(8,128)(2,1)S(1)}, u32[]{:S(2)}, u32[]{:S(2)}) collective-permute-start(bf16[64,640]{1,0:T(8,128)(2,1)S(1)} %get-tuple-element.57), channel_id=1, source_target_pairs={{0,8},{2,10},{4,12},{6,14},{8,0},{10,2},{12,4},{14,6},{16,24},{18,... | collective-permute-start | bytes 245768 | tf_op jit(solution)/shard_map/ppermute | solution.py:62
  27.6 12.7 %collective-permute-start.7 = (bf16[256,640]{1,0:T(8,128)(2,1)S(1)}, bf16[256,640]{1,0:T(8,128)(2,1)S(1)}, u32[]{:S(2)}, u32[]{:S(2)}) collective-permute-start(bf16[256,640]{1,0:T(8,128)(2,1)S(1)} %get-tuple-element.59), channel_id=1, source_target_pairs={{0,8},{2,10},{4,12},{6,14},{8,0},{10,2},{12,4},{14,6},{16,24},{18,... | collective-permute-start | bytes 983048 | tf_op jit(solution)/shard_map/ppermute | solution.py:62
  33.2 11.3 %collective-permute-start.11 = (bf16[256,640]{1,0:T(8,128)(2,1)S(1)}, bf16[256,640]{1,0:T(8,128)(2,1)S(1)}, u32[]{:S(2)}, u32[]{:S(2)}) collective-permute-start(bf16[256,640]{1,0:T(8,128)(2,1)S(1)} %get-tuple-element.66), channel_id=1, source_target_pairs={{0,4},{2,6},{4,0},{6,2},{8,12},{10,14},{12,8},{14,10},{16,20},{18,... | collective-permute-start | bytes 983048 | tf_op jit(solution)/shard_map/ppermute | solution.py:62
  34.8 7.3 %collective-permute-start.12 = (bf16[2,4,48,256]{3,2,1,0:T(8,128)(2,1)S(1)}, bf16[2,4,48,256]{3,2,1,0:T(8,128)(2,1)S(1)}, u32[]{:S(2)}, u32[]{:S(2)}) collective-permute-start(bf16[2,4,48,256]{3,2,1,0:T(8,128)(2,1)S(1)} %get-tuple-element.67.refs_0_), channel_id=1, source_target_pairs={{0,1},{1,0},{2,3},{3,2},{4,5},{5,4},{6,7},{7,6},{8,9},{9,8},{10,11... | collective-permute-start | bytes 589832 | tf_op jit(solution)/shard_map/ppermute | solution.py:62
  38.4 10.3 %collective-permute-start.16 = (bf16[256,640]{1,0:T(8,128)(2,1)S(1)}, bf16[256,640]{1,0:T(8,128)(2,1)S(1)}, u32[]{:S(2)}, u32[]{:S(2)}) collective-permute-start(bf16[256,640]{1,0:T(8,128)(2,1)S(1)} %get-tuple-element.74), channel_id=1, source_target_pairs={{0,8},{2,10},{4,12},{6,14},{8,0},{10,2},{12,4},{14,6},{16,24},{18,... | collective-permute-start | bytes 983048 | tf_op jit(solution)/shard_map/ppermute | solution.py:62
  40.4 7.4 %collective-permute-start.10 = (bf16[160,640]{1,0:T(8,128)(2,1)S(1)}, bf16[160,640]{1,0:T(8,128)(2,1)S(1)}, u32[]{:S(2)}, u32[]{:S(2)}) collective-permute-start(bf16[160,640]{1,0:T(8,128)(2,1)S(1)} %get-tuple-element.65), channel_id=1, source_target_pairs={{0,4},{2,6},{4,0},{6,2},{8,12},{10,14},{12,8},{14,10},{16,20},{18,... | collective-permute-start | bytes 614408 | tf_op jit(solution)/shard_map/ppermute | solution.py:62
  44.1 9.7 %collective-permute-start.14 = (bf16[192,640]{1,0:T(8,128)(2,1)S(1)}, bf16[192,640]{1,0:T(8,128)(2,1)S(1)}, u32[]{:S(2)}, u32[]{:S(2)}) collective-permute-start(bf16[192,640]{1,0:T(8,128)(2,1)S(1)} %get-tuple-element.72), channel_id=1, source_target_pairs={{0,4},{2,6},{4,0},{6,2},{8,12},{10,14},{12,8},{14,10},{16,20},{18,... | collective-permute-start | bytes 737288 | tf_op jit(solution)/shard_map/ppermute | solution.py:62
  44.6 9.2 %collective-permute-start.15 = (bf16[128,640]{1,0:T(8,128)(2,1)S(1)}, bf16[128,640]{1,0:T(8,128)(2,1)S(1)}, u32[]{:S(2)}, u32[]{:S(2)}) collective-permute-start(bf16[128,640]{1,0:T(8,128)(2,1)S(1)} %get-tuple-element.73), channel_id=1, source_target_pairs={{0,8},{2,10},{4,12},{6,14},{8,0},{10,2},{12,4},{14,6},{16,24},{18,... | collective-permute-start | bytes 491528 | tf_op jit(solution)/shard_map/ppermute | solution.py:62
  48.8 12.4 %collective-permute-start.18 = (bf16[128,640]{1,0:T(8,128)(2,1)S(1)}, bf16[128,640]{1,0:T(8,128)(2,1)S(1)}, u32[]{:S(2)}, u32[]{:S(2)}) collective-permute-start(bf16[128,640]{1,0:T(8,128)(2,1)S(1)} %get-tuple-element.79), channel_id=1, source_target_pairs={{0,4},{2,6},{4,0},{6,2},{8,12},{10,14},{12,8},{14,10},{16,20},{18,... | collective-permute-start | bytes 491528 | tf_op jit(solution)/shard_map/ppermute | solution.py:62
  50.4 10.8 %collective-permute-start.13 = (bf16[80,640]{1,0:T(8,128)(2,1)S(1)}, bf16[80,640]{1,0:T(8,128)(2,1)S(1)}, u32[]{:S(2)}, u32[]{:S(2)}) collective-permute-start(bf16[80,640]{1,0:T(8,128)(2,1)S(1)} %get-tuple-element.71), channel_id=1, source_target_pairs={{0,16},{2,18},{4,20},{6,22},{8,24},{10,26},{12,28},{14,30},{16,0},... | collective-permute-start | bytes 307208 | tf_op jit(solution)/shard_map/ppermute | solution.py:62
  53.9 9.2 %collective-permute-start.20 = (bf16[96,640]{1,0:T(8,128)(2,1)S(1)}, bf16[96,640]{1,0:T(8,128)(2,1)S(1)}, u32[]{:S(2)}, u32[]{:S(2)}) collective-permute-start(bf16[96,640]{1,0:T(8,128)(2,1)S(1)} %get-tuple-element.82), channel_id=1, source_target_pairs={{0,8},{2,10},{4,12},{6,14},{8,0},{10,2},{12,4},{14,6},{16,24},{18,... | collective-permute-start | bytes 368648 | tf_op jit(solution)/shard_map/ppermute | solution.py:62
  54.0 9.1 %collective-permute-start.17 = (bf16[64,640]{1,0:T(8,128)(2,1)S(1)}, bf16[64,640]{1,0:T(8,128)(2,1)S(1)}, u32[]{:S(2)}, u32[]{:S(2)}) collective-permute-start(bf16[64,640]{1,0:T(8,128)(2,1)S(1)} %get-tuple-element.78), channel_id=1, source_target_pairs={{0,16},{2,18},{4,20},{6,22},{8,24},{10,26},{12,28},{14,30},{16,0},... | collective-permute-start | bytes 245768 | tf_op jit(solution)/shard_map/ppermute | solution.py:62
  61.3 5.8 %collective-permute-start.19 = (bf16[64,640]{1,0:T(8,128)(2,1)S(1)}, bf16[64,640]{1,0:T(8,128)(2,1)S(1)}, u32[]{:S(2)}, u32[]{:S(2)}) collective-permute-start(bf16[64,640]{1,0:T(8,128)(2,1)S(1)} %get-tuple-element.81), channel_id=1, source_target_pairs={{0,16},{2,18},{4,20},{6,22},{8,24},{10,26},{12,28},{14,30},{16,0},... | collective-permute-start | bytes 245768 | tf_op jit(solution)/shard_map/ppermute | solution.py:62
  63.2 5.2 %collective-permute-start.21 = (bf16[48,640]{1,0:T(8,128)(2,1)S(1)}, bf16[48,640]{1,0:T(8,128)(2,1)S(1)}, u32[]{:S(2)}, u32[]{:S(2)}) collective-permute-start(bf16[48,640]{1,0:T(8,128)(2,1)S(1)} %get-tuple-element.84), channel_id=1, source_target_pairs={{0,16},{2,18},{4,20},{6,22},{8,24},{10,26},{12,28},{14,30},{16,0},... | collective-permute-start | bytes 184328 | tf_op jit(solution)/shard_map/ppermute | solution.py:62

commit v3 on v2

--- a/solution.py
+++ b/solution.py
@@ -18,25 +18,28 @@
 DECIM = 4
 SPAN = DECIM * TD
 VMEM_LIMIT = 20 * 1024 * 1024
-BLOCK = 320
-CHUNKS = (2, 8, 8, 8, 6)
-FIRST = (1, 1, 0, 1, 0)
-SECOND = ((2,), (4,), (0, 1), (3,))
+CHUNKS = (10, 8, 8, 6)
+FIRST = (1, 0, 1, 0)
+SECOND = ((1,), (3,), (0,), (2,))
 THIRD = ((2,), (0,), (3,), (1,))
+ACROSS = ((1,), (2,), (3,))
 PLAN = (
+    ('merge', 0, (1, 2, 3), ()),
     ('split', 0, (), ()),
-    ('merge', 0, (1, 2, 3, 4), ()),
-    ('product', 0, (), ()),
-    ('product', 1, (), (('y', 1),)),
-    ('product', 2, (), (('y', 2), ('first', 0))),
-    ('product', 3, (), (('y', 3),)),
-    ('second', 2, (), (('first', 1),)),
-    ('product', 4, (), (('y', 4),)),
-    ('second', 0, (), (('first', 2),)),
-    ('third', 0, (), (('second', 2),)),
-    ('second', 3, (), (('first', 3),)),
+    ('send', 0, (), ()),
+    ('keep', 0, (), ()),
+    ('send', 1, (), (('y', 1),)),
+    ('keep', 1, (), ()),
+    ('send', 2, (), (('y', 2),)),
+    ('keep', 2, (), ()),
+    ('second', 2, (), (('first', 0),)),
+    ('send', 3, (), (('y', 3), ('first', 1))),
+    ('second', 0, (), ()),
+    ('keep', 3, (), ()),
+    ('third', 0, (), ()),
+    ('second', 3, (), (('first', 2), ('second', 2))),
     ('third', 1, (), (('second', 0),)),
-    ('second', 1, (), (('first', 4),)),
+    ('second', 1, (), (('first', 3),)),
     ('sum', 0, (), (('third', 0),)),
     ('third', 2, (), (('second', 3),)),
     ('sum', 1, (), (('third', 1),)),
@@ -44,7 +47,32 @@
     ('sum', 2, (), (('third', 2),)),
 )
 BASE_COST = 0.05
-COSTS = {'split_0': 8, 'merge_0': 1, 'product_0': 0.265, 'product_1': 0.558, 'product_2': 0.604, 'product_3': 0.385, 'second_2': 0.186, 'product_4': 0.345, 'second_0': 0.23, 'third_0': 0.266, 'second_3': 0.245, 'third_1': 0.266, 'second_1': 0.186, 'sum_0': 0.047, 'third_2': 0.271, 'sum_1': 0.111, 'third_3': 0.368, 'sum_2': 0.293}
+COSTS = {
+    'merge_0': 0.52,
+    'split_0': 0.165,
+    'send_0': 0.297,
+    'keep_0': 0.182,
+    'send_1': 15,
+    'keep_1': 0.347,
+    'send_2': 0.277,
+    'second_2': 0.191,
+    'keep_2': 0.112,
+    'send_3': 0.275,
+    'second_0': 0.191,
+    'keep_3': 0.11,
+    'third_0': 0.286,
+    'second_3': 0.191,
+    'third_1': 0.286,
+    'second_1': 4,
+    'sum_0': 0.027,
+    'third_2': 0.304,
+    'sum_1': 1,
+    'third_3': 0.373,
+    'sum_2': 0.293,
+    'panels': 0.5,
+    'gate': 0.05,
+    'first': 0.5,
+}
 
 VMEM = pl.BlockSpec(memory_space=pltpu.VMEM)
 ANY = pl.BlockSpec(memory_space=pl.ANY)
@@ -180,24 +208,29 @@
         panel_ref[w] = pick(select, white_ref[w])
 
 
-def panels_kernel(skip, counts, select_ref, white_ref, own_ref, other_ref):
+def panels_kernel(skip, groups, select_ref, white_ref, *refs):
+    own_refs, other_refs = refs[: len(groups)], refs[len(groups) :]
     for w in range(white_ref.shape[0]):
         chosen = pick(select_ref[skip:], white_ref[w])
-        row, place = 0, 0
-        for count in counts:
-            own_ref[w, place : place + count] = chosen[row : row + count]
-            other_ref[w, place : place + count] = chosen[row + count : row + 2 * count]
-            row += 2 * count
-            place += count
-
-
-def merge_kernel(own_ref, sib_ref, *panel_refs):
-    row = 0
-    for panel_ref in panel_refs:
-        count = panel_ref.shape[2]
-        panel_ref[0] = own_ref[:, row : row + count]
-        panel_ref[1] = sib_ref[:, row : row + count]
-        row += count
+        row = 0
+        for group, own_ref, other_ref in zip(groups, own_refs, other_refs):
+            place = 0
+            for count in group:
+                own_ref[w, place : place + count] = chosen[row : row + count]
+                other_ref[w, place : place + count] = chosen[row + count : row + 2 * count]
+                row += 2 * count
+                place += count
+
+
+def merge_kernel(*refs):
+    groups = len(refs) // 3
+    for own_ref, sib_ref, panel_ref in zip(refs[:groups], refs[groups : 2 * groups], refs[2 * groups :]):
+        panel_ref[0] = own_ref[...]
+        panel_ref[1] = sib_ref[...]
+
+
+def gate_kernel(table_ref, out_ref):
+    out_ref[...] = jnp.zeros_like(out_ref)
 
 
 def split_kernel(panel_ref, recv_ref, keep_ref, send_ref):
@@ -206,42 +239,41 @@
     send_ref[...] = panel_ref[:, count:] + recv_ref[:, count:]
 
 
-def product_kernel(sources, white_ref, white_sib_ref, cos_ref, sin_ref, keep_ref, send_ref, lag_ref):
+def product_kernel(sources, begin, white_ref, white_sib_ref, cos_ref, sin_ref, out_ref):
     windows = white_ref.shape[0]
-    half = keep_ref.shape[0]
+    count = out_ref.shape[0]
     cos_lag = cos_ref[...][None]
     sin_lag = sin_ref[...][None]
+    white = jnp.concatenate(
+        [ref[w] for ref in (white_ref, white_sib_ref) for w in range(windows)], axis=1
+    )
+    parts = []
     for side in range(2):
         for w in range(windows):
-            source = sources(side, w)
-            count = source.shape[0]
+            source = sources(side, w, begin // NLAG, count // NLAG)
             real_src = source[:, None, :HALF]
             imag_src = source[:, None, HALF:]
-            real_out = real_src * cos_lag + imag_src * sin_lag
-            imag_out = imag_src * cos_lag - real_src * sin_lag
-            k = (side * windows + w) * TD
-            lag_ref[:, k : k + HALF] = real_out.reshape(count * NLAG, HALF).astype(jnp.bfloat16)
-            lag_ref[:, k + HALF : k + TD] = imag_out.reshape(count * NLAG, HALF).astype(jnp.bfloat16)
-    white = jnp.concatenate(
-        [ref[w] for ref in (white_ref, white_sib_ref) for w in range(windows)], axis=1
-    )
-    blocks = -(-half // BLOCK)
-    size = half // blocks
-    for row in range(0, half, size):
-        send_ref[row : row + size] = nt_dot(lag_ref[half + row : half + row + size], white).astype(jnp.bfloat16)
-    for row in range(0, half, size):
-        keep_ref[row : row + size] = nt_dot(lag_ref[row : row + size], white)
-
-
-def taken_kernel(own_ref, sib_ref, *refs):
-    product_kernel(lambda side, w: (own_ref, sib_ref)[side][w].astype(jnp.float32), *refs)
-
-
-def summed_kernel(panel_ref, recv_ref, *refs):
-    def sources(side, w):
-        return panel_ref[side, w].astype(jnp.float32) + recv_ref[side, w].astype(jnp.float32)
-
-    product_kernel(sources, *refs)
+            for part in (
+                real_src * cos_lag + imag_src * sin_lag,
+                imag_src * cos_lag - real_src * sin_lag,
+            ):
+                parts.append(part.reshape(count, HALF).astype(jnp.bfloat16))
+    out_ref[...] = nt_dot(jnp.concatenate(parts, axis=1), white).astype(out_ref.dtype)
+
+
+def taken_kernel(first, own_ref, sib_ref, *refs):
+    def sources(side, w, begin, count):
+        return (own_ref, sib_ref)[side][w, begin : begin + count].astype(jnp.float32)
+
+    product_kernel(sources, first, *refs)
+
+
+def summed_kernel(place, first, panel_ref, recv_ref, *refs):
+    def sources(side, w, begin, count):
+        rows = slice(place + begin, place + begin + count)
+        return panel_ref[side, w, rows].astype(jnp.float32) + recv_ref[side, w, rows].astype(jnp.float32)
+
+    product_kernel(sources, first, *refs)
 
 
 def halves_kernel(pieces, *refs):
@@ -264,26 +296,33 @@
 
 
 def last_kernel(pieces, *refs):
-    *parts, out_ref = refs
+    *parts, out_ref, late_ref, sems = refs
     parts = iter(parts)
-    for summed, places in pieces:
+    copies, place = [], 0
+    for summed, places in sorted(pieces, key=lambda piece: not piece[0]):
         keep_ref = next(parts)
         recv_ref = None if summed else next(parts)
         row = 0
         for begin, count in places:
-            rows = slice(row, row + count)
-            value = keep_ref[rows, :]
+            source = keep_ref.at[row : row + count]
             if not summed:
-                value = value + recv_ref[rows, :].astype(jnp.float32)
-            out_ref[begin : begin + count, :] = value
+                rows = slice(row, row + count)
+                late_ref[place : place + count] = keep_ref[rows, :] + recv_ref[rows, :].astype(jnp.float32)
+                source = late_ref.at[place : place + count]
+                place += count
+            copy = pltpu.make_async_copy(source, out_ref.at[begin : begin + count], sems.at[len(copies)])
+            copy.start()
+            copies.append(copy)
             row += count
+    for copy in copies:
+        copy.wait()
 
 
 class Chain:
     def __init__(self):
         self.last = None
 
-    def __call__(self, name, kernel, args, outs, scratch=(), gates=(), waits=(), limit=VMEM_LIMIT, first=VMEM):
+    def __call__(self, name, kernel, args, outs, scratch=(), gates=(), waits=(), limit=VMEM_LIMIT, first=VMEM, result=VMEM):
         args, gates = list(args), list(gates)
         order = [*waits] if self.last is None else [*waits, self.last]
         taken, passed = len(args), len(args) + len(gates) + len(order)
@@ -296,7 +335,7 @@
             body,
             out_shape=[*outs, *(jax.ShapeDtypeStruct(g.shape, g.dtype) for g in gates)],
             in_specs=[first] + [VMEM] * (taken - 1) + [ANY] * (len(gates) + len(order)),
-            out_specs=[VMEM] * len(outs) + [ANY] * len(gates),
+            out_specs=[result] * len(outs) + [ANY] * len(gates),
             input_output_aliases={taken + i: len(outs) + i for i in range(len(gates))},
             scratch_shapes=list(scratch),
             compiler_params=params(limit),
@@ -317,10 +356,13 @@
     codes = time_parts // 2
     bits = [1 << i for i in range(1, time_parts.bit_length() - 1)]
     sizes, firsts, seconds, thirds, plan = CHUNKS, FIRST, SECOND, THIRD, PLAN
+    across_groups = ACROSS
     if per_dest != sum(CHUNKS) or len(bits) != 3:
         sizes, firsts = (per_dest // 2,) * 2, (0, 0)
         seconds = thirds = ((0,), (1,))
-        plan = [("split", 0, (), ()), ("merge", 0, (), ()), ("product", 0, (1,), ()), ("product", 1, (), ())]
+        across_groups = ((1,),)
+        plan = [("split", 0, (), ()), ("merge", 0, (1,), ())]
+        plan += [(kind, q, (), ()) for q in (0, 1) for kind in ("send", "keep")]
         final = "third" + "+" * (len(bits) - 3)
         plan += [(name, q, (), ()) for name in ("second", *(final[:5 + i] for i in range(len(final) - 4))) for q in (0, 1)]
     final = "third" + "+" * (len(bits) - 3)
@@ -355,12 +397,12 @@
         [raw_traces, history, fir, table, band, alive, late_white, select],
         [shape((windows, 2 * counts[0], TD), bf16), shape((windows, rows, TD), bf16)],
     )
-    rest = shape((windows, sum(counts[1:]), TD), bf16)
-    own, other = chain(
-        "panels", functools.partial(panels_kernel, 2 * counts[0], counts[1:]), [select, white], [rest, rest]
-    )
+    members = [[counts[chunk] for chunk in group] for group in across_groups]
+    rest = [shape((windows, sum(group), TD), bf16) for group in members]
+    parts = chain("panels", functools.partial(panels_kernel, 2 * counts[0], members), [select, white], rest + rest)
+    own, sib = parts[: len(rest)], [swap(other, "tm", 1) for other in parts[len(rest) :]]
+    _, white = chain("gate", gate_kernel, [table], [shape((8, HALF), f32)], gates=[white])
     white_sib = swap(white, "tm", 1)
-    sib = swap(other, "tm", 1)
     tables = [jnp.asarray(t) for t in lag_tables(1.0 / math.sqrt(time_parts * windows * TD))]
     spectra = [white, white_sib, *tables]
 
@@ -382,20 +424,26 @@
             keep, send, *let = call(split_kernel, [panel, across(panel)], [half, half])
             taken = [keep, swap(send, "tm", 1)]
         elif kind == "merge":
-            made = call(merge_kernel, [own, sib], [shape((2, windows, c, TD), bf16) for c in counts[1:]])
+            totals = [sum(counts[chunk] for chunk in group) for group in across_groups]
+            made = call(merge_kernel, [*own, *sib], [shape((2, windows, total, TD), bf16) for total in totals])
             panels.update(enumerate(made, 1))
             let = []
-        elif kind == "product":
+        elif kind in ("send", "keep"):
             half = counts[q] * NLAG // 2
-            args = taken if q == 0 else [panels[q], arrived[q]]
-            keep, send, *let = call(
-                summed_kernel if q else taken_kernel, [*args, *spectra],
-                [shape((half, rows), f32), shape((half, rows), bf16)],
-                [pltpu.VMEM((2 * half, 2 * windows * TD), bf16)],
+            args, kernel = taken, taken_kernel
+            for g, group in enumerate(across_groups, 1):
+                if q in group:
+                    place = sum(counts[chunk] for chunk in group if chunk < q)
+                    args, kernel = [panels[g], arrived[g]], functools.partial(summed_kernel, place)
+            made, *let = call(
+                functools.partial(kernel, half if kind == "send" else 0), [*args, *spectra],
+                [shape((half, rows), bf16 if kind == "send" else f32)],
             )
-            moved["first", q] = swap(send, "tm", orders[q][0])
-            state["first", q] = keep, moved["first", q]
-            pieces["first", q] = [half]
+            if kind == "send":
+                moved["first", q] = swap(made, "tm", orders[q][0])
+                pieces["first", q] = [half]
+            else:
+                state["first", q] = made, moved["first", q]
         elif kind == "sum":
             keep, recv = state["third", q]
             total, *let = call(total_kernel, [keep, recv], [shape(keep.shape, f32)])
@@ -422,12 +470,17 @@
 
     starts = [sum(sizes[:q]) * NLAG for q in range(len(sizes))]
     args, places = [], []
-    for q, group in enumerate(thirds):
+    for q, group in sorted(enumerate(thirds), key=lambda item: state[final, item[0]][1] is not None):
         args += [x for x in state[final, q] if x is not None]
         chunks = [chunk for member in group for chunk in seconds[member]]
         places.append((state[final, q][1] is None, [(starts[chunk], sizes[chunk] * NLAG) for chunk in chunks]))
     (stacked,) = chain(
-        "last", functools.partial(last_kernel, places), args, [shape((per_dest * NLAG, rows), f32)]
+        "last",
+        functools.partial(last_kernel, places),
+        args,
+        [shape((per_dest * NLAG, rows), f32)],
+        [pltpu.VMEM((per_dest * NLAG, rows), f32), pltpu.SemaphoreType.DMA((len(sizes),))],
+        result=ANY,
     )
     return stacked.reshape(per_dest, NLAG, rows)
 

time: 69.4 us -> 65.6 us (0.945)
  starting transfers between devices: 31.5 us -> 28.8 us
  waiting for transfers between devices: 18.7 us -> 17.8 us
    ppermute x21, starting transfers between devices: 29 us -> 26.3 us  [swap(): lax.ppermute(value, axis, [(i, i ^ bit) for i in range(lax.axis_size(axis...]
    ppermute x21, waiting for transfers between devices: 18.7 us -> 17.8 us  [swap(): lax.ppermute(value, axis, [(i, i ^ bit) for i in range(lax.axis_size(axis...]
    pallas_call x23 -> x27, Pallas kernels: 17.9 us -> 17.6 us  [__call__(): pl.pallas_call(body, out_shape=[*outs, *(jax.ShapeDtypeStruct(g.shape, g....]
  transfers between devices with their start and end apart: 22 -> 22, of which waited for: 10 -> 7; matrix products, arithmetic and copies ran while one was open for 0% -> 0% of each run, Pallas kernels for 21% -> 20%
where the time goes in v3:
time: 65.6 us; the launch traced here: 65.4 us
  starting transfers between devices  28.8 us (44%)
  waiting for transfers between devices  17.8 us (27%)
  Pallas kernels  17.6 us (27%)
  local copies, waits for them, and re-layouts  0.87 us (1%)
    ppermute x21, starting transfers between devices, swap(): lax.ppermute(value, axis, [(i, i ^ bit) for i in range(lax.axis_size(axis...  26.3 us
    ppermute x21, waiting for transfers between devices, swap(): lax.ppermute(value, axis, [(i, i ^ bit) for i in range(lax.axis_size(axis...  17.8 us
    pallas_call x27, Pallas kernels, __call__(): pl.pallas_call(body, out_shape=[*outs, *(jax.ShapeDtypeStruct(g.shape, g....  17.6 us
    ppermute x1, starting transfers between devices, local(): lax.ppermute(tail, 'tm', [(i, i + 1) for i in range(time_parts - 1)])  2.51 us
  transfers between devices with their start and end apart: 22, of which 7 were waited for; matrix products, arithmetic and copies ran while one was open for 0% of the time, Pallas kernels for 20%

profile of v3, /device:TPU:0, one launch (start us, length us, event | category | flops | bytes accessed | tf_op | source)
XLA Modules:
  0.0 65.4 jit_solution(13651500946940158075)
XLA Ops:
  0.0 1.1 %history.1.refs_6_ = bf16[640,128]{1,0:T(8,128)(2,1)S(1)} custom-call(bf16[640,4096]{1,0:T(8,128)(2,1)} %refs_0_.6), custom_call_target="tpu_custom_call" | custom-call | flops 50000000 | bytes 10000 | tf_op jit(solution)/shard_map/history/pallas_call | solution.py:334
  1.1 2.5 %collective-permute-start = (bf16[640,128]{1,0:T(8,128)(2,1)S(1)}, bf16[640,128]{1,0:T(8,128)(2,1)S(1)}, u32[]{:S(2)}, u32[]{:S(2)}) collective-permute-start(bf16[640,128]{1,0:T(8,128)(2,1)S(1)} %history.1.refs_6_), channel_id=1, source_target_pairs={{0,2},{2,4},{4,6},{6,8},{8,10},{10,12},{12,14},{14,16},{16,18},{18... | collective-permute-start | bytes 491528 | tf_op jit(solution)/shard_map/ppermute | solution.py:379
  4.5 3.0 %late.1 = (bf16[3,640,256]{2,1,0:T(8,128)(2,1)S(1)}, bf16[256,1152]{1,0:T(8,128)(2,1)S(1)}, f32[640,128]{1,0:T(8,128)S(1)}, bf16[512,640]{1,0:T(8,128)(2,1)S(1)}) custom-call(bf16[640,4096]{1,0:T(8,128)(2,1)S(1)} %copy-done, bf16[1,128]{1,0:T(2,128)(2,1)S(1)} %bitcast.4, s32[1,640]{1,0:T(1,128)S(1)} %reshape.13.refs_2_, s32[1,512]{1,0:T(1,128)S(1)} %bitcast.3, ...), custom_call_target="tpu_custom_call" | custom-call | flops 50000000 | bytes 10000 | tf_op jit(solution)/shard_map/late/pallas_call | solution.py:334
  7.6 1.9 %first.1 = (bf16[4,160,256]{2,1,0:T(8,128)(2,1)S(1)}, bf16[4,640,256]{2,1,0:T(8,128)(2,1)S(1)}) custom-call(bf16[640,4096]{1,0:T(8,128)(2,1)S(1)} %copy-done, bf16[640,128]{1,0:T(8,128)(2,1)S(1)} %collective-permute-done.refs_1_, bf16[256,1152]{1,0:T(8,128)(2,1)S(1)} %get-tuple-element.40.refs_2_, bf16[256,256]{1,0:T(8,128)(2,1)S(1)} %copy-done.1, ...), custom_call_target="tpu_custom_call" | custom-call | flops 500000000 | bytes 10000 | tf_op jit(solution)/shard_map/first/pallas_call | solution.py:334
  10.2 2.7 %collective-permute-start.6 = (bf16[4,640,256]{2,1,0:T(8,128)(2,1)S(1)}, bf16[4,640,256]{2,1,0:T(8,128)(2,1)S(1)}, u32[]{:S(2)}, u32[]{:S(2)}) collective-permute-start(bf16[4,640,256]{2,1,0:T(8,128)(2,1)S(1)} %get-tuple-element.56.refs_2_), channel_id=1, source_target_pairs={{0,2},{2,0},{4,6},{6,4},{8,10},{10,8},{12,14},{14,12},{16,18},{18,... | collective-permute-start | bytes 3932168 | tf_op jit(solution)/shard_map/ppermute | solution.py:90
  12.9 1.5 %collective-permute-start.1 = (bf16[4,160,256]{2,1,0:T(8,128)(2,1)S(1)}, bf16[4,160,256]{2,1,0:T(8,128)(2,1)S(1)}, u32[]{:S(2)}, u32[]{:S(2)}) collective-permute-start(bf16[4,160,256]{2,1,0:T(8,128)(2,1)S(1)} %get-tuple-element.44.refs_2_.refs_0_), channel_id=1, source_target_pairs={{0,1},{1,0},{2,3},{3,2},{4,5},{5,4},{6,7},{7,6},{8,9},{9,8},{10,11... | collective-permute-start | bytes 983048 | tf_op jit(solution)/shard_map/ppermute | solution.py:90
  14.9 1.3 %collective-permute-done.4.refs_5_ = bf16[4,48,256]{2,1,0:T(8,128)(2,1)S(1)} collective-permute-done((bf16[4,48,256]{2,1,0:T(8,128)(2,1)S(1)}, bf16[4,48,256]{2,1,0:T(8,128)(2,1)S(1)}, u32[]{:S(2)}, u32[]{:S(2)}) %collective-permute-start.4) | collective-permute-done | bytes 98336 | tf_op jit(solution)/shard_map/ppermute | solution.py:90
  16.3 1.4 %collective-permute-start.9 = (bf16[2,4,64,256]{3,2,1,0:T(8,128)(2,1)S(1)}, bf16[2,4,64,256]{3,2,1,0:T(8,128)(2,1)S(1)}, u32[]{:S(2)}, u32[]{:S(2)}) collective-permute-start(bf16[2,4,64,256]{3,2,1,0:T(8,128)(2,1)S(1)} %get-tuple-element.53.refs_2_.refs_0_), channel_id=1, source_target_pairs={{0,1},{1,0},{2,3},{3,2},{4,5},{5,4},{6,7},{7,6},{8,9},{9,8},{10,11... | collective-permute-start | bytes 786440 | tf_op jit(solution)/shard_map/ppermute | solution.py:90
  17.7 5.7 %collective-permute-done.1.refs_1_ = bf16[4,160,256]{2,1,0:T(8,128)(2,1)S(1)} collective-permute-done((bf16[4,160,256]{2,1,0:T(8,128)(2,1)S(1)}, bf16[4,160,256]{2,1,0:T(8,128)(2,1)S(1)}, u32[]{:S(2)}, u32[]{:S(2)}) %collective-permute-start.1) | collective-permute-done | bytes 327712 | tf_op jit(solution)/shard_map/ppermute | solution.py:90
  23.6 1.6 %collective-permute-start.8 = (bf16[2,4,64,256]{3,2,1,0:T(8,128)(2,1)S(1)}, bf16[2,4,64,256]{3,2,1,0:T(8,128)(2,1)S(1)}, u32[]{:S(2)}, u32[]{:S(2)}) collective-permute-start(bf16[2,4,64,256]{3,2,1,0:T(8,128)(2,1)S(1)} %get-tuple-element.57.refs_0_), channel_id=1, source_target_pairs={{0,1},{1,0},{2,3},{3,2},{4,5},{5,4},{6,7},{7,6},{8,9},{9,8},{10,11... | collective-permute-start | bytes 786440 | tf_op jit(solution)/shard_map/ppermute | solution.py:90
  25.2 1.4 %send_0.1.refs_6_ = bf16[320,640]{1,0:T(8,128)(2,1)S(1)} custom-call(bf16[4,80,256]{2,1,0:T(8,128)(2,1)S(1)} %get-tuple-element.54.refs_0_.refs_6_, bf16[4,80,256]{2,1,0:T(8,128)(2,1)S(1)} %collective-permute-done.5.refs_1_, bf16[4,640,256]{2,1,0:T(8,128)(2,1)S(1)} %get-tuple-element.56.refs_2_, bf16[4,640,256]{2,1,0:T(8,128)(2,1)S(1)} %collective-permute-done.6.refs_3_, ...), custom_call_target="tpu_custom_call" | custom-call | flops 297000000 | bytes 10000 | tf_op jit(solution)/shard_map/send_0/pallas_call | solution.py:334
  26.6 1.7 %collective-permute-start.7 = (bf16[320,640]{1,0:T(8,128)(2,1)S(1)}, bf16[320,640]{1,0:T(8,128)(2,1)S(1)}, u32[]{:S(2)}, u32[]{:S(2)}) collective-permute-start(bf16[320,640]{1,0:T(8,128)(2,1)S(1)} %send_0.1.refs_6_), channel_id=1, source_target_pairs={{0,8},{2,10},{4,12},{6,14},{8,0},{10,2},{12,4},{14,6},{16,24},{18,... | collective-permute-start | bytes 1228808 | tf_op jit(solution)/shard_map/ppermute | solution.py:90
  28.3 1.4 %keep_0.1.refs_7_.refs_0_ = f32[320,640]{1,0:T(8,128)S(1)} custom-call(bf16[4,80,256]{2,1,0:T(8,128)(2,1)S(1)} %get-tuple-element.54.refs_0_.refs_6_, bf16[4,80,256]{2,1,0:T(8,128)(2,1)S(1)} %collective-permute-done.5.refs_1_, bf16[4,640,256]{2,1,0:T(8,128)(2,1)S(1)} %get-tuple-element.56.refs_2_, bf16[4,640,256]{2,1,0:T(8,128)(2,1)S(1)} %collective-permute-done.6.refs_3_, ...), custom_call_target="tpu_custom_call" | custom-call | flops 182000000 | bytes 10000 | tf_op jit(solution)/shard_map/keep_0/pallas_call | solution.py:334
  29.7 1.2 %send_1.1.refs_6_ = bf16[256,640]{1,0:T(8,128)(2,1)S(1)} custom-call(bf16[2,4,64,256]{3,2,1,0:T(8,128)(2,1)S(1)} %get-tuple-element.53.refs_2_.refs_0_, bf16[2,4,64,256]{3,2,1,0:T(8,128)(2,1)S(1)} %collective-permute-done.9.refs_1_.refs_6_, bf16[4,640,256]{2,1,0:T(8,128)(2,1)S(1)} %get-tuple-element.56.refs_2_, ...), custom_call_target="tpu_custom_call" | custom-call | flops 15000000512 | bytes 10000 | tf_op jit(solution)/shard_map/send_1/pallas_call | solution.py:334
  30.9 1.5 %collective-permute-start.12 = (bf16[256,640]{1,0:T(8,128)(2,1)S(1)}, bf16[256,640]{1,0:T(8,128)(2,1)S(1)}, u32[]{:S(2)}, u32[]{:S(2)}) collective-permute-start(bf16[256,640]{1,0:T(8,128)(2,1)S(1)} %send_1.1.refs_6_), channel_id=1, source_target_pairs={{0,4},{2,6},{4,0},{6,2},{8,12},{10,14},{12,8},{14,10},{16,20},{18,... | collective-permute-start | bytes 983048 | tf_op jit(solution)/shard_map/ppermute | solution.py:90
  32.4 1.3 %collective-permute-start.11 = (bf16[2,4,48,256]{3,2,1,0:T(8,128)(2,1)S(1)}, bf16[2,4,48,256]{3,2,1,0:T(8,128)(2,1)S(1)}, u32[]{:S(2)}, u32[]{:S(2)}) collective-permute-start(bf16[2,4,48,256]{3,2,1,0:T(8,128)(2,1)S(1)} %get-tuple-element.60.refs_0_), channel_id=1, source_target_pairs={{0,1},{1,0},{2,3},{3,2},{4,5},{5,4},{6,7},{7,6},{8,9},{9,8},{10,11... | collective-permute-start | bytes 589832 | tf_op jit(solution)/shard_map/ppermute | solution.py:90
  33.7 1.2 %keep_1.1.refs_7_.refs_0_ = f32[256,640]{1,0:T(8,128)S(1)} custom-call(bf16[2,4,64,256]{3,2,1,0:T(8,128)(2,1)S(1)} %get-tuple-element.53.refs_2_.refs_0_, bf16[2,4,64,256]{3,2,1,0:T(8,128)(2,1)S(1)} %collective-permute-done.9.refs_1_.refs_6_, bf16[4,640,256]{2,1,0:T(8,128)(2,1)S(1)} %get-tuple-element.56.refs_2_, ...), custom_call_target="tpu_custom_call" | custom-call | flops 347000000 | bytes 10000 | tf_op jit(solution)/shard_map/keep_1/pallas_call | solution.py:334
  34.9 1.2 %send_2.1.refs_6_ = bf16[256,640]{1,0:T(8,128)(2,1)S(1)} custom-call(bf16[2,4,64,256]{3,2,1,0:T(8,128)(2,1)S(1)} %get-tuple-element.57.refs_0_, bf16[2,4,64,256]{3,2,1,0:T(8,128)(2,1)S(1)} %collective-permute-done.8.refs_1_.refs_6_, bf16[4,640,256]{2,1,0:T(8,128)(2,1)S(1)} %get-tuple-element.56.refs_2_, ...), custom_call_target="tpu_custom_call" | custom-call | flops 277000000 | bytes 10000 | tf_op jit(solution)/shard_map/send_2/pallas_call | solution.py:334
  36.1 1.5 %collective-permute-start.16 = (bf16[256,640]{1,0:T(8,128)(2,1)S(1)}, bf16[256,640]{1,0:T(8,128)(2,1)S(1)}, u32[]{:S(2)}, u32[]{:S(2)}) collective-permute-start(bf16[256,640]{1,0:T(8,128)(2,1)S(1)} %send_2.1.refs_6_), channel_id=1, source_target_pairs={{0,8},{2,10},{4,12},{6,14},{8,0},{10,2},{12,4},{14,6},{16,24},{18,... | collective-permute-start | bytes 983048 | tf_op jit(solution)/shard_map/ppermute | solution.py:90
  37.6 1.2 %keep_2.1.refs_3_.refs_0_ = f32[256,640]{1,0:T(8,128)S(1)} custom-call(bf16[2,4,64,256]{3,2,1,0:T(8,128)(2,1)S(1)} %get-tuple-element.57.refs_0_, bf16[2,4,64,256]{3,2,1,0:T(8,128)(2,1)S(1)} %collective-permute-done.8.refs_1_.refs_6_, bf16[4,640,256]{2,1,0:T(8,128)(2,1)S(1)} %get-tuple-element.56.refs_2_, ...), custom_call_target="tpu_custom_call" | custom-call | flops 112000000 | bytes 10000 | tf_op jit(solution)/shard_map/keep_2/pallas_call | solution.py:334
  38.9 1.8 %collective-permute-start.10 = (bf16[160,640]{1,0:T(8,128)(2,1)S(1)}, bf16[160,640]{1,0:T(8,128)(2,1)S(1)}, u32[]{:S(2)}, u32[]{:S(2)}) collective-permute-start(bf16[160,640]{1,0:T(8,128)(2,1)S(1)} %get-tuple-element.59), channel_id=1, source_target_pairs={{0,4},{2,6},{4,0},{6,2},{8,12},{10,14},{12,8},{14,10},{16,20},{18,... | collective-permute-start | bytes 614408 | tf_op jit(solution)/shard_map/ppermute | solution.py:90
  41.7 1.3 %collective-permute-start.14 = (bf16[192,640]{1,0:T(8,128)(2,1)S(1)}, bf16[192,640]{1,0:T(8,128)(2,1)S(1)}, u32[]{:S(2)}, u32[]{:S(2)}) collective-permute-start(bf16[192,640]{1,0:T(8,128)(2,1)S(1)} %send_3.1.refs_2_), channel_id=1, source_target_pairs={{0,4},{2,6},{4,0},{6,2},{8,12},{10,14},{12,8},{14,10},{16,20},{18,... | collective-permute-start | bytes 737288 | tf_op jit(solution)/shard_map/ppermute | solution.py:90
  43.7 1.0 %keep_3.1.refs_2_.refs_0_ = f32[192,640]{1,0:T(8,128)S(1)} custom-call(bf16[2,4,48,256]{3,2,1,0:T(8,128)(2,1)S(1)} %get-tuple-element.60.refs_0_, bf16[2,4,48,256]{3,2,1,0:T(8,128)(2,1)S(1)} %collective-permute-done.11.refs_1_.refs_6_, bf16[4,640,256]{2,1,0:T(8,128)(2,1)S(1)} %get-tuple-element.56.refs_2_, ...), custom_call_target="tpu_custom_call" | custom-call | flops 110000000 | bytes 10000 | tf_op jit(solution)/shard_map/keep_3/pallas_call | solution.py:334
  44.7 1.9 %collective-permute-done.10.refs_1_.refs_3_ = bf16[160,640]{1,0:T(8,128)(2,1)S(1)} collective-permute-done((bf16[160,640]{1,0:T(8,128)(2,1)S(1)}, bf16[160,640]{1,0:T(8,128)(2,1)S(1)}, u32[]{:S(2)}, u32[]{:S(2)}) %collective-permute-start.10) | collective-permute-done | bytes 204832 | tf_op jit(solution)/shard_map/ppermute | solution.py:90
  46.6 2.7 %collective-permute-start.13 = (bf16[80,640]{1,0:T(8,128)(2,1)S(1)}, bf16[80,640]{1,0:T(8,128)(2,1)S(1)}, u32[]{:S(2)}, u32[]{:S(2)}) collective-permute-start(bf16[80,640]{1,0:T(8,128)(2,1)S(1)} %get-tuple-element.63), channel_id=1, source_target_pairs={{0,16},{2,18},{4,20},{6,22},{8,24},{10,26},{12,28},{14,30},{16,0},... | collective-permute-start | bytes 307208 | tf_op jit(solution)/shard_map/ppermute | solution.py:90
  49.4 2.1 %collective-permute-start.18 = (bf16[128,640]{1,0:T(8,128)(2,1)S(1)}, bf16[128,640]{1,0:T(8,128)(2,1)S(1)}, u32[]{:S(2)}, u32[]{:S(2)}) collective-permute-start(bf16[128,640]{1,0:T(8,128)(2,1)S(1)} %get-tuple-element.69), channel_id=1, source_target_pairs={{0,4},{2,6},{4,0},{6,2},{8,12},{10,14},{12,8},{14,10},{16,20},{18,... | collective-permute-start | bytes 491528 | tf_op jit(solution)/shard_map/ppermute | solution.py:90
  51.5 1.1 %collective-permute-start.17 = (bf16[64,640]{1,0:T(8,128)(2,1)S(1)}, bf16[64,640]{1,0:T(8,128)(2,1)S(1)}, u32[]{:S(2)}, u32[]{:S(2)}) collective-permute-start(bf16[64,640]{1,0:T(8,128)(2,1)S(1)} %get-tuple-element.68), channel_id=1, source_target_pairs={{0,16},{2,18},{4,20},{6,22},{8,24},{10,26},{12,28},{14,30},{16,0},... | collective-permute-start | bytes 245768 | tf_op jit(solution)/shard_map/ppermute | solution.py:90
  52.6 1.6 %collective-permute-start.20 = (bf16[96,640]{1,0:T(8,128)(2,1)S(1)}, bf16[96,640]{1,0:T(8,128)(2,1)S(1)}, u32[]{:S(2)}, u32[]{:S(2)}) collective-permute-start(bf16[96,640]{1,0:T(8,128)(2,1)S(1)} %get-tuple-element.72), channel_id=1, source_target_pairs={{0,8},{2,10},{4,12},{6,14},{8,0},{10,2},{12,4},{14,6},{16,24},{18,... | collective-permute-start | bytes 368648 | tf_op jit(solution)/shard_map/ppermute | solution.py:90
  55.3 1.0 %collective-permute-start.19 = (bf16[64,640]{1,0:T(8,128)(2,1)S(1)}, bf16[64,640]{1,0:T(8,128)(2,1)S(1)}, u32[]{:S(2)}, u32[]{:S(2)}) collective-permute-start(bf16[64,640]{1,0:T(8,128)(2,1)S(1)} %get-tuple-element.71), channel_id=1, source_target_pairs={{0,16},{2,18},{4,20},{6,22},{8,24},{10,26},{12,28},{14,30},{16,0},... | collective-permute-start | bytes 245768 | tf_op jit(solution)/shard_map/ppermute | solution.py:90
  56.3 3.0 %collective-permute-done.17.refs_1_.refs_2_ = bf16[64,640]{1,0:T(8,128)(2,1)S(1)} collective-permute-done((bf16[64,640]{1,0:T(8,128)(2,1)S(1)}, bf16[64,640]{1,0:T(8,128)(2,1)S(1)}, u32[]{:S(2)}, u32[]{:S(2)}) %collective-permute-start.17) | collective-permute-done | bytes 81952 | tf_op jit(solution)/shard_map/ppermute | solution.py:90
  59.6 1.2 %collective-permute-done.19.refs_1_.refs_2_ = bf16[64,640]{1,0:T(8,128)(2,1)S(1)} collective-permute-done((bf16[64,640]{1,0:T(8,128)(2,1)S(1)}, bf16[64,640]{1,0:T(8,128)(2,1)S(1)}, u32[]{:S(2)}, u32[]{:S(2)}) %collective-permute-start.19) | collective-permute-done | bytes 81952 | tf_op jit(solution)/shard_map/ppermute | solution.py:90
  60.9 3.7 %collective-permute-done.21.refs_4_ = bf16[48,640]{1,0:T(8,128)(2,1)S(1)} collective-permute-done((bf16[48,640]{1,0:T(8,128)(2,1)S(1)}, bf16[48,640]{1,0:T(8,128)(2,1)S(1)}, u32[]{:S(2)}, u32[]{:S(2)}) %collective-permute-start.21) | collective-permute-done | bytes 61472 | tf_op jit(solution)/shard_map/ppermute | solution.py:90
  (56 shorter events, 6.4 us)
Async XLA Ops:
  0.0 3.6 %copy-start.1 = (bf16[256,256]{1,0:T(8,128)(2,1)S(1)}, bf16[256,256]{1,0:T(8,128)(2,1)}, u32[]{:S(2)}) copy-start(bf16[256,256]{1,0:T(8,128)(2,1)} %constant.8.clone.refs_4_.refs_3_.refs_0_) | copy-start | bytes 393220
  0.0 3.6 %copy-start.7 = (s32[640]{0:T(1024)S(1)}, s32[640]{0:T(1024)}, u32[]{:S(2)}) copy-start(s32[640]{0:T(1024)} %param.11) | copy-start | bytes 7684
  0.0 3.6 %copy-start.6 = (bf16[128]{0:T(256)(128)(2,1)S(1)}, bf16[128]{0:T(256)(128)(2,1)}, u32[]{:S(2)}) copy-start(bf16[128]{0:T(256)(128)(2,1)} %param.9) | copy-start | bytes 772
  0.0 3.7 %copy-start = (bf16[640,4096]{1,0:T(8,128)(2,1)S(1)}, bf16[640,4096]{1,0:T(8,128)(2,1)}, u32[]{:S(2)}) copy-start(bf16[640,4096]{1,0:T(8,128)(2,1)} %refs_0_.6) | copy-start | bytes 15728644
  0.0 3.7 %copy-start.5 = (s32[512]{0:T(512)S(1)}, s32[512]{0:T(512)}, u32[]{:S(2)}) copy-start(s32[512]{0:T(512)} %param.10) | copy-start | bytes 6148
  1.1 6.5 %collective-permute-start = (bf16[640,128]{1,0:T(8,128)(2,1)S(1)}, bf16[640,128]{1,0:T(8,128)(2,1)S(1)}, u32[]{:S(2)}, u32[]{:S(2)}) collective-permute-start(bf16[640,128]{1,0:T(8,128)(2,1)S(1)} %history.1.refs_6_), channel_id=1, source_target_pairs={{0,2},{2,4},{4,6},{6,8},{8,10},{10,12},{12,14},{14,16},{16,18},{18... | collective-permute-start | bytes 491528 | tf_op jit(solution)/shard_map/ppermute | solution.py:379
  3.7 0.8 %copy-start.2 = (bf16[256,128]{1,0:T(8,128)(2,1)S(1)}, bf16[256,128]{1,0:T(8,128)(2,1)}, u32[]{:S(2)}) copy-start(bf16[256,128]{1,0:T(8,128)(2,1)} %constant.9.clone.refs_5_.refs_4_) | copy-start | bytes 196612
  10.2 14.9 %collective-permute-start.6 = (bf16[4,640,256]{2,1,0:T(8,128)(2,1)S(1)}, bf16[4,640,256]{2,1,0:T(8,128)(2,1)S(1)}, u32[]{:S(2)}, u32[]{:S(2)}) collective-permute-start(bf16[4,640,256]{2,1,0:T(8,128)(2,1)S(1)} %get-tuple-element.56.refs_2_), channel_id=1, source_target_pairs={{0,2},{2,0},{4,6},{6,4},{8,10},{10,8},{12,14},{14,12},{16,18},{18,... | collective-permute-start | bytes 3932168 | tf_op jit(solution)/shard_map/ppermute | solution.py:90
  12.9 10.6 %collective-permute-start.1 = (bf16[4,160,256]{2,1,0:T(8,128)(2,1)S(1)}, bf16[4,160,256]{2,1,0:T(8,128)(2,1)S(1)}, u32[]{:S(2)}, u32[]{:S(2)}) collective-permute-start(bf16[4,160,256]{2,1,0:T(8,128)(2,1)S(1)} %get-tuple-element.44.refs_2_.refs_0_), channel_id=1, source_target_pairs={{0,1},{1,0},{2,3},{3,2},{4,5},{5,4},{6,7},{7,6},{8,9},{9,8},{10,11... | collective-permute-start | bytes 983048 | tf_op jit(solution)/shard_map/ppermute | solution.py:90
  14.4 1.8 %collective-permute-start.2 = (bf16[4,64,256]{2,1,0:T(8,128)(2,1)S(1)}, bf16[4,64,256]{2,1,0:T(8,128)(2,1)S(1)}, u32[]{:S(2)}, u32[]{:S(2)}) collective-permute-start(bf16[4,64,256]{2,1,0:T(8,128)(2,1)S(1)} %get-tuple-element.49), channel_id=1, source_target_pairs={{0,2},{2,0},{4,6},{6,4},{8,10},{10,8},{12,14},{14,12},{16,18},{18,... | collective-permute-start | bytes 393224 | tf_op jit(solution)/shard_map/ppermute | solution.py:90
  14.4 1.8 %collective-permute-start.3 = (bf16[4,64,256]{2,1,0:T(8,128)(2,1)S(1)}, bf16[4,64,256]{2,1,0:T(8,128)(2,1)S(1)}, u32[]{:S(2)}, u32[]{:S(2)}) collective-permute-start(bf16[4,64,256]{2,1,0:T(8,128)(2,1)S(1)} %get-tuple-element.50), channel_id=1, source_target_pairs={{0,2},{2,0},{4,6},{6,4},{8,10},{10,8},{12,14},{14,12},{16,18},{18,... | collective-permute-start | bytes 393224 | tf_op jit(solution)/shard_map/ppermute | solution.py:90
  14.9 1.3 %collective-permute-start.4 = (bf16[4,48,256]{2,1,0:T(8,128)(2,1)S(1)}, bf16[4,48,256]{2,1,0:T(8,128)(2,1)S(1)}, u32[]{:S(2)}, u32[]{:S(2)}) collective-permute-start(bf16[4,48,256]{2,1,0:T(8,128)(2,1)S(1)} %get-tuple-element.51), channel_id=1, source_target_pairs={{0,2},{2,0},{4,6},{6,4},{8,10},{10,8},{12,14},{14,12},{16,18},{18,... | collective-permute-start | bytes 294920 | tf_op jit(solution)/shard_map/ppermute | solution.py:90
  16.2 8.9 %copy-start.3 = (f32[8,128]{1,0:T(8,128)S(1)}, f32[8,128]{1,0:T(8,128)}, u32[]{:S(2)}) copy-start(f32[8,128]{1,0:T(8,128)} %constant.10.clone.refs_4_) | copy-start | bytes 12292
  16.2 8.9 %copy-start.4 = (f32[8,128]{1,0:T(8,128)S(1)}, f32[8,128]{1,0:T(8,128)}, u32[]{:S(2)}) copy-start(f32[8,128]{1,0:T(8,128)} %constant.11.clone.refs_5_) | copy-start | bytes 12292
  16.3 13.4 %collective-permute-start.9 = (bf16[2,4,64,256]{3,2,1,0:T(8,128)(2,1)S(1)}, bf16[2,4,64,256]{3,2,1,0:T(8,128)(2,1)S(1)}, u32[]{:S(2)}, u32[]{:S(2)}) collective-permute-start(bf16[2,4,64,256]{3,2,1,0:T(8,128)(2,1)S(1)} %get-tuple-element.53.refs_2_.refs_0_), channel_id=1, source_target_pairs={{0,1},{1,0},{2,3},{3,2},{4,5},{5,4},{6,7},{7,6},{8,9},{9,8},{10,11... | collective-permute-start | bytes 786440 | tf_op jit(solution)/shard_map/ppermute | solution.py:90
  23.5 1.7 %collective-permute-start.5 = (bf16[4,80,256]{2,1,0:T(8,128)(2,1)S(1)}, bf16[4,80,256]{2,1,0:T(8,128)(2,1)S(1)}, u32[]{:S(2)}, u32[]{:S(2)}) collective-permute-start(bf16[4,80,256]{2,1,0:T(8,128)(2,1)S(1)} %get-tuple-element.55), channel_id=1, source_target_pairs={{0,2},{2,0},{4,6},{6,4},{8,10},{10,8},{12,14},{14,12},{16,18},{18,... | collective-permute-start | bytes 491528 | tf_op jit(solution)/shard_map/ppermute | solution.py:90
  23.6 11.3 %collective-permute-start.8 = (bf16[2,4,64,256]{3,2,1,0:T(8,128)(2,1)S(1)}, bf16[2,4,64,256]{3,2,1,0:T(8,128)(2,1)S(1)}, u32[]{:S(2)}, u32[]{:S(2)}) collective-permute-start(bf16[2,4,64,256]{3,2,1,0:T(8,128)(2,1)S(1)} %get-tuple-element.57.refs_0_), channel_id=1, source_target_pairs={{0,1},{1,0},{2,3},{3,2},{4,5},{5,4},{6,7},{7,6},{8,9},{9,8},{10,11... | collective-permute-start | bytes 786440 | tf_op jit(solution)/shard_map/ppermute | solution.py:90
  26.6 12.2 %collective-permute-start.7 = (bf16[320,640]{1,0:T(8,128)(2,1)S(1)}, bf16[320,640]{1,0:T(8,128)(2,1)S(1)}, u32[]{:S(2)}, u32[]{:S(2)}) collective-permute-start(bf16[320,640]{1,0:T(8,128)(2,1)S(1)} %send_0.1.refs_6_), channel_id=1, source_target_pairs={{0,8},{2,10},{4,12},{6,14},{8,0},{10,2},{12,4},{14,6},{16,24},{18,... | collective-permute-start | bytes 1228808 | tf_op jit(solution)/shard_map/ppermute | solution.py:90
  30.9 9.8 %collective-permute-start.12 = (bf16[256,640]{1,0:T(8,128)(2,1)S(1)}, bf16[256,640]{1,0:T(8,128)(2,1)S(1)}, u32[]{:S(2)}, u32[]{:S(2)}) collective-permute-start(bf16[256,640]{1,0:T(8,128)(2,1)S(1)} %send_1.1.refs_6_), channel_id=1, source_target_pairs={{0,4},{2,6},{4,0},{6,2},{8,12},{10,14},{12,8},{14,10},{16,20},{18,... | collective-permute-start | bytes 983048 | tf_op jit(solution)/shard_map/ppermute | solution.py:90
  32.4 8.3 %collective-permute-start.11 = (bf16[2,4,48,256]{3,2,1,0:T(8,128)(2,1)S(1)}, bf16[2,4,48,256]{3,2,1,0:T(8,128)(2,1)S(1)}, u32[]{:S(2)}, u32[]{:S(2)}) collective-permute-start(bf16[2,4,48,256]{3,2,1,0:T(8,128)(2,1)S(1)} %get-tuple-element.60.refs_0_), channel_id=1, source_target_pairs={{0,1},{1,0},{2,3},{3,2},{4,5},{5,4},{6,7},{7,6},{8,9},{9,8},{10,11... | collective-permute-start | bytes 589832 | tf_op jit(solution)/shard_map/ppermute | solution.py:90
  36.1 13.2 %collective-permute-start.16 = (bf16[256,640]{1,0:T(8,128)(2,1)S(1)}, bf16[256,640]{1,0:T(8,128)(2,1)S(1)}, u32[]{:S(2)}, u32[]{:S(2)}) collective-permute-start(bf16[256,640]{1,0:T(8,128)(2,1)S(1)} %send_2.1.refs_6_), channel_id=1, source_target_pairs={{0,8},{2,10},{4,12},{6,14},{8,0},{10,2},{12,4},{14,6},{16,24},{18,... | collective-permute-start | bytes 983048 | tf_op jit(solution)/shard_map/ppermute | solution.py:90
  38.9 7.7 %collective-permute-start.10 = (bf16[160,640]{1,0:T(8,128)(2,1)S(1)}, bf16[160,640]{1,0:T(8,128)(2,1)S(1)}, u32[]{:S(2)}, u32[]{:S(2)}) collective-permute-start(bf16[160,640]{1,0:T(8,128)(2,1)S(1)} %get-tuple-element.59), channel_id=1, source_target_pairs={{0,4},{2,6},{4,0},{6,2},{8,12},{10,14},{12,8},{14,10},{16,20},{18,... | collective-permute-start | bytes 614408 | tf_op jit(solution)/shard_map/ppermute | solution.py:90
  41.7 10.9 %collective-permute-start.14 = (bf16[192,640]{1,0:T(8,128)(2,1)S(1)}, bf16[192,640]{1,0:T(8,128)(2,1)S(1)}, u32[]{:S(2)}, u32[]{:S(2)}) collective-permute-start(bf16[192,640]{1,0:T(8,128)(2,1)S(1)} %send_3.1.refs_2_), channel_id=1, source_target_pairs={{0,4},{2,6},{4,0},{6,2},{8,12},{10,14},{12,8},{14,10},{16,20},{18,... | collective-permute-start | bytes 737288 | tf_op jit(solution)/shard_map/ppermute | solution.py:90
  43.1 8.4 %collective-permute-start.15 = (bf16[128,640]{1,0:T(8,128)(2,1)S(1)}, bf16[128,640]{1,0:T(8,128)(2,1)S(1)}, u32[]{:S(2)}, u32[]{:S(2)}) collective-permute-start(bf16[128,640]{1,0:T(8,128)(2,1)S(1)} %get-tuple-element.64), channel_id=1, source_target_pairs={{0,8},{2,10},{4,12},{6,14},{8,0},{10,2},{12,4},{14,6},{16,24},{18,... | collective-permute-start | bytes 491528 | tf_op jit(solution)/shard_map/ppermute | solution.py:90
  46.6 8.6 %collective-permute-start.13 = (bf16[80,640]{1,0:T(8,128)(2,1)S(1)}, bf16[80,640]{1,0:T(8,128)(2,1)S(1)}, u32[]{:S(2)}, u32[]{:S(2)}) collective-permute-start(bf16[80,640]{1,0:T(8,128)(2,1)S(1)} %get-tuple-element.63), channel_id=1, source_target_pairs={{0,16},{2,18},{4,20},{6,22},{8,24},{10,26},{12,28},{14,30},{16,0},... | collective-permute-start | bytes 307208 | tf_op jit(solution)/shard_map/ppermute | solution.py:90
  49.4 5.9 %collective-permute-start.18 = (bf16[128,640]{1,0:T(8,128)(2,1)S(1)}, bf16[128,640]{1,0:T(8,128)(2,1)S(1)}, u32[]{:S(2)}, u32[]{:S(2)}) collective-permute-start(bf16[128,640]{1,0:T(8,128)(2,1)S(1)} %get-tuple-element.69), channel_id=1, source_target_pairs={{0,4},{2,6},{4,0},{6,2},{8,12},{10,14},{12,8},{14,10},{16,20},{18,... | collective-permute-start | bytes 491528 | tf_op jit(solution)/shard_map/ppermute | solution.py:90
  51.5 7.8 %collective-permute-start.17 = (bf16[64,640]{1,0:T(8,128)(2,1)S(1)}, bf16[64,640]{1,0:T(8,128)(2,1)S(1)}, u32[]{:S(2)}, u32[]{:S(2)}) collective-permute-start(bf16[64,640]{1,0:T(8,128)(2,1)S(1)} %get-tuple-element.68), channel_id=1, source_target_pairs={{0,16},{2,18},{4,20},{6,22},{8,24},{10,26},{12,28},{14,30},{16,0},... | collective-permute-start | bytes 245768 | tf_op jit(solution)/shard_map/ppermute | solution.py:90
  52.6 6.7 %collective-permute-start.20 = (bf16[96,640]{1,0:T(8,128)(2,1)S(1)}, bf16[96,640]{1,0:T(8,128)(2,1)S(1)}, u32[]{:S(2)}, u32[]{:S(2)}) collective-permute-start(bf16[96,640]{1,0:T(8,128)(2,1)S(1)} %get-tuple-element.72), channel_id=1, source_target_pairs={{0,8},{2,10},{4,12},{6,14},{8,0},{10,2},{12,4},{14,6},{16,24},{18,... | collective-permute-start | bytes 368648 | tf_op jit(solution)/shard_map/ppermute | solution.py:90
  55.3 5.6 %collective-permute-start.19 = (bf16[64,640]{1,0:T(8,128)(2,1)S(1)}, bf16[64,640]{1,0:T(8,128)(2,1)S(1)}, u32[]{:S(2)}, u32[]{:S(2)}) collective-permute-start(bf16[64,640]{1,0:T(8,128)(2,1)S(1)} %get-tuple-element.71), channel_id=1, source_target_pairs={{0,16},{2,18},{4,20},{6,22},{8,24},{10,26},{12,28},{14,30},{16,0},... | collective-permute-start | bytes 245768 | tf_op jit(solution)/shard_map/ppermute | solution.py:90
  59.4 5.2 %collective-permute-start.21 = (bf16[48,640]{1,0:T(8,128)(2,1)S(1)}, bf16[48,640]{1,0:T(8,128)(2,1)S(1)}, u32[]{:S(2)}, u32[]{:S(2)}) collective-permute-start(bf16[48,640]{1,0:T(8,128)(2,1)S(1)} %get-tuple-element.74), channel_id=1, source_target_pairs={{0,16},{2,18},{4,20},{6,22},{8,24},{10,26},{12,28},{14,30},{16,0},... | collective-permute-start | bytes 184328 | tf_op jit(solution)/shard_map/ppermute | solution.py:90

commit v4 on v3

--- a/solution.py
+++ b/solution.py
@@ -24,33 +24,33 @@
 THIRD = ((2,), (0,), (3,), (1,))
 ACROSS = ((1,), (2,), (3,))
 PLAN = (
-    ('merge', 0, (1, 2, 3), ()),
-    ('split', 0, (), ()),
+    ('merge', 0, (1, 2), ()),
+    ('split', 0, (3,), ()),
     ('send', 0, (), ()),
     ('keep', 0, (), ()),
     ('send', 1, (), (('y', 1),)),
     ('keep', 1, (), ()),
     ('send', 2, (), (('y', 2),)),
+    ('second', 2, (), (('first', 0),)),
     ('keep', 2, (), ()),
-    ('second', 2, (), (('first', 0),)),
     ('send', 3, (), (('y', 3), ('first', 1))),
     ('second', 0, (), ()),
+    ('third', 0, (), ()),
+    ('second', 3, (), (('first', 2),)),
     ('keep', 3, (), ()),
-    ('third', 0, (), ()),
-    ('second', 3, (), (('first', 2), ('second', 2))),
     ('third', 1, (), (('second', 0),)),
-    ('second', 1, (), (('first', 3),)),
+    ('second', 1, (), (('first', 3), ('second', 2))),
     ('sum', 0, (), (('third', 0),)),
     ('third', 2, (), (('second', 3),)),
     ('sum', 1, (), (('third', 1),)),
     ('third', 3, (), (('second', 1),)),
-    ('sum', 2, (), (('third', 2),)),
+    ('sum', 2, (), ()),
 )
 BASE_COST = 0.05
 COSTS = {
     'merge_0': 0.52,
-    'split_0': 0.165,
-    'send_0': 0.297,
+    'split_0': 15,
+    'send_0': 0.5,
     'keep_0': 0.182,
     'send_1': 15,
     'keep_1': 0.347,
@@ -69,7 +69,7 @@
     'sum_1': 1,
     'third_3': 0.373,
     'sum_2': 0.293,
-    'panels': 0.5,
+    'panels': 0.05,
     'gate': 0.05,
     'first': 0.5,
 }
@@ -100,12 +100,6 @@
     phase = (np.arange(NLAG) - NLAG // 2)[:, None] * np.arange(HALF)[None, :] % TD
     angles = 2.0 * math.pi / TD * phase.astype(np.float64)
     return (gain * np.cos(angles)).astype(np.float32), (gain * np.sin(angles)).astype(np.float32)
-
-
-def band_table():
-    bins = np.arange(HALF)
-    band = (np.abs(bins[:, None] - bins[None, :]) <= HW).astype(np.float32)
-    return np.concatenate([band, band], axis=0).astype(jnp.bfloat16)
 
 
 def nt_dot(left, right):
@@ -133,6 +127,12 @@
     alive = 1.0 - dead_ref[...].astype(jnp.float32)
     for i in range(0, alive_ref.shape[0], HALF):
         alive_ref[i : i + HALF, :] = jnp.broadcast_to(alive[:, i : i + HALF], (HALF, HALF)).T
+
+
+def fill_band(band_ref):
+    bins = lax.broadcasted_iota(jnp.int32, band_ref.shape, 0) & (HALF - 1)
+    apart = jnp.abs(bins - lax.broadcasted_iota(jnp.int32, band_ref.shape, 1))
+    band_ref[...] = jnp.where(apart <= HW, 1.0, 0.0).astype(jnp.bfloat16)
 
 
 def fill_selector(sizes, orders, sources_ref, select_ref):
@@ -176,12 +176,13 @@
 
 
 def late_kernel(
-    sizes, orders, raw_ref, taps_ref, dead_ref, sources_ref, table_ref, band_ref,
-    out_ref, fir_ref, alive_ref, select_ref,
+    sizes, orders, raw_ref, taps_ref, dead_ref, sources_ref, table_ref,
+    out_ref, fir_ref, alive_ref, band_ref, select_ref,
 ):
     windows, rows, _ = out_ref.shape
     fill_fir(taps_ref, fir_ref)
     fill_alive(dead_ref, alive_ref)
+    fill_band(band_ref)
     fill_selector(sizes, orders, sources_ref, select_ref)
     samples = jnp.concatenate(
         [raw_ref[:, w * SPAN - TAPS : (w + 1) * SPAN] for w in range(1, windows + 1)], axis=0
@@ -379,15 +380,15 @@
     history = lax.ppermute(tail, "tm", [(i, i + 1) for i in range(time_parts - 1)])
 
     table = jnp.asarray(dft_table())
-    band = jnp.asarray(band_table())
-    late_white, fir, alive, select = chain(
+    late_white, fir, alive, band, select = chain(
         "late",
         functools.partial(late_kernel, sizes, orders),
-        [raw_traces, fir_taps.reshape(1, -1), dead_flags.reshape(1, -1), sources.reshape(1, -1), table, band],
+        [raw_traces, fir_taps.reshape(1, -1), dead_flags.reshape(1, -1), sources.reshape(1, -1), table],
         [
             shape((late, rows, TD), bf16),
             shape((TD, SPAN + TAPS), bf16),
             shape((rows, HALF), f32),
+            shape((TD, HALF), bf16),
             shape((VS, rows), bf16),
         ],
     )
@@ -397,12 +398,12 @@
         [raw_traces, history, fir, table, band, alive, late_white, select],
         [shape((windows, 2 * counts[0], TD), bf16), shape((windows, rows, TD), bf16)],
     )
+    _, white = chain("gate", gate_kernel, [table], [shape((8, HALF), f32)], gates=[white])
+    white_sib = swap(white, "tm", 1)
     members = [[counts[chunk] for chunk in group] for group in across_groups]
     rest = [shape((windows, sum(group), TD), bf16) for group in members]
     parts = chain("panels", functools.partial(panels_kernel, 2 * counts[0], members), [select, white], rest + rest)
     own, sib = parts[: len(rest)], [swap(other, "tm", 1) for other in parts[len(rest) :]]
-    _, white = chain("gate", gate_kernel, [table], [shape((8, HALF), f32)], gates=[white])
-    white_sib = swap(white, "tm", 1)
     tables = [jnp.asarray(t) for t in lag_tables(1.0 / math.sqrt(time_parts * windows * TD))]
     spectra = [white, white_sib, *tables]
 

time: 65.6 us -> 64.4 us (0.982)
  waiting for transfers between devices: 17.8 us -> 13.5 us
  starting transfers between devices: 28.8 us -> 32.4 us
  local copies, waits for them, and re-layouts: 0.87 us -> 0.03 us
    ppermute x21, waiting for transfers between devices: 17.8 us -> 13.5 us  [swap(): lax.ppermute(value, axis, [(i, i ^ bit) for i in range(lax.axis_size(axis...]
    ppermute x21, starting transfers between devices: 26.3 us -> 29.9 us  [swap(): lax.ppermute(value, axis, [(i, i ^ bit) for i in range(lax.axis_size(axis...]
    unnamed x16 -> x14, local copies, waits for them, and re-layouts: 0.86 us -> 0.03 us
  transfers between devices with their start and end apart: 22 -> 22, of which waited for: 7 -> 9; matrix products, arithmetic and copies ran while one was open for 0% -> 0% of each run, Pallas kernels for 20% -> 22%
where the time goes in v4:
time: 64.4 us; the launch traced here: 63.7 us
  starting transfers between devices  32.4 us (50%)
  Pallas kernels  17.6 us (27%)
  waiting for transfers between devices  13.5 us (21%)
    ppermute x21, starting transfers between devices, swap(): lax.ppermute(value, axis, [(i, i ^ bit) for i in range(lax.axis_size(axis...  29.9 us
    pallas_call x27, Pallas kernels, __call__(): pl.pallas_call(body, out_shape=[*outs, *(jax.ShapeDtypeStruct(g.shape, g....  17.6 us
    ppermute x21, waiting for transfers between devices, swap(): lax.ppermute(value, axis, [(i, i ^ bit) for i in range(lax.axis_size(axis...  13.5 us
    ppermute x1, starting transfers between devices, local(): lax.ppermute(tail, 'tm', [(i, i + 1) for i in range(time_parts - 1)])  2.51 us
  transfers between devices with their start and end apart: 22, of which 9 were waited for; matrix products, arithmetic and copies ran while one was open for 0% of the time, Pallas kernels for 22%

profile of v4, /device:TPU:0, one launch (start us, length us, event | category | flops | bytes accessed | tf_op | source)
XLA Modules:
  0.0 63.7 jit_solution(3485695270388265802)
XLA Ops:
  0.0 1.1 %history.1.refs_5_ = bf16[640,128]{1,0:T(8,128)(2,1)S(1)} custom-call(bf16[640,4096]{1,0:T(8,128)(2,1)} %refs_0_.6), custom_call_target="tpu_custom_call" | custom-call | flops 50000000 | bytes 10000 | tf_op jit(solution)/shard_map/history/pallas_call | solution.py:335
  1.1 2.5 %collective-permute-start = (bf16[640,128]{1,0:T(8,128)(2,1)S(1)}, bf16[640,128]{1,0:T(8,128)(2,1)S(1)}, u32[]{:S(2)}, u32[]{:S(2)}) collective-permute-start(bf16[640,128]{1,0:T(8,128)(2,1)S(1)} %history.1.refs_5_), channel_id=1, source_target_pairs={{0,2},{2,4},{4,6},{6,8},{8,10},{10,12},{12,14},{14,16},{16,18},{18... | collective-permute-start | bytes 491528 | tf_op jit(solution)/shard_map/ppermute | solution.py:380
  3.7 3.0 %late.1 = (bf16[3,640,256]{2,1,0:T(8,128)(2,1)S(1)}, bf16[256,1152]{1,0:T(8,128)(2,1)S(1)}, f32[640,128]{1,0:T(8,128)S(1)}, bf16[256,128]{1,0:T(8,128)(2,1)S(1)}, bf16[512,640]{1,0:T(8,128)(2,1)S(1)}) custom-call(bf16[640,4096]{1,0:T(8,128)(2,1)S(1)} %copy-done, bf16[1,128]{1,0:T(2,128)(2,1)S(1)} %bitcast.4, s32[1,640]{1,0:T(1,128)S(1)} %reshape.13.refs_2_, ...), custom_call_target="tpu_custom_call" | custom-call | flops 50000000 | bytes 10000 | tf_op jit(solution)/shard_map/late/pallas_call | solution.py:335
  6.7 1.9 %first.1 = (bf16[4,160,256]{2,1,0:T(8,128)(2,1)S(1)}, bf16[4,640,256]{2,1,0:T(8,128)(2,1)S(1)}) custom-call(bf16[640,4096]{1,0:T(8,128)(2,1)S(1)} %copy-done, bf16[640,128]{1,0:T(8,128)(2,1)S(1)} %collective-permute-done.refs_1_, bf16[256,1152]{1,0:T(8,128)(2,1)S(1)} %get-tuple-element.42.refs_2_, bf16[256,256]{1,0:T(8,128)(2,1)S(1)} %copy-done.1, ...), custom_call_target="tpu_custom_call" | custom-call | flops 500000000 | bytes 10000 | tf_op jit(solution)/shard_map/first/pallas_call | solution.py:335
  8.6 2.4 %collective-permute-start.1 = (bf16[4,160,256]{2,1,0:T(8,128)(2,1)S(1)}, bf16[4,160,256]{2,1,0:T(8,128)(2,1)S(1)}, u32[]{:S(2)}, u32[]{:S(2)}) collective-permute-start(bf16[4,160,256]{2,1,0:T(8,128)(2,1)S(1)} %get-tuple-element.47.refs_2_.refs_0_), channel_id=1, source_target_pairs={{0,1},{1,0},{2,3},{3,2},{4,5},{5,4},{6,7},{7,6},{8,9},{9,8},{10,11... | collective-permute-start | bytes 983048 | tf_op jit(solution)/shard_map/ppermute | solution.py:90
  11.8 1.6 %collective-permute-start.2 = (bf16[4,64,256]{2,1,0:T(8,128)(2,1)S(1)}, bf16[4,64,256]{2,1,0:T(8,128)(2,1)S(1)}, u32[]{:S(2)}, u32[]{:S(2)}) collective-permute-start(bf16[4,64,256]{2,1,0:T(8,128)(2,1)S(1)} %get-tuple-element.54), channel_id=1, source_target_pairs={{0,2},{2,0},{4,6},{6,4},{8,10},{10,8},{12,14},{14,12},{16,18},{18,... | collective-permute-start | bytes 393224 | tf_op jit(solution)/shard_map/ppermute | solution.py:90
  15.5 2.9 %collective-permute-done.1.refs_1_ = bf16[4,160,256]{2,1,0:T(8,128)(2,1)S(1)} collective-permute-done((bf16[4,160,256]{2,1,0:T(8,128)(2,1)S(1)}, bf16[4,160,256]{2,1,0:T(8,128)(2,1)S(1)}, u32[]{:S(2)}, u32[]{:S(2)}) %collective-permute-start.1) | collective-permute-done | bytes 327712 | tf_op jit(solution)/shard_map/ppermute | solution.py:90
  18.4 2.4 %collective-permute-start.5 = (bf16[4,80,256]{2,1,0:T(8,128)(2,1)S(1)}, bf16[4,80,256]{2,1,0:T(8,128)(2,1)S(1)}, u32[]{:S(2)}, u32[]{:S(2)}) collective-permute-start(bf16[4,80,256]{2,1,0:T(8,128)(2,1)S(1)} %get-tuple-element.60), channel_id=1, source_target_pairs={{0,2},{2,0},{4,6},{6,4},{8,10},{10,8},{12,14},{14,12},{16,18},{18,... | collective-permute-start | bytes 491528 | tf_op jit(solution)/shard_map/ppermute | solution.py:90
  20.9 1.8 %collective-permute-start.8 = (bf16[2,4,64,256]{3,2,1,0:T(8,128)(2,1)S(1)}, bf16[2,4,64,256]{3,2,1,0:T(8,128)(2,1)S(1)}, u32[]{:S(2)}, u32[]{:S(2)}) collective-permute-start(bf16[2,4,64,256]{3,2,1,0:T(8,128)(2,1)S(1)} %get-tuple-element.61.refs_0_), channel_id=1, source_target_pairs={{0,1},{1,0},{2,3},{3,2},{4,5},{5,4},{6,7},{7,6},{8,9},{9,8},{10,11... | collective-permute-start | bytes 786440 | tf_op jit(solution)/shard_map/ppermute | solution.py:90
  22.7 1.4 %send_0.1.refs_6_ = bf16[320,640]{1,0:T(8,128)(2,1)S(1)} custom-call(bf16[4,80,256]{2,1,0:T(8,128)(2,1)S(1)} %get-tuple-element.59.refs_0_.refs_6_, bf16[4,80,256]{2,1,0:T(8,128)(2,1)S(1)} %collective-permute-done.5.refs_1_, bf16[4,640,256]{2,1,0:T(8,128)(2,1)S(1)} %get-tuple-element.49.refs_1_.refs_2_, ...), custom_call_target="tpu_custom_call" | custom-call | flops 500000000 | bytes 10000 | tf_op jit(solution)/shard_map/send_0/pallas_call | solution.py:335
  24.1 3.6 %collective-permute-start.7 = (bf16[320,640]{1,0:T(8,128)(2,1)S(1)}, bf16[320,640]{1,0:T(8,128)(2,1)S(1)}, u32[]{:S(2)}, u32[]{:S(2)}) collective-permute-start(bf16[320,640]{1,0:T(8,128)(2,1)S(1)} %send_0.1.refs_6_), channel_id=1, source_target_pairs={{0,8},{2,10},{4,12},{6,14},{8,0},{10,2},{12,4},{14,6},{16,24},{18,... | collective-permute-start | bytes 1228808 | tf_op jit(solution)/shard_map/ppermute | solution.py:90
  27.6 1.4 %keep_0.1.refs_7_.refs_0_ = f32[320,640]{1,0:T(8,128)S(1)} custom-call(bf16[4,80,256]{2,1,0:T(8,128)(2,1)S(1)} %get-tuple-element.59.refs_0_.refs_6_, bf16[4,80,256]{2,1,0:T(8,128)(2,1)S(1)} %collective-permute-done.5.refs_1_, bf16[4,640,256]{2,1,0:T(8,128)(2,1)S(1)} %get-tuple-element.49.refs_1_.refs_2_, ...), custom_call_target="tpu_custom_call" | custom-call | flops 182000000 | bytes 10000 | tf_op jit(solution)/shard_map/keep_0/pallas_call | solution.py:335
  29.0 1.2 %send_1.1.refs_6_ = bf16[256,640]{1,0:T(8,128)(2,1)S(1)} custom-call(bf16[2,4,64,256]{3,2,1,0:T(8,128)(2,1)S(1)} %get-tuple-element.58.refs_3_.refs_0_, bf16[2,4,64,256]{3,2,1,0:T(8,128)(2,1)S(1)} %collective-permute-done.9.refs_1_.refs_6_, bf16[4,640,256]{2,1,0:T(8,128)(2,1)S(1)} %get-tuple-element.49.refs_1_.refs_2_, ...), custom_call_target="tpu_custom_call" | custom-call | flops 15000000512 | bytes 10000 | tf_op jit(solution)/shard_map/send_1/pallas_call | solution.py:335
  30.8 1.3 %collective-permute-start.12 = (bf16[2,4,48,256]{3,2,1,0:T(8,128)(2,1)S(1)}, bf16[2,4,48,256]{3,2,1,0:T(8,128)(2,1)S(1)}, u32[]{:S(2)}, u32[]{:S(2)}) collective-permute-start(bf16[2,4,48,256]{3,2,1,0:T(8,128)(2,1)S(1)} %get-tuple-element.64.refs_0_), channel_id=1, source_target_pairs={{0,1},{1,0},{2,3},{3,2},{4,5},{5,4},{6,7},{7,6},{8,9},{9,8},{10,11... | collective-permute-start | bytes 589832 | tf_op jit(solution)/shard_map/ppermute | solution.py:90
  32.1 1.2 %keep_1.1.refs_7_.refs_0_ = f32[256,640]{1,0:T(8,128)S(1)} custom-call(bf16[2,4,64,256]{3,2,1,0:T(8,128)(2,1)S(1)} %get-tuple-element.58.refs_3_.refs_0_, bf16[2,4,64,256]{3,2,1,0:T(8,128)(2,1)S(1)} %collective-permute-done.9.refs_1_.refs_6_, bf16[4,640,256]{2,1,0:T(8,128)(2,1)S(1)} %get-tuple-element.49.refs_1_.refs_2_, ...), custom_call_target="tpu_custom_call" | custom-call | flops 347000000 | bytes 10000 | tf_op jit(solution)/shard_map/keep_1/pallas_call | solution.py:335
  33.3 1.2 %send_2.1.refs_3_ = bf16[256,640]{1,0:T(8,128)(2,1)S(1)} custom-call(bf16[2,4,64,256]{3,2,1,0:T(8,128)(2,1)S(1)} %get-tuple-element.61.refs_0_, bf16[2,4,64,256]{3,2,1,0:T(8,128)(2,1)S(1)} %collective-permute-done.8.refs_1_.refs_6_, bf16[4,640,256]{2,1,0:T(8,128)(2,1)S(1)} %get-tuple-element.49.refs_1_.refs_2_, ...), custom_call_target="tpu_custom_call" | custom-call | flops 277000000 | bytes 10000 | tf_op jit(solution)/shard_map/send_2/pallas_call | solution.py:335
  34.4 1.3 %collective-permute-start.14 = (bf16[256,640]{1,0:T(8,128)(2,1)S(1)}, bf16[256,640]{1,0:T(8,128)(2,1)S(1)}, u32[]{:S(2)}, u32[]{:S(2)}) collective-permute-start(bf16[256,640]{1,0:T(8,128)(2,1)S(1)} %send_2.1.refs_3_), channel_id=1, source_target_pairs={{0,8},{2,10},{4,12},{6,14},{8,0},{10,2},{12,4},{14,6},{16,24},{18,... | collective-permute-start | bytes 983048 | tf_op jit(solution)/shard_map/ppermute | solution.py:90
  35.7 2.1 %collective-permute-done.7.refs_1_.refs_2_ = bf16[320,640]{1,0:T(8,128)(2,1)S(1)} collective-permute-done((bf16[320,640]{1,0:T(8,128)(2,1)S(1)}, bf16[320,640]{1,0:T(8,128)(2,1)S(1)}, u32[]{:S(2)}, u32[]{:S(2)}) %collective-permute-start.7) | collective-permute-done | bytes 409632 | tf_op jit(solution)/shard_map/ppermute | solution.py:90
  38.4 1.2 %keep_2.1.refs_8_.refs_0_ = f32[256,640]{1,0:T(8,128)S(1)} custom-call(bf16[2,4,64,256]{3,2,1,0:T(8,128)(2,1)S(1)} %get-tuple-element.61.refs_0_, bf16[2,4,64,256]{3,2,1,0:T(8,128)(2,1)S(1)} %collective-permute-done.8.refs_1_.refs_6_, bf16[4,640,256]{2,1,0:T(8,128)(2,1)S(1)} %get-tuple-element.49.refs_1_.refs_2_, ...), custom_call_target="tpu_custom_call" | custom-call | flops 112000000 | bytes 10000 | tf_op jit(solution)/shard_map/keep_2/pallas_call | solution.py:335
  39.8 1.0 %send_3.1.refs_2_ = bf16[192,640]{1,0:T(8,128)(2,1)S(1)} custom-call(bf16[2,4,48,256]{3,2,1,0:T(8,128)(2,1)S(1)} %get-tuple-element.64.refs_0_, bf16[2,4,48,256]{3,2,1,0:T(8,128)(2,1)S(1)} %collective-permute-done.12.refs_1_.refs_6_, bf16[4,640,256]{2,1,0:T(8,128)(2,1)S(1)} %get-tuple-element.49.refs_1_.refs_2_, ...), custom_call_target="tpu_custom_call" | custom-call | flops 275000000 | bytes 10000 | tf_op jit(solution)/shard_map/send_3/pallas_call | solution.py:335
  40.8 1.5 %collective-permute-start.15 = (bf16[192,640]{1,0:T(8,128)(2,1)S(1)}, bf16[192,640]{1,0:T(8,128)(2,1)S(1)}, u32[]{:S(2)}, u32[]{:S(2)}) collective-permute-start(bf16[192,640]{1,0:T(8,128)(2,1)S(1)} %send_3.1.refs_2_), channel_id=1, source_target_pairs={{0,4},{2,6},{4,0},{6,2},{8,12},{10,14},{12,8},{14,10},{16,20},{18,... | collective-permute-start | bytes 737288 | tf_op jit(solution)/shard_map/ppermute | solution.py:90
  42.4 2.1 %collective-permute-start.16 = (bf16[128,640]{1,0:T(8,128)(2,1)S(1)}, bf16[128,640]{1,0:T(8,128)(2,1)S(1)}, u32[]{:S(2)}, u32[]{:S(2)}) collective-permute-start(bf16[128,640]{1,0:T(8,128)(2,1)S(1)} %get-tuple-element.69), channel_id=1, source_target_pairs={{0,8},{2,10},{4,12},{6,14},{8,0},{10,2},{12,4},{14,6},{16,24},{18,... | collective-permute-start | bytes 491528 | tf_op jit(solution)/shard_map/ppermute | solution.py:90
  44.5 1.5 %collective-permute-done.10.refs_1_.refs_3_ = bf16[160,640]{1,0:T(8,128)(2,1)S(1)} collective-permute-done((bf16[160,640]{1,0:T(8,128)(2,1)S(1)}, bf16[160,640]{1,0:T(8,128)(2,1)S(1)}, u32[]{:S(2)}, u32[]{:S(2)}) %collective-permute-start.10) | collective-permute-done | bytes 204832 | tf_op jit(solution)/shard_map/ppermute | solution.py:90
  46.1 2.8 %collective-permute-start.13 = (bf16[80,640]{1,0:T(8,128)(2,1)S(1)}, bf16[80,640]{1,0:T(8,128)(2,1)S(1)}, u32[]{:S(2)}, u32[]{:S(2)}) collective-permute-start(bf16[80,640]{1,0:T(8,128)(2,1)S(1)} %get-tuple-element.67), channel_id=1, source_target_pairs={{0,16},{2,18},{4,20},{6,22},{8,24},{10,26},{12,28},{14,30},{16,0},... | collective-permute-start | bytes 307208 | tf_op jit(solution)/shard_map/ppermute | solution.py:90
  49.0 1.0 %keep_3.1.refs_3_.refs_0_ = f32[192,640]{1,0:T(8,128)S(1)} custom-call(bf16[2,4,48,256]{3,2,1,0:T(8,128)(2,1)S(1)} %get-tuple-element.64.refs_0_, bf16[2,4,48,256]{3,2,1,0:T(8,128)(2,1)S(1)} %collective-permute-done.12.refs_1_.refs_6_, bf16[4,640,256]{2,1,0:T(8,128)(2,1)S(1)} %get-tuple-element.49.refs_1_.refs_2_, ...), custom_call_target="tpu_custom_call" | custom-call | flops 110000000 | bytes 10000 | tf_op jit(solution)/shard_map/keep_3/pallas_call | solution.py:335
  50.1 1.8 %collective-permute-start.17 = (bf16[64,640]{1,0:T(8,128)(2,1)S(1)}, bf16[64,640]{1,0:T(8,128)(2,1)S(1)}, u32[]{:S(2)}, u32[]{:S(2)}) collective-permute-start(bf16[64,640]{1,0:T(8,128)(2,1)S(1)} %get-tuple-element.72), channel_id=1, source_target_pairs={{0,16},{2,18},{4,20},{6,22},{8,24},{10,26},{12,28},{14,30},{16,0},... | collective-permute-start | bytes 245768 | tf_op jit(solution)/shard_map/ppermute | solution.py:90
  52.0 1.6 %collective-permute-start.20 = (bf16[96,640]{1,0:T(8,128)(2,1)S(1)}, bf16[96,640]{1,0:T(8,128)(2,1)S(1)}, u32[]{:S(2)}, u32[]{:S(2)}) collective-permute-start(bf16[96,640]{1,0:T(8,128)(2,1)S(1)} %get-tuple-element.76), channel_id=1, source_target_pairs={{0,8},{2,10},{4,12},{6,14},{8,0},{10,2},{12,4},{14,6},{16,24},{18,... | collective-permute-start | bytes 368648 | tf_op jit(solution)/shard_map/ppermute | solution.py:90
  54.5 1.2 %collective-permute-start.19 = (bf16[64,640]{1,0:T(8,128)(2,1)S(1)}, bf16[64,640]{1,0:T(8,128)(2,1)S(1)}, u32[]{:S(2)}, u32[]{:S(2)}) collective-permute-start(bf16[64,640]{1,0:T(8,128)(2,1)S(1)} %get-tuple-element.75), channel_id=1, source_target_pairs={{0,16},{2,18},{4,20},{6,22},{8,24},{10,26},{12,28},{14,30},{16,0},... | collective-permute-start | bytes 245768 | tf_op jit(solution)/shard_map/ppermute | solution.py:90
  55.8 1.5 %collective-permute-done.20.refs_1_.refs_2_ = bf16[96,640]{1,0:T(8,128)(2,1)S(1)} collective-permute-done((bf16[96,640]{1,0:T(8,128)(2,1)S(1)}, bf16[96,640]{1,0:T(8,128)(2,1)S(1)}, u32[]{:S(2)}, u32[]{:S(2)}) %collective-permute-start.20) | collective-permute-done | bytes 122912 | tf_op jit(solution)/shard_map/ppermute | solution.py:90
  57.3 2.2 %collective-permute-start.21 = (bf16[48,640]{1,0:T(8,128)(2,1)S(1)}, bf16[48,640]{1,0:T(8,128)(2,1)S(1)}, u32[]{:S(2)}, u32[]{:S(2)}) collective-permute-start(bf16[48,640]{1,0:T(8,128)(2,1)S(1)} %get-tuple-element.78), channel_id=1, source_target_pairs={{0,16},{2,18},{4,20},{6,22},{8,24},{10,26},{12,28},{14,30},{16,0},... | collective-permute-start | bytes 184328 | tf_op jit(solution)/shard_map/ppermute | solution.py:90
  59.4 1.5 %collective-permute-done.19.refs_1_ = bf16[64,640]{1,0:T(8,128)(2,1)S(1)} collective-permute-done((bf16[64,640]{1,0:T(8,128)(2,1)S(1)}, bf16[64,640]{1,0:T(8,128)(2,1)S(1)}, u32[]{:S(2)}, u32[]{:S(2)}) %collective-permute-start.19) | collective-permute-done | bytes 81952 | tf_op jit(solution)/shard_map/ppermute | solution.py:90
  60.9 2.0 %collective-permute-done.21.refs_4_ = bf16[48,640]{1,0:T(8,128)(2,1)S(1)} collective-permute-done((bf16[48,640]{1,0:T(8,128)(2,1)S(1)}, bf16[48,640]{1,0:T(8,128)(2,1)S(1)}, u32[]{:S(2)}, u32[]{:S(2)}) %collective-permute-start.21) | collective-permute-done | bytes 61472 | tf_op jit(solution)/shard_map/ppermute | solution.py:90
  (54 shorter events, 6.4 us)
Async XLA Ops:
  0.0 3.6 %copy-start.1 = (bf16[256,256]{1,0:T(8,128)(2,1)S(1)}, bf16[256,256]{1,0:T(8,128)(2,1)}, u32[]{:S(2)}) copy-start(bf16[256,256]{1,0:T(8,128)(2,1)} %constant.6.clone.refs_4_.refs_3_.refs_0_) | copy-start | bytes 393220
  0.0 3.6 %copy-start.6 = (s32[640]{0:T(1024)S(1)}, s32[640]{0:T(1024)}, u32[]{:S(2)}) copy-start(s32[640]{0:T(1024)} %param.10) | copy-start | bytes 7684
  0.0 3.6 %copy-start.5 = (bf16[128]{0:T(256)(128)(2,1)S(1)}, bf16[128]{0:T(256)(128)(2,1)}, u32[]{:S(2)}) copy-start(bf16[128]{0:T(256)(128)(2,1)} %param.8) | copy-start | bytes 772
  0.0 3.7 %copy-start = (bf16[640,4096]{1,0:T(8,128)(2,1)S(1)}, bf16[640,4096]{1,0:T(8,128)(2,1)}, u32[]{:S(2)}) copy-start(bf16[640,4096]{1,0:T(8,128)(2,1)} %refs_0_.6) | copy-start | bytes 15728644
  0.0 3.7 %copy-start.4 = (s32[512]{0:T(512)S(1)}, s32[512]{0:T(512)}, u32[]{:S(2)}) copy-start(s32[512]{0:T(512)} %param.9) | copy-start | bytes 6148
  1.1 5.6 %collective-permute-start = (bf16[640,128]{1,0:T(8,128)(2,1)S(1)}, bf16[640,128]{1,0:T(8,128)(2,1)S(1)}, u32[]{:S(2)}, u32[]{:S(2)}) collective-permute-start(bf16[640,128]{1,0:T(8,128)(2,1)S(1)} %history.1.refs_5_), channel_id=1, source_target_pairs={{0,2},{2,4},{4,6},{6,8},{8,10},{10,12},{12,14},{14,16},{16,18},{18... | collective-permute-start | bytes 491528 | tf_op jit(solution)/shard_map/ppermute | solution.py:380
  8.6 9.8 %collective-permute-start.1 = (bf16[4,160,256]{2,1,0:T(8,128)(2,1)S(1)}, bf16[4,160,256]{2,1,0:T(8,128)(2,1)S(1)}, u32[]{:S(2)}, u32[]{:S(2)}) collective-permute-start(bf16[4,160,256]{2,1,0:T(8,128)(2,1)S(1)} %get-tuple-element.47.refs_2_.refs_0_), channel_id=1, source_target_pairs={{0,1},{1,0},{2,3},{3,2},{4,5},{5,4},{6,7},{7,6},{8,9},{9,8},{10,11... | collective-permute-start | bytes 983048 | tf_op jit(solution)/shard_map/ppermute | solution.py:90
  11.8 3.0 %collective-permute-start.2 = (bf16[4,64,256]{2,1,0:T(8,128)(2,1)S(1)}, bf16[4,64,256]{2,1,0:T(8,128)(2,1)S(1)}, u32[]{:S(2)}, u32[]{:S(2)}) collective-permute-start(bf16[4,64,256]{2,1,0:T(8,128)(2,1)S(1)} %get-tuple-element.54), channel_id=1, source_target_pairs={{0,2},{2,0},{4,6},{6,4},{8,10},{10,8},{12,14},{14,12},{16,18},{18,... | collective-permute-start | bytes 393224 | tf_op jit(solution)/shard_map/ppermute | solution.py:90
  13.3 1.5 %collective-permute-start.3 = (bf16[4,64,256]{2,1,0:T(8,128)(2,1)S(1)}, bf16[4,64,256]{2,1,0:T(8,128)(2,1)S(1)}, u32[]{:S(2)}, u32[]{:S(2)}) collective-permute-start(bf16[4,64,256]{2,1,0:T(8,128)(2,1)S(1)} %get-tuple-element.55), channel_id=1, source_target_pairs={{0,2},{2,0},{4,6},{6,4},{8,10},{10,8},{12,14},{14,12},{16,18},{18,... | collective-permute-start | bytes 393224 | tf_op jit(solution)/shard_map/ppermute | solution.py:90
  13.4 1.4 %collective-permute-start.4 = (bf16[4,48,256]{2,1,0:T(8,128)(2,1)S(1)}, bf16[4,48,256]{2,1,0:T(8,128)(2,1)S(1)}, u32[]{:S(2)}, u32[]{:S(2)}) collective-permute-start(bf16[4,48,256]{2,1,0:T(8,128)(2,1)S(1)} %get-tuple-element.56), channel_id=1, source_target_pairs={{0,2},{2,0},{4,6},{6,4},{8,10},{10,8},{12,14},{14,12},{16,18},{18,... | collective-permute-start | bytes 294920 | tf_op jit(solution)/shard_map/ppermute | solution.py:90
  13.9 8.8 %collective-permute-start.6 = (bf16[4,640,256]{2,1,0:T(8,128)(2,1)S(1)}, bf16[4,640,256]{2,1,0:T(8,128)(2,1)S(1)}, u32[]{:S(2)}, u32[]{:S(2)}) collective-permute-start(bf16[4,640,256]{2,1,0:T(8,128)(2,1)S(1)} %get-tuple-element.49.refs_1_.refs_2_), channel_id=1, source_target_pairs={{0,2},{2,0},{4,6},{6,4},{8,10},{10,8},{12,14},{14,12},{16,18},{18,... | collective-permute-start | bytes 3932168 | tf_op jit(solution)/shard_map/ppermute | solution.py:90
  14.9 14.1 %collective-permute-start.9 = (bf16[2,4,64,256]{3,2,1,0:T(8,128)(2,1)S(1)}, bf16[2,4,64,256]{3,2,1,0:T(8,128)(2,1)S(1)}, u32[]{:S(2)}, u32[]{:S(2)}) collective-permute-start(bf16[2,4,64,256]{3,2,1,0:T(8,128)(2,1)S(1)} %get-tuple-element.58.refs_3_.refs_0_), channel_id=1, source_target_pairs={{0,1},{1,0},{2,3},{3,2},{4,5},{5,4},{6,7},{7,6},{8,9},{9,8},{10,11... | collective-permute-start | bytes 786440 | tf_op jit(solution)/shard_map/ppermute | solution.py:90
  18.4 4.2 %copy-start.2 = (f32[8,128]{1,0:T(8,128)S(1)}, f32[8,128]{1,0:T(8,128)}, u32[]{:S(2)}) copy-start(f32[8,128]{1,0:T(8,128)} %constant.7.clone.refs_4_) | copy-start | bytes 12292
  18.4 4.2 %copy-start.3 = (f32[8,128]{1,0:T(8,128)S(1)}, f32[8,128]{1,0:T(8,128)}, u32[]{:S(2)}) copy-start(f32[8,128]{1,0:T(8,128)} %constant.8.clone.refs_5_) | copy-start | bytes 12292
  18.4 4.2 %collective-permute-start.5 = (bf16[4,80,256]{2,1,0:T(8,128)(2,1)S(1)}, bf16[4,80,256]{2,1,0:T(8,128)(2,1)S(1)}, u32[]{:S(2)}, u32[]{:S(2)}) collective-permute-start(bf16[4,80,256]{2,1,0:T(8,128)(2,1)S(1)} %get-tuple-element.60), channel_id=1, source_target_pairs={{0,2},{2,0},{4,6},{6,4},{8,10},{10,8},{12,14},{14,12},{16,18},{18,... | collective-permute-start | bytes 491528 | tf_op jit(solution)/shard_map/ppermute | solution.py:90
  20.9 12.4 %collective-permute-start.8 = (bf16[2,4,64,256]{3,2,1,0:T(8,128)(2,1)S(1)}, bf16[2,4,64,256]{3,2,1,0:T(8,128)(2,1)S(1)}, u32[]{:S(2)}, u32[]{:S(2)}) collective-permute-start(bf16[2,4,64,256]{3,2,1,0:T(8,128)(2,1)S(1)} %get-tuple-element.61.refs_0_), channel_id=1, source_target_pairs={{0,1},{1,0},{2,3},{3,2},{4,5},{5,4},{6,7},{7,6},{8,9},{9,8},{10,11... | collective-permute-start | bytes 786440 | tf_op jit(solution)/shard_map/ppermute | solution.py:90
  24.1 13.8 %collective-permute-start.7 = (bf16[320,640]{1,0:T(8,128)(2,1)S(1)}, bf16[320,640]{1,0:T(8,128)(2,1)S(1)}, u32[]{:S(2)}, u32[]{:S(2)}) collective-permute-start(bf16[320,640]{1,0:T(8,128)(2,1)S(1)} %send_0.1.refs_6_), channel_id=1, source_target_pairs={{0,8},{2,10},{4,12},{6,14},{8,0},{10,2},{12,4},{14,6},{16,24},{18,... | collective-permute-start | bytes 1228808 | tf_op jit(solution)/shard_map/ppermute | solution.py:90
  30.2 9.6 %collective-permute-start.11 = (bf16[256,640]{1,0:T(8,128)(2,1)S(1)}, bf16[256,640]{1,0:T(8,128)(2,1)S(1)}, u32[]{:S(2)}, u32[]{:S(2)}) collective-permute-start(bf16[256,640]{1,0:T(8,128)(2,1)S(1)} %send_1.1.refs_6_), channel_id=1, source_target_pairs={{0,4},{2,6},{4,0},{6,2},{8,12},{10,14},{12,8},{14,10},{16,20},{18,... | collective-permute-start | bytes 983048 | tf_op jit(solution)/shard_map/ppermute | solution.py:90
  30.8 8.8 %collective-permute-start.12 = (bf16[2,4,48,256]{3,2,1,0:T(8,128)(2,1)S(1)}, bf16[2,4,48,256]{3,2,1,0:T(8,128)(2,1)S(1)}, u32[]{:S(2)}, u32[]{:S(2)}) collective-permute-start(bf16[2,4,48,256]{3,2,1,0:T(8,128)(2,1)S(1)} %get-tuple-element.64.refs_0_), channel_id=1, source_target_pairs={{0,1},{1,0},{2,3},{3,2},{4,5},{5,4},{6,7},{7,6},{8,9},{9,8},{10,11... | collective-permute-start | bytes 589832 | tf_op jit(solution)/shard_map/ppermute | solution.py:90
  34.4 14.4 %collective-permute-start.14 = (bf16[256,640]{1,0:T(8,128)(2,1)S(1)}, bf16[256,640]{1,0:T(8,128)(2,1)S(1)}, u32[]{:S(2)}, u32[]{:S(2)}) collective-permute-start(bf16[256,640]{1,0:T(8,128)(2,1)S(1)} %send_2.1.refs_3_), channel_id=1, source_target_pairs={{0,8},{2,10},{4,12},{6,14},{8,0},{10,2},{12,4},{14,6},{16,24},{18,... | collective-permute-start | bytes 983048 | tf_op jit(solution)/shard_map/ppermute | solution.py:90
  38.0 8.1 %collective-permute-start.10 = (bf16[160,640]{1,0:T(8,128)(2,1)S(1)}, bf16[160,640]{1,0:T(8,128)(2,1)S(1)}, u32[]{:S(2)}, u32[]{:S(2)}) collective-permute-start(bf16[160,640]{1,0:T(8,128)(2,1)S(1)} %get-tuple-element.63), channel_id=1, source_target_pairs={{0,4},{2,6},{4,0},{6,2},{8,12},{10,14},{12,8},{14,10},{16,20},{18,... | collective-permute-start | bytes 614408 | tf_op jit(solution)/shard_map/ppermute | solution.py:90
  40.8 11.1 %collective-permute-start.15 = (bf16[192,640]{1,0:T(8,128)(2,1)S(1)}, bf16[192,640]{1,0:T(8,128)(2,1)S(1)}, u32[]{:S(2)}, u32[]{:S(2)}) collective-permute-start(bf16[192,640]{1,0:T(8,128)(2,1)S(1)} %send_3.1.refs_2_), channel_id=1, source_target_pairs={{0,4},{2,6},{4,0},{6,2},{8,12},{10,14},{12,8},{14,10},{16,20},{18,... | collective-permute-start | bytes 737288 | tf_op jit(solution)/shard_map/ppermute | solution.py:90
  42.4 7.7 %collective-permute-start.16 = (bf16[128,640]{1,0:T(8,128)(2,1)S(1)}, bf16[128,640]{1,0:T(8,128)(2,1)S(1)}, u32[]{:S(2)}, u32[]{:S(2)}) collective-permute-start(bf16[128,640]{1,0:T(8,128)(2,1)S(1)} %get-tuple-element.69), channel_id=1, source_target_pairs={{0,8},{2,10},{4,12},{6,14},{8,0},{10,2},{12,4},{14,6},{16,24},{18,... | collective-permute-start | bytes 491528 | tf_op jit(solution)/shard_map/ppermute | solution.py:90
  46.1 8.4 %collective-permute-start.13 = (bf16[80,640]{1,0:T(8,128)(2,1)S(1)}, bf16[80,640]{1,0:T(8,128)(2,1)S(1)}, u32[]{:S(2)}, u32[]{:S(2)}) collective-permute-start(bf16[80,640]{1,0:T(8,128)(2,1)S(1)} %get-tuple-element.67), channel_id=1, source_target_pairs={{0,16},{2,18},{4,20},{6,22},{8,24},{10,26},{12,28},{14,30},{16,0},... | collective-permute-start | bytes 307208 | tf_op jit(solution)/shard_map/ppermute | solution.py:90
  49.0 5.5 %collective-permute-start.18 = (bf16[128,640]{1,0:T(8,128)(2,1)S(1)}, bf16[128,640]{1,0:T(8,128)(2,1)S(1)}, u32[]{:S(2)}, u32[]{:S(2)}) collective-permute-start(bf16[128,640]{1,0:T(8,128)(2,1)S(1)} %get-tuple-element.73), channel_id=1, source_target_pairs={{0,4},{2,6},{4,0},{6,2},{8,12},{10,14},{12,8},{14,10},{16,20},{18,... | collective-permute-start | bytes 491528 | tf_op jit(solution)/shard_map/ppermute | solution.py:90
  50.1 5.6 %collective-permute-start.17 = (bf16[64,640]{1,0:T(8,128)(2,1)S(1)}, bf16[64,640]{1,0:T(8,128)(2,1)S(1)}, u32[]{:S(2)}, u32[]{:S(2)}) collective-permute-start(bf16[64,640]{1,0:T(8,128)(2,1)S(1)} %get-tuple-element.72), channel_id=1, source_target_pairs={{0,16},{2,18},{4,20},{6,22},{8,24},{10,26},{12,28},{14,30},{16,0},... | collective-permute-start | bytes 245768 | tf_op jit(solution)/shard_map/ppermute | solution.py:90
  52.0 5.3 %collective-permute-start.20 = (bf16[96,640]{1,0:T(8,128)(2,1)S(1)}, bf16[96,640]{1,0:T(8,128)(2,1)S(1)}, u32[]{:S(2)}, u32[]{:S(2)}) collective-permute-start(bf16[96,640]{1,0:T(8,128)(2,1)S(1)} %get-tuple-element.76), channel_id=1, source_target_pairs={{0,8},{2,10},{4,12},{6,14},{8,0},{10,2},{12,4},{14,6},{16,24},{18,... | collective-permute-start | bytes 368648 | tf_op jit(solution)/shard_map/ppermute | solution.py:90
  54.5 6.4 %collective-permute-start.19 = (bf16[64,640]{1,0:T(8,128)(2,1)S(1)}, bf16[64,640]{1,0:T(8,128)(2,1)S(1)}, u32[]{:S(2)}, u32[]{:S(2)}) collective-permute-start(bf16[64,640]{1,0:T(8,128)(2,1)S(1)} %get-tuple-element.75), channel_id=1, source_target_pairs={{0,16},{2,18},{4,20},{6,22},{8,24},{10,26},{12,28},{14,30},{16,0},... | collective-permute-start | bytes 245768 | tf_op jit(solution)/shard_map/ppermute | solution.py:90
  57.3 5.6 %collective-permute-start.21 = (bf16[48,640]{1,0:T(8,128)(2,1)S(1)}, bf16[48,640]{1,0:T(8,128)(2,1)S(1)}, u32[]{:S(2)}, u32[]{:S(2)}) collective-permute-start(bf16[48,640]{1,0:T(8,128)(2,1)S(1)} %get-tuple-element.78), channel_id=1, source_target_pairs={{0,16},{2,18},{4,20},{6,22},{8,24},{10,26},{12,28},{14,30},{16,0},... | collective-permute-start | bytes 184328 | tf_op jit(solution)/shard_map/ppermute | solution.py:90

commit v5 on v4

--- a/solution.py
+++ b/solution.py
@@ -18,28 +18,30 @@
 DECIM = 4
 SPAN = DECIM * TD
 VMEM_LIMIT = 20 * 1024 * 1024
-CHUNKS = (10, 8, 8, 6)
-FIRST = (1, 0, 1, 0)
-SECOND = ((1,), (3,), (0,), (2,))
+CHUNKS = (6, 6, 6, 8, 6)
+FIRST = (1, 1, 0, 1, 0)
+SECOND = ((2,), (4,), (0, 1), (3,))
 THIRD = ((2,), (0,), (3,), (1,))
-ACROSS = ((1,), (2,), (3,))
+ACROSS = ((1,), (2,), (3,), (4,))
 PLAN = (
-    ('merge', 0, (1, 2), ()),
-    ('split', 0, (3,), ()),
+    ('merge', 0, (1, 2, 3), ()),
+    ('split', 0, (), ()),
     ('send', 0, (), ()),
-    ('keep', 0, (), ()),
-    ('send', 1, (), (('y', 1),)),
+    ('keep', 0, (4,), ()),
+    ('send', 1, (), ()),
     ('keep', 1, (), ()),
     ('send', 2, (), (('y', 2),)),
-    ('second', 2, (), (('first', 0),)),
-    ('keep', 2, (), ()),
-    ('send', 3, (), (('y', 3), ('first', 1))),
+    ('keep', 2, (), (('first', 0),)),
+    ('send', 3, (), (('y', 3),)),
+    ('second', 2, (), ()),
+    ('keep', 3, (), ()),
+    ('send', 4, (), (('y', 4),)),
     ('second', 0, (), ()),
-    ('third', 0, (), ()),
-    ('second', 3, (), (('first', 2),)),
-    ('keep', 3, (), ()),
+    ('third', 0, (), (('first', 2),)),
+    ('second', 3, (), (('first', 3),)),
+    ('keep', 4, (), ()),
     ('third', 1, (), (('second', 0),)),
-    ('second', 1, (), (('first', 3), ('second', 2))),
+    ('second', 1, (), (('first', 4), ('second', 2))),
     ('sum', 0, (), (('third', 0),)),
     ('third', 2, (), (('second', 3),)),
     ('sum', 1, (), (('third', 1),)),
@@ -52,26 +54,28 @@
     'split_0': 15,
     'send_0': 0.5,
     'keep_0': 0.182,
-    'send_1': 15,
-    'keep_1': 0.347,
-    'send_2': 0.277,
+    'send_2': 15,
+    'keep_2': 0.347,
+    'send_3': 0.277,
     'second_2': 0.191,
-    'keep_2': 0.112,
-    'send_3': 0.275,
+    'keep_3': 0.112,
+    'send_4': 0.275,
     'second_0': 0.191,
-    'keep_3': 0.11,
+    'keep_4': 0.11,
     'third_0': 0.286,
     'second_3': 0.191,
     'third_1': 0.286,
-    'second_1': 4,
+    'second_1': 2,
     'sum_0': 0.027,
     'third_2': 0.304,
     'sum_1': 1,
     'third_3': 0.373,
     'sum_2': 0.293,
     'panels': 0.05,
-    'gate': 0.05,
+    'gate': 4,
     'first': 0.5,
+    'send_1': 0.05,
+    'keep_1': 0.05,
 }
 
 VMEM = pl.BlockSpec(memory_space=pltpu.VMEM)

time: 64.4 us -> 63.4 us (0.984)
  starting transfers between devices: 32.4 us -> 30.6 us
  Pallas kernels: 17.6 us -> 18.6 us
    ppermute x21 -> x24, starting transfers between devices: 29.9 us -> 28.1 us  [swap(): lax.ppermute(value, axis, [(i, i ^ bit) for i in range(lax.axis_size(axis...]
    pallas_call x27 -> x29, Pallas kernels: 17.6 us -> 18.6 us  [__call__(): pl.pallas_call(body, out_shape=[*outs, *(jax.ShapeDtypeStruct(g.shape, g....]
    ppermute x21 -> x24, waiting for transfers between devices: 13.5 us -> 13.6 us  [swap(): lax.ppermute(value, axis, [(i, i ^ bit) for i in range(lax.axis_size(axis...]
  transfers between devices with their start and end apart: 22 -> 25, of which waited for: 9 -> 11; matrix products, arithmetic and copies ran while one was open for 0% -> 0% of each run, Pallas kernels for 22% -> 24%
where the time goes in v5:
time: 63.4 us; the launch traced here: 63.2 us
  starting transfers between devices  30.6 us (48%)
  Pallas kernels  18.6 us (29%)
  waiting for transfers between devices  13.6 us (21%)
    ppermute x24, starting transfers between devices, swap(): lax.ppermute(value, axis, [(i, i ^ bit) for i in range(lax.axis_size(axis...  28.1 us
    pallas_call x29, Pallas kernels, __call__(): pl.pallas_call(body, out_shape=[*outs, *(jax.ShapeDtypeStruct(g.shape, g....  18.6 us
    ppermute x24, waiting for transfers between devices, swap(): lax.ppermute(value, axis, [(i, i ^ bit) for i in range(lax.axis_size(axis...  13.6 us
    ppermute x1, starting transfers between devices, local(): lax.ppermute(tail, 'tm', [(i, i + 1) for i in range(time_parts - 1)])  2.51 us
  transfers between devices with their start and end apart: 25, of which 11 were waited for; matrix products, arithmetic and copies ran while one was open for 0% of the time, Pallas kernels for 24%

profile of v5, /device:TPU:0, one launch (start us, length us, event | category | flops | bytes accessed | tf_op | source)
XLA Modules:
  0.0 63.2 jit_solution(4641624144393743670)
XLA Ops:
  0.0 1.1 %history.1.refs_5_ = bf16[640,128]{1,0:T(8,128)(2,1)S(1)} custom-call(bf16[640,4096]{1,0:T(8,128)(2,1)} %refs_0_.6), custom_call_target="tpu_custom_call" | custom-call | flops 50000000 | bytes 10000 | tf_op jit(solution)/shard_map/history/pallas_call | solution.py:339
  1.1 2.5 %collective-permute-start = (bf16[640,128]{1,0:T(8,128)(2,1)S(1)}, bf16[640,128]{1,0:T(8,128)(2,1)S(1)}, u32[]{:S(2)}, u32[]{:S(2)}) collective-permute-start(bf16[640,128]{1,0:T(8,128)(2,1)S(1)} %history.1.refs_5_), channel_id=1, source_target_pairs={{0,2},{2,4},{4,6},{6,8},{8,10},{10,12},{12,14},{14,16},{16,18},{18... | collective-permute-start | bytes 491528 | tf_op jit(solution)/shard_map/ppermute | solution.py:384
  3.7 3.0 %late.1 = (bf16[3,640,256]{2,1,0:T(8,128)(2,1)S(1)}, bf16[256,1152]{1,0:T(8,128)(2,1)S(1)}, f32[640,128]{1,0:T(8,128)S(1)}, bf16[256,128]{1,0:T(8,128)(2,1)S(1)}, bf16[512,640]{1,0:T(8,128)(2,1)S(1)}) custom-call(bf16[640,4096]{1,0:T(8,128)(2,1)S(1)} %copy-done, bf16[1,128]{1,0:T(2,128)(2,1)S(1)} %bitcast.4, s32[1,640]{1,0:T(1,128)S(1)} %reshape.13.refs_2_, ...), custom_call_target="tpu_custom_call" | custom-call | flops 50000000 | bytes 10000 | tf_op jit(solution)/shard_map/late/pallas_call | solution.py:339
  6.7 1.8 %first.1 = (bf16[4,96,256]{2,1,0:T(8,128)(2,1)S(1)}, bf16[4,640,256]{2,1,0:T(8,128)(2,1)S(1)}) custom-call(bf16[640,4096]{1,0:T(8,128)(2,1)S(1)} %copy-done, bf16[640,128]{1,0:T(8,128)(2,1)S(1)} %collective-permute-done.refs_1_, bf16[256,1152]{1,0:T(8,128)(2,1)S(1)} %get-tuple-element.46.refs_2_, bf16[256,256]{1,0:T(8,128)(2,1)S(1)} %copy-done.1, ...), custom_call_target="tpu_custom_call" | custom-call | flops 500000000 | bytes 10000 | tf_op jit(solution)/shard_map/first/pallas_call | solution.py:339
  8.5 2.4 %collective-permute-start.1 = (bf16[4,96,256]{2,1,0:T(8,128)(2,1)S(1)}, bf16[4,96,256]{2,1,0:T(8,128)(2,1)S(1)}, u32[]{:S(2)}, u32[]{:S(2)}) collective-permute-start(bf16[4,96,256]{2,1,0:T(8,128)(2,1)S(1)} %get-tuple-element.51.refs_2_.refs_0_), channel_id=1, source_target_pairs={{0,1},{1,0},{2,3},{3,2},{4,5},{5,4},{6,7},{7,6},{8,9},{9,8},{10,11... | collective-permute-start | bytes 589832 | tf_op jit(solution)/shard_map/ppermute | solution.py:94
  11.7 1.6 %collective-permute-start.4 = (bf16[4,64,256]{2,1,0:T(8,128)(2,1)S(1)}, bf16[4,64,256]{2,1,0:T(8,128)(2,1)S(1)}, u32[]{:S(2)}, u32[]{:S(2)}) collective-permute-start(bf16[4,64,256]{2,1,0:T(8,128)(2,1)S(1)} %get-tuple-element.61), channel_id=1, source_target_pairs={{0,2},{2,0},{4,6},{6,4},{8,10},{10,8},{12,14},{14,12},{16,18},{18,... | collective-permute-start | bytes 393224 | tf_op jit(solution)/shard_map/ppermute | solution.py:94
  15.7 1.5 %collective-permute-start.12 = (bf16[2,4,48,256]{3,2,1,0:T(8,128)(2,1)S(1)}, bf16[2,4,48,256]{3,2,1,0:T(8,128)(2,1)S(1)}, u32[]{:S(2)}, u32[]{:S(2)}) collective-permute-start(bf16[2,4,48,256]{3,2,1,0:T(8,128)(2,1)S(1)} %get-tuple-element.69.refs_0_), channel_id=1, source_target_pairs={{0,1},{1,0},{2,3},{3,2},{4,5},{5,4},{6,7},{7,6},{8,9},{9,8},{10,11... | collective-permute-start | bytes 589832 | tf_op jit(solution)/shard_map/ppermute | solution.py:94
  17.4 1.2 %collective-permute-start.11 = (bf16[2,4,64,256]{3,2,1,0:T(8,128)(2,1)S(1)}, bf16[2,4,64,256]{3,2,1,0:T(8,128)(2,1)S(1)}, u32[]{:S(2)}, u32[]{:S(2)}) collective-permute-start(bf16[2,4,64,256]{3,2,1,0:T(8,128)(2,1)S(1)} %get-tuple-element.68.refs_0_), channel_id=1, source_target_pairs={{0,1},{1,0},{2,3},{3,2},{4,5},{5,4},{6,7},{7,6},{8,9},{9,8},{10,11... | collective-permute-start | bytes 786440 | tf_op jit(solution)/shard_map/ppermute | solution.py:94
  18.7 1.0 %send_0.1.refs_7_ = bf16[192,640]{1,0:T(8,128)(2,1)S(1)} custom-call(bf16[4,48,256]{2,1,0:T(8,128)(2,1)S(1)} %get-tuple-element.64.refs_0_.refs_6_, bf16[4,48,256]{2,1,0:T(8,128)(2,1)S(1)} %collective-permute-done.6.refs_1_, bf16[4,640,256]{2,1,0:T(8,128)(2,1)S(1)} %get-tuple-element.53.refs_1_.refs_2_, ...), custom_call_target="tpu_custom_call" | custom-call | flops 500000000 | bytes 10000 | tf_op jit(solution)/shard_map/send_0/pallas_call | solution.py:339
  19.7 3.0 %collective-permute-start.8 = (bf16[192,640]{1,0:T(8,128)(2,1)S(1)}, bf16[192,640]{1,0:T(8,128)(2,1)S(1)}, u32[]{:S(2)}, u32[]{:S(2)}) collective-permute-start(bf16[192,640]{1,0:T(8,128)(2,1)S(1)} %send_0.1.refs_7_), channel_id=1, source_target_pairs={{0,8},{2,10},{4,12},{6,14},{8,0},{10,2},{12,4},{14,6},{16,24},{18,... | collective-permute-start | bytes 737288 | tf_op jit(solution)/shard_map/ppermute | solution.py:94
  22.7 1.0 %keep_0.1 = (f32[192,640]{1,0:T(8,128)S(1)}, bf16[2,4,48,256]{3,2,1,0:T(8,128)(2,1)S(1)}) custom-call(bf16[4,48,256]{2,1,0:T(8,128)(2,1)S(1)} %get-tuple-element.64.refs_0_.refs_6_, bf16[4,48,256]{2,1,0:T(8,128)(2,1)S(1)} %collective-permute-done.6.refs_1_, ...), custom_call_target="tpu_custom_call", output_to_operand_aliasing={{1}: (6, {})} | custom-call | flops 182000000 | bytes 10000 | tf_op jit(solution)/shard_map/keep_0/pallas_call | solution.py:339
  23.7 1.0 %send_1.1.refs_6_ = bf16[192,640]{1,0:T(8,128)(2,1)S(1)} custom-call(bf16[2,4,48,256]{3,2,1,0:T(8,128)(2,1)S(1)} %get-tuple-element.63.refs_2_.refs_0_, bf16[2,4,48,256]{3,2,1,0:T(8,128)(2,1)S(1)} %collective-permute-done.9.refs_1_, bf16[4,640,256]{2,1,0:T(8,128)(2,1)S(1)} %get-tuple-element.53.refs_1_.refs_2_, ...), custom_call_target="tpu_custom_call" | custom-call | flops 50000000 | bytes 10000 | tf_op jit(solution)/shard_map/send_1/pallas_call | solution.py:339
  24.7 2.3 %collective-permute-start.10 = (bf16[192,640]{1,0:T(8,128)(2,1)S(1)}, bf16[192,640]{1,0:T(8,128)(2,1)S(1)}, u32[]{:S(2)}, u32[]{:S(2)}) collective-permute-start(bf16[192,640]{1,0:T(8,128)(2,1)S(1)} %send_1.1.refs_6_), channel_id=1, source_target_pairs={{0,8},{2,10},{4,12},{6,14},{8,0},{10,2},{12,4},{14,6},{16,24},{18,... | collective-permute-start | bytes 737288 | tf_op jit(solution)/shard_map/ppermute | solution.py:94
  27.5 1.0 %keep_1.1.refs_7_.refs_2_ = f32[192,640]{1,0:T(8,128)S(1)} custom-call(bf16[2,4,48,256]{3,2,1,0:T(8,128)(2,1)S(1)} %get-tuple-element.63.refs_2_.refs_0_, bf16[2,4,48,256]{3,2,1,0:T(8,128)(2,1)S(1)} %collective-permute-done.9.refs_1_, bf16[4,640,256]{2,1,0:T(8,128)(2,1)S(1)} %get-tuple-element.53.refs_1_.refs_2_, ...), custom_call_target="tpu_custom_call" | custom-call | flops 50000000 | bytes 10000 | tf_op jit(solution)/shard_map/keep_1/pallas_call | solution.py:339
  28.5 1.0 %send_2.1.refs_7_ = bf16[192,640]{1,0:T(8,128)(2,1)S(1)} custom-call(bf16[2,4,48,256]{3,2,1,0:T(8,128)(2,1)S(1)} %get-tuple-element.69.refs_0_, bf16[2,4,48,256]{3,2,1,0:T(8,128)(2,1)S(1)} %collective-permute-done.12.refs_1_.refs_6_, bf16[4,640,256]{2,1,0:T(8,128)(2,1)S(1)} %get-tuple-element.53.refs_1_.refs_2_, ...), custom_call_target="tpu_custom_call" | custom-call | flops 15000000512 | bytes 10000 | tf_op jit(solution)/shard_map/send_2/pallas_call | solution.py:339
  30.3 1.0 %keep_2.1.refs_7_.refs_0_ = f32[192,640]{1,0:T(8,128)S(1)} custom-call(bf16[2,4,48,256]{3,2,1,0:T(8,128)(2,1)S(1)} %get-tuple-element.69.refs_0_, bf16[2,4,48,256]{3,2,1,0:T(8,128)(2,1)S(1)} %collective-permute-done.12.refs_1_.refs_6_, bf16[4,640,256]{2,1,0:T(8,128)(2,1)S(1)} %get-tuple-element.53.refs_1_.refs_2_, ...), custom_call_target="tpu_custom_call" | custom-call | flops 347000000 | bytes 10000 | tf_op jit(solution)/shard_map/keep_2/pallas_call | solution.py:339
  31.3 1.5 %collective-permute-done.11.refs_1_.refs_6_ = bf16[2,4,64,256]{3,2,1,0:T(8,128)(2,1)S(1)} collective-permute-done((bf16[2,4,64,256]{3,2,1,0:T(8,128)(2,1)S(1)}, bf16[2,4,64,256]{3,2,1,0:T(8,128)(2,1)S(1)}, u32[]{:S(2)}, u32[]{:S(2)}) %collective-permute-start.11) | collective-permute-done | bytes 262176 | tf_op jit(solution)/shard_map/ppermute | solution.py:94
  32.8 1.2 %send_3.1.refs_4_ = bf16[256,640]{1,0:T(8,128)(2,1)S(1)} custom-call(bf16[2,4,64,256]{3,2,1,0:T(8,128)(2,1)S(1)} %get-tuple-element.68.refs_0_, bf16[2,4,64,256]{3,2,1,0:T(8,128)(2,1)S(1)} %collective-permute-done.11.refs_1_.refs_6_, bf16[4,640,256]{2,1,0:T(8,128)(2,1)S(1)} %get-tuple-element.53.refs_1_.refs_2_, ...), custom_call_target="tpu_custom_call" | custom-call | flops 277000000 | bytes 10000 | tf_op jit(solution)/shard_map/send_3/pallas_call | solution.py:339
  34.0 3.0 %collective-permute-start.17 = (bf16[256,640]{1,0:T(8,128)(2,1)S(1)}, bf16[256,640]{1,0:T(8,128)(2,1)S(1)}, u32[]{:S(2)}, u32[]{:S(2)}) collective-permute-start(bf16[256,640]{1,0:T(8,128)(2,1)S(1)} %send_3.1.refs_4_), channel_id=1, source_target_pairs={{0,8},{2,10},{4,12},{6,14},{8,0},{10,2},{12,4},{14,6},{16,24},{18,... | collective-permute-start | bytes 983048 | tf_op jit(solution)/shard_map/ppermute | solution.py:94
  37.7 1.3 %keep_3.1.refs_7_.refs_0_ = f32[256,640]{1,0:T(8,128)S(1)} custom-call(bf16[2,4,64,256]{3,2,1,0:T(8,128)(2,1)S(1)} %get-tuple-element.68.refs_0_, bf16[2,4,64,256]{3,2,1,0:T(8,128)(2,1)S(1)} %collective-permute-done.11.refs_1_.refs_6_, bf16[4,640,256]{2,1,0:T(8,128)(2,1)S(1)} %get-tuple-element.53.refs_1_.refs_2_, ...), custom_call_target="tpu_custom_call" | custom-call | flops 112000000 | bytes 10000 | tf_op jit(solution)/shard_map/keep_3/pallas_call | solution.py:339
  39.1 1.0 %send_4.1.refs_2_ = bf16[192,640]{1,0:T(8,128)(2,1)S(1)} custom-call(bf16[2,4,48,256]{3,2,1,0:T(8,128)(2,1)S(1)} %get-tuple-element.72.refs_0_, bf16[2,4,48,256]{3,2,1,0:T(8,128)(2,1)S(1)} %collective-permute-done.15.refs_1_.refs_6_, bf16[4,640,256]{2,1,0:T(8,128)(2,1)S(1)} %get-tuple-element.53.refs_1_.refs_2_, ...), custom_call_target="tpu_custom_call" | custom-call | flops 275000000 | bytes 10000 | tf_op jit(solution)/shard_map/send_4/pallas_call | solution.py:339
  40.1 1.5 %collective-permute-start.18 = (bf16[192,640]{1,0:T(8,128)(2,1)S(1)}, bf16[192,640]{1,0:T(8,128)(2,1)S(1)}, u32[]{:S(2)}, u32[]{:S(2)}) collective-permute-start(bf16[192,640]{1,0:T(8,128)(2,1)S(1)} %send_4.1.refs_2_), channel_id=1, source_target_pairs={{0,4},{2,6},{4,0},{6,2},{8,12},{10,14},{12,8},{14,10},{16,20},{18,... | collective-permute-start | bytes 737288 | tf_op jit(solution)/shard_map/ppermute | solution.py:94
  41.7 4.3 %collective-permute-done.13.refs_1_.refs_3_ = bf16[192,640]{1,0:T(8,128)(2,1)S(1)} collective-permute-done((bf16[192,640]{1,0:T(8,128)(2,1)S(1)}, bf16[192,640]{1,0:T(8,128)(2,1)S(1)}, u32[]{:S(2)}, u32[]{:S(2)}) %collective-permute-start.13) | collective-permute-done | bytes 245792 | tf_op jit(solution)/shard_map/ppermute | solution.py:94
  46.1 2.7 %collective-permute-start.16 = (bf16[96,640]{1,0:T(8,128)(2,1)S(1)}, bf16[96,640]{1,0:T(8,128)(2,1)S(1)}, u32[]{:S(2)}, u32[]{:S(2)}) collective-permute-start(bf16[96,640]{1,0:T(8,128)(2,1)S(1)} %get-tuple-element.75), channel_id=1, source_target_pairs={{0,16},{2,18},{4,20},{6,22},{8,24},{10,26},{12,28},{14,30},{16,0},... | collective-permute-start | bytes 368648 | tf_op jit(solution)/shard_map/ppermute | solution.py:94
  48.9 1.0 %keep_4.1.refs_3_.refs_0_ = f32[192,640]{1,0:T(8,128)S(1)} custom-call(bf16[2,4,48,256]{3,2,1,0:T(8,128)(2,1)S(1)} %get-tuple-element.72.refs_0_, bf16[2,4,48,256]{3,2,1,0:T(8,128)(2,1)S(1)} %collective-permute-done.15.refs_1_.refs_6_, bf16[4,640,256]{2,1,0:T(8,128)(2,1)S(1)} %get-tuple-element.53.refs_1_.refs_2_, ...), custom_call_target="tpu_custom_call" | custom-call | flops 110000000 | bytes 10000 | tf_op jit(solution)/shard_map/keep_4/pallas_call | solution.py:339
  50.7 2.0 %collective-permute-start.23 = (bf16[96,640]{1,0:T(8,128)(2,1)S(1)}, bf16[96,640]{1,0:T(8,128)(2,1)S(1)}, u32[]{:S(2)}, u32[]{:S(2)}) collective-permute-start(bf16[96,640]{1,0:T(8,128)(2,1)S(1)} %get-tuple-element.84), channel_id=1, source_target_pairs={{0,8},{2,10},{4,12},{6,14},{8,0},{10,2},{12,4},{14,6},{16,24},{18,... | collective-permute-start | bytes 368648 | tf_op jit(solution)/shard_map/ppermute | solution.py:94
  54.2 1.4 %collective-permute-start.22 = (bf16[64,640]{1,0:T(8,128)(2,1)S(1)}, bf16[64,640]{1,0:T(8,128)(2,1)S(1)}, u32[]{:S(2)}, u32[]{:S(2)}) collective-permute-start(bf16[64,640]{1,0:T(8,128)(2,1)S(1)} %get-tuple-element.83), channel_id=1, source_target_pairs={{0,16},{2,18},{4,20},{6,22},{8,24},{10,26},{12,28},{14,30},{16,0},... | collective-permute-start | bytes 245768 | tf_op jit(solution)/shard_map/ppermute | solution.py:94
  55.7 1.3 %collective-permute-done.20.refs_1_.refs_2_ = bf16[48,640]{1,0:T(8,128)(2,1)S(1)} collective-permute-done((bf16[48,640]{1,0:T(8,128)(2,1)S(1)}, bf16[48,640]{1,0:T(8,128)(2,1)S(1)}, u32[]{:S(2)}, u32[]{:S(2)}) %collective-permute-start.20) | collective-permute-done | bytes 61472 | tf_op jit(solution)/shard_map/ppermute | solution.py:94
  57.0 1.4 %collective-permute-start.24 = (bf16[48,640]{1,0:T(8,128)(2,1)S(1)}, bf16[48,640]{1,0:T(8,128)(2,1)S(1)}, u32[]{:S(2)}, u32[]{:S(2)}) collective-permute-start(bf16[48,640]{1,0:T(8,128)(2,1)S(1)} %get-tuple-element.86), channel_id=1, source_target_pairs={{0,16},{2,18},{4,20},{6,22},{8,24},{10,26},{12,28},{14,30},{16,0},... | collective-permute-start | bytes 184328 | tf_op jit(solution)/shard_map/ppermute | solution.py:94
  58.4 1.9 %collective-permute-done.22.refs_1_ = bf16[64,640]{1,0:T(8,128)(2,1)S(1)} collective-permute-done((bf16[64,640]{1,0:T(8,128)(2,1)S(1)}, bf16[64,640]{1,0:T(8,128)(2,1)S(1)}, u32[]{:S(2)}, u32[]{:S(2)}) %collective-permute-start.22) | collective-permute-done | bytes 81952 | tf_op jit(solution)/shard_map/ppermute | solution.py:94
  60.3 1.9 %collective-permute-done.24.refs_4_ = bf16[48,640]{1,0:T(8,128)(2,1)S(1)} collective-permute-done((bf16[48,640]{1,0:T(8,128)(2,1)S(1)}, bf16[48,640]{1,0:T(8,128)(2,1)S(1)}, u32[]{:S(2)}, u32[]{:S(2)}) %collective-permute-start.24) | collective-permute-done | bytes 61472 | tf_op jit(solution)/shard_map/ppermute | solution.py:94
  62.2 0.9 %last.1 = f32[256,640]{1,0:T(8,128)} custom-call(f32[96,640]{1,0:T(8,128)S(1)} %sum_0.1.refs_3_.refs_0_, f32[48,640]{1,0:T(8,128)S(1)} %sum_1.1.refs_3_.refs_1_, f32[64,640]{1,0:T(8,128)S(1)} %sum_2.1.refs_2_.refs_5_, f32[48,640]{1,0:T(8,128)S(1)} %get-tuple-element.85.refs_2_.refs_3_, bf16[48,640]{1,0:T(8,128)(2,1)S(1)} %collective-permute-done.24.refs_4_, ...), custom_call_target="tpu_custom_call" | custom-call | flops 50000000 | bytes 10000 | tf_op jit(solution)/shard_map/last/pallas_call | solution.py:339
  (62 shorter events, 8.2 us)
Async XLA Ops:
  0.0 3.6 %copy-start.1 = (bf16[256,256]{1,0:T(8,128)(2,1)S(1)}, bf16[256,256]{1,0:T(8,128)(2,1)}, u32[]{:S(2)}) copy-start(bf16[256,256]{1,0:T(8,128)(2,1)} %constant.6.clone.refs_4_.refs_3_.refs_0_) | copy-start | bytes 393220
  0.0 3.6 %copy-start.6 = (s32[640]{0:T(1024)S(1)}, s32[640]{0:T(1024)}, u32[]{:S(2)}) copy-start(s32[640]{0:T(1024)} %param.10) | copy-start | bytes 7684
  0.0 3.6 %copy-start.5 = (bf16[128]{0:T(256)(128)(2,1)S(1)}, bf16[128]{0:T(256)(128)(2,1)}, u32[]{:S(2)}) copy-start(bf16[128]{0:T(256)(128)(2,1)} %param.8) | copy-start | bytes 772
  0.0 3.7 %copy-start = (bf16[640,4096]{1,0:T(8,128)(2,1)S(1)}, bf16[640,4096]{1,0:T(8,128)(2,1)}, u32[]{:S(2)}) copy-start(bf16[640,4096]{1,0:T(8,128)(2,1)} %refs_0_.6) | copy-start | bytes 15728644
  0.0 3.7 %copy-start.4 = (s32[512]{0:T(512)S(1)}, s32[512]{0:T(512)}, u32[]{:S(2)}) copy-start(s32[512]{0:T(512)} %param.9) | copy-start | bytes 6148
  1.1 5.6 %collective-permute-start = (bf16[640,128]{1,0:T(8,128)(2,1)S(1)}, bf16[640,128]{1,0:T(8,128)(2,1)S(1)}, u32[]{:S(2)}, u32[]{:S(2)}) collective-permute-start(bf16[640,128]{1,0:T(8,128)(2,1)S(1)} %history.1.refs_5_), channel_id=1, source_target_pairs={{0,2},{2,4},{4,6},{6,8},{8,10},{10,12},{12,14},{14,16},{16,18},{18... | collective-permute-start | bytes 491528 | tf_op jit(solution)/shard_map/ppermute | solution.py:384
  8.5 8.8 %collective-permute-start.1 = (bf16[4,96,256]{2,1,0:T(8,128)(2,1)S(1)}, bf16[4,96,256]{2,1,0:T(8,128)(2,1)S(1)}, u32[]{:S(2)}, u32[]{:S(2)}) collective-permute-start(bf16[4,96,256]{2,1,0:T(8,128)(2,1)S(1)} %get-tuple-element.51.refs_2_.refs_0_), channel_id=1, source_target_pairs={{0,1},{1,0},{2,3},{3,2},{4,5},{5,4},{6,7},{7,6},{8,9},{9,8},{10,11... | collective-permute-start | bytes 589832 | tf_op jit(solution)/shard_map/ppermute | solution.py:94
  11.7 3.4 %collective-permute-start.4 = (bf16[4,64,256]{2,1,0:T(8,128)(2,1)S(1)}, bf16[4,64,256]{2,1,0:T(8,128)(2,1)S(1)}, u32[]{:S(2)}, u32[]{:S(2)}) collective-permute-start(bf16[4,64,256]{2,1,0:T(8,128)(2,1)S(1)} %get-tuple-element.61), channel_id=1, source_target_pairs={{0,2},{2,0},{4,6},{6,4},{8,10},{10,8},{12,14},{14,12},{16,18},{18,... | collective-permute-start | bytes 393224 | tf_op jit(solution)/shard_map/ppermute | solution.py:94
  13.3 1.3 %collective-permute-start.2 = (bf16[4,48,256]{2,1,0:T(8,128)(2,1)S(1)}, bf16[4,48,256]{2,1,0:T(8,128)(2,1)S(1)}, u32[]{:S(2)}, u32[]{:S(2)}) collective-permute-start(bf16[4,48,256]{2,1,0:T(8,128)(2,1)S(1)} %get-tuple-element.59), channel_id=1, source_target_pairs={{0,2},{2,0},{4,6},{6,4},{8,10},{10,8},{12,14},{14,12},{16,18},{18,... | collective-permute-start | bytes 294920 | tf_op jit(solution)/shard_map/ppermute | solution.py:94
  13.3 1.4 %collective-permute-start.3 = (bf16[4,48,256]{2,1,0:T(8,128)(2,1)S(1)}, bf16[4,48,256]{2,1,0:T(8,128)(2,1)S(1)}, u32[]{:S(2)}, u32[]{:S(2)}) collective-permute-start(bf16[4,48,256]{2,1,0:T(8,128)(2,1)S(1)} %get-tuple-element.60), channel_id=1, source_target_pairs={{0,2},{2,0},{4,6},{6,4},{8,10},{10,8},{12,14},{14,12},{16,18},{18,... | collective-permute-start | bytes 294920 | tf_op jit(solution)/shard_map/ppermute | solution.py:94
  13.8 1.3 %collective-permute-start.5 = (bf16[4,48,256]{2,1,0:T(8,128)(2,1)S(1)}, bf16[4,48,256]{2,1,0:T(8,128)(2,1)S(1)}, u32[]{:S(2)}, u32[]{:S(2)}) collective-permute-start(bf16[4,48,256]{2,1,0:T(8,128)(2,1)S(1)} %get-tuple-element.62), channel_id=1, source_target_pairs={{0,2},{2,0},{4,6},{6,4},{8,10},{10,8},{12,14},{14,12},{16,18},{18,... | collective-permute-start | bytes 294920 | tf_op jit(solution)/shard_map/ppermute | solution.py:94
  14.6 4.1 %collective-permute-start.7 = (bf16[4,640,256]{2,1,0:T(8,128)(2,1)S(1)}, bf16[4,640,256]{2,1,0:T(8,128)(2,1)S(1)}, u32[]{:S(2)}, u32[]{:S(2)}) collective-permute-start(bf16[4,640,256]{2,1,0:T(8,128)(2,1)S(1)} %get-tuple-element.53.refs_1_.refs_2_), channel_id=1, source_target_pairs={{0,2},{2,0},{4,6},{6,4},{8,10},{10,8},{12,14},{14,12},{16,18},{18,... | collective-permute-start | bytes 3932168 | tf_op jit(solution)/shard_map/ppermute | solution.py:94
  15.1 8.5 %collective-permute-start.9 = (bf16[2,4,48,256]{3,2,1,0:T(8,128)(2,1)S(1)}, bf16[2,4,48,256]{3,2,1,0:T(8,128)(2,1)S(1)}, u32[]{:S(2)}, u32[]{:S(2)}) collective-permute-start(bf16[2,4,48,256]{3,2,1,0:T(8,128)(2,1)S(1)} %get-tuple-element.63.refs_2_.refs_0_), channel_id=1, source_target_pairs={{0,1},{1,0},{2,3},{3,2},{4,5},{5,4},{6,7},{7,6},{8,9},{9,8},{10,11... | collective-permute-start | bytes 589832 | tf_op jit(solution)/shard_map/ppermute | solution.py:94
  15.7 2.9 %copy-start.2 = (f32[8,128]{1,0:T(8,128)S(1)}, f32[8,128]{1,0:T(8,128)}, u32[]{:S(2)}) copy-start(f32[8,128]{1,0:T(8,128)} %constant.7.clone.refs_4_) | copy-start | bytes 12292
  15.7 2.9 %copy-start.3 = (f32[8,128]{1,0:T(8,128)S(1)}, f32[8,128]{1,0:T(8,128)}, u32[]{:S(2)}) copy-start(f32[8,128]{1,0:T(8,128)} %constant.8.clone.refs_5_) | copy-start | bytes 12292
  15.7 12.8 %collective-permute-start.12 = (bf16[2,4,48,256]{3,2,1,0:T(8,128)(2,1)S(1)}, bf16[2,4,48,256]{3,2,1,0:T(8,128)(2,1)S(1)}, u32[]{:S(2)}, u32[]{:S(2)}) collective-permute-start(bf16[2,4,48,256]{3,2,1,0:T(8,128)(2,1)S(1)} %get-tuple-element.69.refs_0_), channel_id=1, source_target_pairs={{0,1},{1,0},{2,3},{3,2},{4,5},{5,4},{6,7},{7,6},{8,9},{9,8},{10,11... | collective-permute-start | bytes 589832 | tf_op jit(solution)/shard_map/ppermute | solution.py:94
  17.3 1.4 %collective-permute-start.6 = (bf16[4,48,256]{2,1,0:T(8,128)(2,1)S(1)}, bf16[4,48,256]{2,1,0:T(8,128)(2,1)S(1)}, u32[]{:S(2)}, u32[]{:S(2)}) collective-permute-start(bf16[4,48,256]{2,1,0:T(8,128)(2,1)S(1)} %get-tuple-element.65), channel_id=1, source_target_pairs={{0,2},{2,0},{4,6},{6,4},{8,10},{10,8},{12,14},{14,12},{16,18},{18,... | collective-permute-start | bytes 294920 | tf_op jit(solution)/shard_map/ppermute | solution.py:94
  17.4 15.4 %collective-permute-start.11 = (bf16[2,4,64,256]{3,2,1,0:T(8,128)(2,1)S(1)}, bf16[2,4,64,256]{3,2,1,0:T(8,128)(2,1)S(1)}, u32[]{:S(2)}, u32[]{:S(2)}) collective-permute-start(bf16[2,4,64,256]{3,2,1,0:T(8,128)(2,1)S(1)} %get-tuple-element.68.refs_0_), channel_id=1, source_target_pairs={{0,1},{1,0},{2,3},{3,2},{4,5},{5,4},{6,7},{7,6},{8,9},{9,8},{10,11... | collective-permute-start | bytes 786440 | tf_op jit(solution)/shard_map/ppermute | solution.py:94
  19.7 10.6 %collective-permute-start.8 = (bf16[192,640]{1,0:T(8,128)(2,1)S(1)}, bf16[192,640]{1,0:T(8,128)(2,1)S(1)}, u32[]{:S(2)}, u32[]{:S(2)}) collective-permute-start(bf16[192,640]{1,0:T(8,128)(2,1)S(1)} %send_0.1.refs_7_), channel_id=1, source_target_pairs={{0,8},{2,10},{4,12},{6,14},{8,0},{10,2},{12,4},{14,6},{16,24},{18,... | collective-permute-start | bytes 737288 | tf_op jit(solution)/shard_map/ppermute | solution.py:94
  24.7 12.3 %collective-permute-start.10 = (bf16[192,640]{1,0:T(8,128)(2,1)S(1)}, bf16[192,640]{1,0:T(8,128)(2,1)S(1)}, u32[]{:S(2)}, u32[]{:S(2)}) collective-permute-start(bf16[192,640]{1,0:T(8,128)(2,1)S(1)} %send_1.1.refs_6_), channel_id=1, source_target_pairs={{0,8},{2,10},{4,12},{6,14},{8,0},{10,2},{12,4},{14,6},{16,24},{18,... | collective-permute-start | bytes 737288 | tf_op jit(solution)/shard_map/ppermute | solution.py:94
  27.0 12.1 %collective-permute-start.15 = (bf16[2,4,48,256]{3,2,1,0:T(8,128)(2,1)S(1)}, bf16[2,4,48,256]{3,2,1,0:T(8,128)(2,1)S(1)}, u32[]{:S(2)}, u32[]{:S(2)}) collective-permute-start(bf16[2,4,48,256]{3,2,1,0:T(8,128)(2,1)S(1)} %get-tuple-element.72.refs_0_), channel_id=1, source_target_pairs={{0,1},{1,0},{2,3},{3,2},{4,5},{5,4},{6,7},{7,6},{8,9},{9,8},{10,11... | collective-permute-start | bytes 589832 | tf_op jit(solution)/shard_map/ppermute | solution.py:94
  29.5 12.1 %collective-permute-start.14 = (bf16[192,640]{1,0:T(8,128)(2,1)S(1)}, bf16[192,640]{1,0:T(8,128)(2,1)S(1)}, u32[]{:S(2)}, u32[]{:S(2)}) collective-permute-start(bf16[192,640]{1,0:T(8,128)(2,1)S(1)} %send_2.1.refs_7_), channel_id=1, source_target_pairs={{0,4},{2,6},{4,0},{6,2},{8,12},{10,14},{12,8},{14,10},{16,20},{18,... | collective-permute-start | bytes 737288 | tf_op jit(solution)/shard_map/ppermute | solution.py:94
  34.0 14.7 %collective-permute-start.17 = (bf16[256,640]{1,0:T(8,128)(2,1)S(1)}, bf16[256,640]{1,0:T(8,128)(2,1)S(1)}, u32[]{:S(2)}, u32[]{:S(2)}) collective-permute-start(bf16[256,640]{1,0:T(8,128)(2,1)S(1)} %send_3.1.refs_4_), channel_id=1, source_target_pairs={{0,8},{2,10},{4,12},{6,14},{8,0},{10,2},{12,4},{14,6},{16,24},{18,... | collective-permute-start | bytes 983048 | tf_op jit(solution)/shard_map/ppermute | solution.py:94
  37.1 9.0 %collective-permute-start.13 = (bf16[192,640]{1,0:T(8,128)(2,1)S(1)}, bf16[192,640]{1,0:T(8,128)(2,1)S(1)}, u32[]{:S(2)}, u32[]{:S(2)}) collective-permute-start(bf16[192,640]{1,0:T(8,128)(2,1)S(1)} %get-tuple-element.71), channel_id=1, source_target_pairs={{0,4},{2,6},{4,0},{6,2},{8,12},{10,14},{12,8},{14,10},{16,20},{18,... | collective-permute-start | bytes 737288 | tf_op jit(solution)/shard_map/ppermute | solution.py:94
  40.1 10.6 %collective-permute-start.18 = (bf16[192,640]{1,0:T(8,128)(2,1)S(1)}, bf16[192,640]{1,0:T(8,128)(2,1)S(1)}, u32[]{:S(2)}, u32[]{:S(2)}) collective-permute-start(bf16[192,640]{1,0:T(8,128)(2,1)S(1)} %send_4.1.refs_2_), channel_id=1, source_target_pairs={{0,4},{2,6},{4,0},{6,2},{8,12},{10,14},{12,8},{14,10},{16,20},{18,... | collective-permute-start | bytes 737288 | tf_op jit(solution)/shard_map/ppermute | solution.py:94
  41.6 8.2 %collective-permute-start.19 = (bf16[96,640]{1,0:T(8,128)(2,1)S(1)}, bf16[96,640]{1,0:T(8,128)(2,1)S(1)}, u32[]{:S(2)}, u32[]{:S(2)}) collective-permute-start(bf16[96,640]{1,0:T(8,128)(2,1)S(1)} %get-tuple-element.77), channel_id=1, source_target_pairs={{0,8},{2,10},{4,12},{6,14},{8,0},{10,2},{12,4},{14,6},{16,24},{18,... | collective-permute-start | bytes 368648 | tf_op jit(solution)/shard_map/ppermute | solution.py:94
  46.1 7.4 %collective-permute-start.16 = (bf16[96,640]{1,0:T(8,128)(2,1)S(1)}, bf16[96,640]{1,0:T(8,128)(2,1)S(1)}, u32[]{:S(2)}, u32[]{:S(2)}) collective-permute-start(bf16[96,640]{1,0:T(8,128)(2,1)S(1)} %get-tuple-element.75), channel_id=1, source_target_pairs={{0,16},{2,18},{4,20},{6,22},{8,24},{10,26},{12,28},{14,30},{16,0},... | collective-permute-start | bytes 368648 | tf_op jit(solution)/shard_map/ppermute | solution.py:94
  48.8 5.4 %collective-permute-start.21 = (bf16[128,640]{1,0:T(8,128)(2,1)S(1)}, bf16[128,640]{1,0:T(8,128)(2,1)S(1)}, u32[]{:S(2)}, u32[]{:S(2)}) collective-permute-start(bf16[128,640]{1,0:T(8,128)(2,1)S(1)} %get-tuple-element.81), channel_id=1, source_target_pairs={{0,4},{2,6},{4,0},{6,2},{8,12},{10,14},{12,8},{14,10},{16,20},{18,... | collective-permute-start | bytes 491528 | tf_op jit(solution)/shard_map/ppermute | solution.py:94
  49.9 7.0 %collective-permute-start.20 = (bf16[48,640]{1,0:T(8,128)(2,1)S(1)}, bf16[48,640]{1,0:T(8,128)(2,1)S(1)}, u32[]{:S(2)}, u32[]{:S(2)}) collective-permute-start(bf16[48,640]{1,0:T(8,128)(2,1)S(1)} %get-tuple-element.80), channel_id=1, source_target_pairs={{0,16},{2,18},{4,20},{6,22},{8,24},{10,26},{12,28},{14,30},{16,0},... | collective-permute-start | bytes 184328 | tf_op jit(solution)/shard_map/ppermute | solution.py:94
  50.7 6.2 %collective-permute-start.23 = (bf16[96,640]{1,0:T(8,128)(2,1)S(1)}, bf16[96,640]{1,0:T(8,128)(2,1)S(1)}, u32[]{:S(2)}, u32[]{:S(2)}) collective-permute-start(bf16[96,640]{1,0:T(8,128)(2,1)S(1)} %get-tuple-element.84), channel_id=1, source_target_pairs={{0,8},{2,10},{4,12},{6,14},{8,0},{10,2},{12,4},{14,6},{16,24},{18,... | collective-permute-start | bytes 368648 | tf_op jit(solution)/shard_map/ppermute | solution.py:94
  54.2 6.1 %collective-permute-start.22 = (bf16[64,640]{1,0:T(8,128)(2,1)S(1)}, bf16[64,640]{1,0:T(8,128)(2,1)S(1)}, u32[]{:S(2)}, u32[]{:S(2)}) collective-permute-start(bf16[64,640]{1,0:T(8,128)(2,1)S(1)} %get-tuple-element.83), channel_id=1, source_target_pairs={{0,16},{2,18},{4,20},{6,22},{8,24},{10,26},{12,28},{14,30},{16,0},... | collective-permute-start | bytes 245768 | tf_op jit(solution)/shard_map/ppermute | solution.py:94
  57.0 5.2 %collective-permute-start.24 = (bf16[48,640]{1,0:T(8,128)(2,1)S(1)}, bf16[48,640]{1,0:T(8,128)(2,1)S(1)}, u32[]{:S(2)}, u32[]{:S(2)}) collective-permute-start(bf16[48,640]{1,0:T(8,128)(2,1)S(1)} %get-tuple-element.86), channel_id=1, source_target_pairs={{0,16},{2,18},{4,20},{6,22},{8,24},{10,26},{12,28},{14,30},{16,0},... | collective-permute-start | bytes 184328 | tf_op jit(solution)/shard_map/ppermute | solution.py:94

commit v6 on v5

--- a/solution.py
+++ b/solution.py
@@ -139,7 +139,7 @@
     band_ref[...] = jnp.where(apart <= HW, 1.0, 0.0).astype(jnp.bfloat16)
 
 
-def fill_selector(sizes, orders, sources_ref, select_ref):
+def fill_selector(sizes, orders, chunks, sources_ref, select_ref):
     rows = select_ref.shape[1]
     me = lax.axis_index("tm")
     first_chan = lax.axis_index("chan") * rows
@@ -147,7 +147,10 @@
     codes = 1 << len(orders[0])
     channels = sources_ref[...].astype(jnp.float32)
     begin, row = 0, 0
-    for size, bits in zip(sizes, orders):
+    for chunk, (size, bits) in enumerate(zip(sizes, orders)):
+        if chunk not in chunks:
+            begin += size
+            continue
         count = 2 * codes * size
         index = lax.broadcasted_iota(jnp.int32, (count, VS), 0)
         scale = (1 << 16) // size + 1
@@ -187,7 +190,7 @@
     fill_fir(taps_ref, fir_ref)
     fill_alive(dead_ref, alive_ref)
     fill_band(band_ref)
-    fill_selector(sizes, orders, sources_ref, select_ref)
+    fill_selector(sizes, orders, (0,), sources_ref, select_ref)
     samples = jnp.concatenate(
         [raw_ref[:, w * SPAN - TAPS : (w + 1) * SPAN] for w in range(1, windows + 1)], axis=0
     )
@@ -208,15 +211,17 @@
     samples = jnp.concatenate([hist_ref[...], raw_ref[:, :SPAN]], axis=1)
     dec = nt_dot(samples, fir_ref[...]).astype(jnp.bfloat16)
     white_ref[0] = whiten(dec, table_ref, band_ref, alive_ref[...])
-    select = select_ref[: panel_ref.shape[1]]
+    select = select_ref[...]
     for w in range(white_ref.shape[0]):
         panel_ref[w] = pick(select, white_ref[w])
 
 
-def panels_kernel(skip, groups, select_ref, white_ref, *refs):
+def panels_kernel(sizes, orders, groups, sources_ref, white_ref, *refs):
+    *refs, select_ref = refs
+    fill_selector(sizes, orders, range(1, len(sizes)), sources_ref, select_ref)
     own_refs, other_refs = refs[: len(groups)], refs[len(groups) :]
     for w in range(white_ref.shape[0]):
-        chosen = pick(select_ref[skip:], white_ref[w])
+        chosen = pick(select_ref[...], white_ref[w])
         row = 0
         for group, own_ref, other_ref in zip(groups, own_refs, other_refs):
             place = 0
@@ -393,7 +398,7 @@
             shape((TD, SPAN + TAPS), bf16),
             shape((rows, HALF), f32),
             shape((TD, HALF), bf16),
-            shape((VS, rows), bf16),
+            shape((2 * counts[0], rows), bf16),
         ],
     )
     panel, white = chain(
@@ -406,7 +411,13 @@
     white_sib = swap(white, "tm", 1)
     members = [[counts[chunk] for chunk in group] for group in across_groups]
     rest = [shape((windows, sum(group), TD), bf16) for group in members]
-    parts = chain("panels", functools.partial(panels_kernel, 2 * counts[0], members), [select, white], rest + rest)
+    parts = chain(
+        "panels",
+        functools.partial(panels_kernel, sizes, orders, members),
+        [sources.reshape(1, -1), white],
+        rest + rest,
+        [pltpu.VMEM((VS - 2 * counts[0], rows), bf16)],
+    )
     own, sib = parts[: len(rest)], [swap(other, "tm", 1) for other in parts[len(rest) :]]
     tables = [jnp.asarray(t) for t in lag_tables(1.0 / math.sqrt(time_parts * windows * TD))]
     spectra = [white, white_sib, *tables]

time: 63.4 us -> 63.7 us (level)
  transfers between devices with their start and end apart: 25 -> 25, of which waited for: 11 -> 11; matrix products, arithmetic and copies ran while one was open for 0% -> 0% of each run, Pallas kernels for 24% -> 23%
where the time goes in v6:
time: 63.7 us; the launch traced here: 63.5 us
  starting transfers between devices  30.7 us (48%)
  Pallas kernels  18.6 us (29%)
  waiting for transfers between devices  13.7 us (22%)
    ppermute x24, starting transfers between devices, swap(): lax.ppermute(value, axis, [(i, i ^ bit) for i in range(lax.axis_size(axis...  28.2 us
    pallas_call x29, Pallas kernels, __call__(): pl.pallas_call(body, out_shape=[*outs, *(jax.ShapeDtypeStruct(g.shape, g....  18.6 us
    ppermute x24, waiting for transfers between devices, swap(): lax.ppermute(value, axis, [(i, i ^ bit) for i in range(lax.axis_size(axis...  13.7 us
    ppermute x1, starting transfers between devices, local(): lax.ppermute(tail, 'tm', [(i, i + 1) for i in range(time_parts - 1)])  2.51 us
  transfers between devices with their start and end apart: 25, of which 11 were waited for; matrix products, arithmetic and copies ran while one was open for 0% of the time, Pallas kernels for 23%

profile of v6, /device:TPU:0, one launch (start us, length us, event | category | flops | bytes accessed | tf_op | source)
XLA Modules:
  0.0 63.5 jit_solution(4995161465487559672)
XLA Ops:
  0.0 1.1 %history.1.refs_5_ = bf16[640,128]{1,0:T(8,128)(2,1)S(1)} custom-call(bf16[640,4096]{1,0:T(8,128)(2,1)} %refs_0_.6), custom_call_target="tpu_custom_call" | custom-call | flops 50000000 | bytes 10000 | tf_op jit(solution)/shard_map/history/pallas_call | solution.py:344
  1.1 2.5 %collective-permute-start = (bf16[640,128]{1,0:T(8,128)(2,1)S(1)}, bf16[640,128]{1,0:T(8,128)(2,1)S(1)}, u32[]{:S(2)}, u32[]{:S(2)}) collective-permute-start(bf16[640,128]{1,0:T(8,128)(2,1)S(1)} %history.1.refs_5_), channel_id=1, source_target_pairs={{0,2},{2,4},{4,6},{6,8},{8,10},{10,12},{12,14},{14,16},{16,18},{18... | collective-permute-start | bytes 491528 | tf_op jit(solution)/shard_map/ppermute | solution.py:389
  3.7 2.8 %late.1 = (bf16[3,640,256]{2,1,0:T(8,128)(2,1)S(1)}, bf16[256,1152]{1,0:T(8,128)(2,1)S(1)}, f32[640,128]{1,0:T(8,128)S(1)}, bf16[256,128]{1,0:T(8,128)(2,1)S(1)}, bf16[96,640]{1,0:T(8,128)(2,1)S(1)}) custom-call(bf16[640,4096]{1,0:T(8,128)(2,1)S(1)} %copy-done, bf16[1,128]{1,0:T(2,128)(2,1)S(1)} %bitcast.5, s32[1,640]{1,0:T(1,128)S(1)} %reshape.14.refs_2_, ...), custom_call_target="tpu_custom_call" | custom-call | flops 50000000 | bytes 10000 | tf_op jit(solution)/shard_map/late/pallas_call | solution.py:344
  6.5 1.8 %first.1 = (bf16[4,96,256]{2,1,0:T(8,128)(2,1)S(1)}, bf16[4,640,256]{2,1,0:T(8,128)(2,1)S(1)}) custom-call(bf16[640,4096]{1,0:T(8,128)(2,1)S(1)} %copy-done, bf16[640,128]{1,0:T(8,128)(2,1)S(1)} %collective-permute-done.refs_1_, bf16[256,1152]{1,0:T(8,128)(2,1)S(1)} %get-tuple-element.46.refs_2_, bf16[256,256]{1,0:T(8,128)(2,1)S(1)} %copy-done.1, ...), custom_call_target="tpu_custom_call" | custom-call | flops 500000000 | bytes 10000 | tf_op jit(solution)/shard_map/first/pallas_call | solution.py:344
  8.2 2.4 %collective-permute-start.1 = (bf16[4,96,256]{2,1,0:T(8,128)(2,1)S(1)}, bf16[4,96,256]{2,1,0:T(8,128)(2,1)S(1)}, u32[]{:S(2)}, u32[]{:S(2)}) collective-permute-start(bf16[4,96,256]{2,1,0:T(8,128)(2,1)S(1)} %get-tuple-element.51.refs_2_.refs_0_), channel_id=1, source_target_pairs={{0,1},{1,0},{2,3},{3,2},{4,5},{5,4},{6,7},{7,6},{8,9},{9,8},{10,11... | collective-permute-start | bytes 589832 | tf_op jit(solution)/shard_map/ppermute | solution.py:94
  10.7 1.0 %panels.1 = (bf16[4,48,256]{2,1,0:T(8,128)(2,1)S(1)}, bf16[4,48,256]{2,1,0:T(8,128)(2,1)S(1)}, bf16[4,64,256]{2,1,0:T(8,128)(2,1)S(1)}, bf16[4,48,256]{2,1,0:T(8...) custom-call(s32[1,512]{1,0:T(1,128)S(1)} %bitcast.4, ...), custom_call_target="tpu_custom_call" | custom-call | flops 50000000 | bytes 10000 | tf_op jit(solution)/shard_map/panels/pallas_call | solution.py:344
  11.7 1.6 %collective-permute-start.4 = (bf16[4,64,256]{2,1,0:T(8,128)(2,1)S(1)}, bf16[4,64,256]{2,1,0:T(8,128)(2,1)S(1)}, u32[]{:S(2)}, u32[]{:S(2)}) collective-permute-start(bf16[4,64,256]{2,1,0:T(8,128)(2,1)S(1)} %get-tuple-element.61), channel_id=1, source_target_pairs={{0,2},{2,0},{4,6},{6,4},{8,10},{10,8},{12,14},{14,12},{16,18},{18,... | collective-permute-start | bytes 393224 | tf_op jit(solution)/shard_map/ppermute | solution.py:94
  15.7 1.5 %collective-permute-start.12 = (bf16[2,4,48,256]{3,2,1,0:T(8,128)(2,1)S(1)}, bf16[2,4,48,256]{3,2,1,0:T(8,128)(2,1)S(1)}, u32[]{:S(2)}, u32[]{:S(2)}) collective-permute-start(bf16[2,4,48,256]{3,2,1,0:T(8,128)(2,1)S(1)} %get-tuple-element.69.refs_0_), channel_id=1, source_target_pairs={{0,1},{1,0},{2,3},{3,2},{4,5},{5,4},{6,7},{7,6},{8,9},{9,8},{10,11... | collective-permute-start | bytes 589832 | tf_op jit(solution)/shard_map/ppermute | solution.py:94
  17.3 1.0 %collective-permute-start.11 = (bf16[2,4,64,256]{3,2,1,0:T(8,128)(2,1)S(1)}, bf16[2,4,64,256]{3,2,1,0:T(8,128)(2,1)S(1)}, u32[]{:S(2)}, u32[]{:S(2)}) collective-permute-start(bf16[2,4,64,256]{3,2,1,0:T(8,128)(2,1)S(1)} %get-tuple-element.68.refs_0_), channel_id=1, source_target_pairs={{0,1},{1,0},{2,3},{3,2},{4,5},{5,4},{6,7},{7,6},{8,9},{9,8},{10,11... | collective-permute-start | bytes 786440 | tf_op jit(solution)/shard_map/ppermute | solution.py:94
  18.6 1.0 %send_0.1.refs_7_ = bf16[192,640]{1,0:T(8,128)(2,1)S(1)} custom-call(bf16[4,48,256]{2,1,0:T(8,128)(2,1)S(1)} %get-tuple-element.64.refs_0_.refs_6_, bf16[4,48,256]{2,1,0:T(8,128)(2,1)S(1)} %collective-permute-done.6.refs_1_, bf16[4,640,256]{2,1,0:T(8,128)(2,1)S(1)} %get-tuple-element.53.refs_1_.refs_2_, ...), custom_call_target="tpu_custom_call" | custom-call | flops 500000000 | bytes 10000 | tf_op jit(solution)/shard_map/send_0/pallas_call | solution.py:344
  19.7 3.2 %collective-permute-start.8 = (bf16[192,640]{1,0:T(8,128)(2,1)S(1)}, bf16[192,640]{1,0:T(8,128)(2,1)S(1)}, u32[]{:S(2)}, u32[]{:S(2)}) collective-permute-start(bf16[192,640]{1,0:T(8,128)(2,1)S(1)} %send_0.1.refs_7_), channel_id=1, source_target_pairs={{0,8},{2,10},{4,12},{6,14},{8,0},{10,2},{12,4},{14,6},{16,24},{18,... | collective-permute-start | bytes 737288 | tf_op jit(solution)/shard_map/ppermute | solution.py:94
  22.9 1.0 %keep_0.1 = (f32[192,640]{1,0:T(8,128)S(1)}, bf16[2,4,48,256]{3,2,1,0:T(8,128)(2,1)S(1)}) custom-call(bf16[4,48,256]{2,1,0:T(8,128)(2,1)S(1)} %get-tuple-element.64.refs_0_.refs_6_, bf16[4,48,256]{2,1,0:T(8,128)(2,1)S(1)} %collective-permute-done.6.refs_1_, ...), custom_call_target="tpu_custom_call", output_to_operand_aliasing={{1}: (6, {})} | custom-call | flops 182000000 | bytes 10000 | tf_op jit(solution)/shard_map/keep_0/pallas_call | solution.py:344
  23.9 1.0 %send_1.1.refs_6_ = bf16[192,640]{1,0:T(8,128)(2,1)S(1)} custom-call(bf16[2,4,48,256]{3,2,1,0:T(8,128)(2,1)S(1)} %get-tuple-element.63.refs_2_.refs_0_, bf16[2,4,48,256]{3,2,1,0:T(8,128)(2,1)S(1)} %collective-permute-done.9.refs_1_, bf16[4,640,256]{2,1,0:T(8,128)(2,1)S(1)} %get-tuple-element.53.refs_1_.refs_2_, ...), custom_call_target="tpu_custom_call" | custom-call | flops 50000000 | bytes 10000 | tf_op jit(solution)/shard_map/send_1/pallas_call | solution.py:344
  24.9 2.2 %collective-permute-start.10 = (bf16[192,640]{1,0:T(8,128)(2,1)S(1)}, bf16[192,640]{1,0:T(8,128)(2,1)S(1)}, u32[]{:S(2)}, u32[]{:S(2)}) collective-permute-start(bf16[192,640]{1,0:T(8,128)(2,1)S(1)} %send_1.1.refs_6_), channel_id=1, source_target_pairs={{0,8},{2,10},{4,12},{6,14},{8,0},{10,2},{12,4},{14,6},{16,24},{18,... | collective-permute-start | bytes 737288 | tf_op jit(solution)/shard_map/ppermute | solution.py:94
  27.7 1.0 %keep_1.1.refs_7_.refs_2_ = f32[192,640]{1,0:T(8,128)S(1)} custom-call(bf16[2,4,48,256]{3,2,1,0:T(8,128)(2,1)S(1)} %get-tuple-element.63.refs_2_.refs_0_, bf16[2,4,48,256]{3,2,1,0:T(8,128)(2,1)S(1)} %collective-permute-done.9.refs_1_, bf16[4,640,256]{2,1,0:T(8,128)(2,1)S(1)} %get-tuple-element.53.refs_1_.refs_2_, ...), custom_call_target="tpu_custom_call" | custom-call | flops 50000000 | bytes 10000 | tf_op jit(solution)/shard_map/keep_1/pallas_call | solution.py:344
  28.7 1.0 %send_2.1.refs_7_ = bf16[192,640]{1,0:T(8,128)(2,1)S(1)} custom-call(bf16[2,4,48,256]{3,2,1,0:T(8,128)(2,1)S(1)} %get-tuple-element.69.refs_0_, bf16[2,4,48,256]{3,2,1,0:T(8,128)(2,1)S(1)} %collective-permute-done.12.refs_1_.refs_6_, bf16[4,640,256]{2,1,0:T(8,128)(2,1)S(1)} %get-tuple-element.53.refs_1_.refs_2_, ...), custom_call_target="tpu_custom_call" | custom-call | flops 15000000512 | bytes 10000 | tf_op jit(solution)/shard_map/send_2/pallas_call | solution.py:344
  30.4 1.0 %keep_2.1.refs_7_.refs_0_ = f32[192,640]{1,0:T(8,128)S(1)} custom-call(bf16[2,4,48,256]{3,2,1,0:T(8,128)(2,1)S(1)} %get-tuple-element.69.refs_0_, bf16[2,4,48,256]{3,2,1,0:T(8,128)(2,1)S(1)} %collective-permute-done.12.refs_1_.refs_6_, bf16[4,640,256]{2,1,0:T(8,128)(2,1)S(1)} %get-tuple-element.53.refs_1_.refs_2_, ...), custom_call_target="tpu_custom_call" | custom-call | flops 347000000 | bytes 10000 | tf_op jit(solution)/shard_map/keep_2/pallas_call | solution.py:344
  31.4 1.4 %collective-permute-done.11.refs_1_.refs_6_ = bf16[2,4,64,256]{3,2,1,0:T(8,128)(2,1)S(1)} collective-permute-done((bf16[2,4,64,256]{3,2,1,0:T(8,128)(2,1)S(1)}, bf16[2,4,64,256]{3,2,1,0:T(8,128)(2,1)S(1)}, u32[]{:S(2)}, u32[]{:S(2)}) %collective-permute-start.11) | collective-permute-done | bytes 262176 | tf_op jit(solution)/shard_map/ppermute | solution.py:94
  32.8 1.2 %send_3.1.refs_4_ = bf16[256,640]{1,0:T(8,128)(2,1)S(1)} custom-call(bf16[2,4,64,256]{3,2,1,0:T(8,128)(2,1)S(1)} %get-tuple-element.68.refs_0_, bf16[2,4,64,256]{3,2,1,0:T(8,128)(2,1)S(1)} %collective-permute-done.11.refs_1_.refs_6_, bf16[4,640,256]{2,1,0:T(8,128)(2,1)S(1)} %get-tuple-element.53.refs_1_.refs_2_, ...), custom_call_target="tpu_custom_call" | custom-call | flops 277000000 | bytes 10000 | tf_op jit(solution)/shard_map/send_3/pallas_call | solution.py:344
  34.0 3.2 %collective-permute-start.17 = (bf16[256,640]{1,0:T(8,128)(2,1)S(1)}, bf16[256,640]{1,0:T(8,128)(2,1)S(1)}, u32[]{:S(2)}, u32[]{:S(2)}) collective-permute-start(bf16[256,640]{1,0:T(8,128)(2,1)S(1)} %send_3.1.refs_4_), channel_id=1, source_target_pairs={{0,8},{2,10},{4,12},{6,14},{8,0},{10,2},{12,4},{14,6},{16,24},{18,... | collective-permute-start | bytes 983048 | tf_op jit(solution)/shard_map/ppermute | solution.py:94
  37.9 1.4 %keep_3.1.refs_7_.refs_0_ = f32[256,640]{1,0:T(8,128)S(1)} custom-call(bf16[2,4,64,256]{3,2,1,0:T(8,128)(2,1)S(1)} %get-tuple-element.68.refs_0_, bf16[2,4,64,256]{3,2,1,0:T(8,128)(2,1)S(1)} %collective-permute-done.11.refs_1_.refs_6_, bf16[4,640,256]{2,1,0:T(8,128)(2,1)S(1)} %get-tuple-element.53.refs_1_.refs_2_, ...), custom_call_target="tpu_custom_call" | custom-call | flops 112000000 | bytes 10000 | tf_op jit(solution)/shard_map/keep_3/pallas_call | solution.py:344
  39.3 1.0 %send_4.1.refs_2_ = bf16[192,640]{1,0:T(8,128)(2,1)S(1)} custom-call(bf16[2,4,48,256]{3,2,1,0:T(8,128)(2,1)S(1)} %get-tuple-element.72.refs_0_, bf16[2,4,48,256]{3,2,1,0:T(8,128)(2,1)S(1)} %collective-permute-done.15.refs_1_.refs_6_, bf16[4,640,256]{2,1,0:T(8,128)(2,1)S(1)} %get-tuple-element.53.refs_1_.refs_2_, ...), custom_call_target="tpu_custom_call" | custom-call | flops 275000000 | bytes 10000 | tf_op jit(solution)/shard_map/send_4/pallas_call | solution.py:344
  40.3 1.5 %collective-permute-start.18 = (bf16[192,640]{1,0:T(8,128)(2,1)S(1)}, bf16[192,640]{1,0:T(8,128)(2,1)S(1)}, u32[]{:S(2)}, u32[]{:S(2)}) collective-permute-start(bf16[192,640]{1,0:T(8,128)(2,1)S(1)} %send_4.1.refs_2_), channel_id=1, source_target_pairs={{0,4},{2,6},{4,0},{6,2},{8,12},{10,14},{12,8},{14,10},{16,20},{18,... | collective-permute-start | bytes 737288 | tf_op jit(solution)/shard_map/ppermute | solution.py:94
  41.9 4.3 %collective-permute-done.13.refs_1_.refs_3_ = bf16[192,640]{1,0:T(8,128)(2,1)S(1)} collective-permute-done((bf16[192,640]{1,0:T(8,128)(2,1)S(1)}, bf16[192,640]{1,0:T(8,128)(2,1)S(1)}, u32[]{:S(2)}, u32[]{:S(2)}) %collective-permute-start.13) | collective-permute-done | bytes 245792 | tf_op jit(solution)/shard_map/ppermute | solution.py:94
  46.3 2.7 %collective-permute-start.16 = (bf16[96,640]{1,0:T(8,128)(2,1)S(1)}, bf16[96,640]{1,0:T(8,128)(2,1)S(1)}, u32[]{:S(2)}, u32[]{:S(2)}) collective-permute-start(bf16[96,640]{1,0:T(8,128)(2,1)S(1)} %get-tuple-element.75), channel_id=1, source_target_pairs={{0,16},{2,18},{4,20},{6,22},{8,24},{10,26},{12,28},{14,30},{16,0},... | collective-permute-start | bytes 368648 | tf_op jit(solution)/shard_map/ppermute | solution.py:94
  49.1 1.0 %keep_4.1.refs_3_.refs_0_ = f32[192,640]{1,0:T(8,128)S(1)} custom-call(bf16[2,4,48,256]{3,2,1,0:T(8,128)(2,1)S(1)} %get-tuple-element.72.refs_0_, bf16[2,4,48,256]{3,2,1,0:T(8,128)(2,1)S(1)} %collective-permute-done.15.refs_1_.refs_6_, bf16[4,640,256]{2,1,0:T(8,128)(2,1)S(1)} %get-tuple-element.53.refs_1_.refs_2_, ...), custom_call_target="tpu_custom_call" | custom-call | flops 110000000 | bytes 10000 | tf_op jit(solution)/shard_map/keep_4/pallas_call | solution.py:344
  51.0 2.0 %collective-permute-start.23 = (bf16[96,640]{1,0:T(8,128)(2,1)S(1)}, bf16[96,640]{1,0:T(8,128)(2,1)S(1)}, u32[]{:S(2)}, u32[]{:S(2)}) collective-permute-start(bf16[96,640]{1,0:T(8,128)(2,1)S(1)} %get-tuple-element.84), channel_id=1, source_target_pairs={{0,8},{2,10},{4,12},{6,14},{8,0},{10,2},{12,4},{14,6},{16,24},{18,... | collective-permute-start | bytes 368648 | tf_op jit(solution)/shard_map/ppermute | solution.py:94
  54.4 1.4 %collective-permute-start.22 = (bf16[64,640]{1,0:T(8,128)(2,1)S(1)}, bf16[64,640]{1,0:T(8,128)(2,1)S(1)}, u32[]{:S(2)}, u32[]{:S(2)}) collective-permute-start(bf16[64,640]{1,0:T(8,128)(2,1)S(1)} %get-tuple-element.83), channel_id=1, source_target_pairs={{0,16},{2,18},{4,20},{6,22},{8,24},{10,26},{12,28},{14,30},{16,0},... | collective-permute-start | bytes 245768 | tf_op jit(solution)/shard_map/ppermute | solution.py:94
  55.9 1.3 %collective-permute-done.20.refs_1_.refs_2_ = bf16[48,640]{1,0:T(8,128)(2,1)S(1)} collective-permute-done((bf16[48,640]{1,0:T(8,128)(2,1)S(1)}, bf16[48,640]{1,0:T(8,128)(2,1)S(1)}, u32[]{:S(2)}, u32[]{:S(2)}) %collective-permute-start.20) | collective-permute-done | bytes 61472 | tf_op jit(solution)/shard_map/ppermute | solution.py:94
  57.3 1.3 %collective-permute-start.24 = (bf16[48,640]{1,0:T(8,128)(2,1)S(1)}, bf16[48,640]{1,0:T(8,128)(2,1)S(1)}, u32[]{:S(2)}, u32[]{:S(2)}) collective-permute-start(bf16[48,640]{1,0:T(8,128)(2,1)S(1)} %get-tuple-element.86), channel_id=1, source_target_pairs={{0,16},{2,18},{4,20},{6,22},{8,24},{10,26},{12,28},{14,30},{16,0},... | collective-permute-start | bytes 184328 | tf_op jit(solution)/shard_map/ppermute | solution.py:94
  58.6 1.9 %collective-permute-done.22.refs_1_ = bf16[64,640]{1,0:T(8,128)(2,1)S(1)} collective-permute-done((bf16[64,640]{1,0:T(8,128)(2,1)S(1)}, bf16[64,640]{1,0:T(8,128)(2,1)S(1)}, u32[]{:S(2)}, u32[]{:S(2)}) %collective-permute-start.22) | collective-permute-done | bytes 81952 | tf_op jit(solution)/shard_map/ppermute | solution.py:94
  60.5 1.9 %collective-permute-done.24.refs_4_ = bf16[48,640]{1,0:T(8,128)(2,1)S(1)} collective-permute-done((bf16[48,640]{1,0:T(8,128)(2,1)S(1)}, bf16[48,640]{1,0:T(8,128)(2,1)S(1)}, u32[]{:S(2)}, u32[]{:S(2)}) %collective-permute-start.24) | collective-permute-done | bytes 61472 | tf_op jit(solution)/shard_map/ppermute | solution.py:94
  (62 shorter events, 8.4 us)
Async XLA Ops:
  0.0 3.6 %copy-start.1 = (bf16[256,256]{1,0:T(8,128)(2,1)S(1)}, bf16[256,256]{1,0:T(8,128)(2,1)}, u32[]{:S(2)}) copy-start(bf16[256,256]{1,0:T(8,128)(2,1)} %constant.6.clone.refs_4_.refs_3_.refs_0_) | copy-start | bytes 393220
  0.0 3.6 %copy-start.6 = (s32[640]{0:T(1024)S(1)}, s32[640]{0:T(1024)}, u32[]{:S(2)}) copy-start(s32[640]{0:T(1024)} %param.10) | copy-start | bytes 7684
  0.0 3.6 %copy-start.4 = (s32[512]{0:T(512)S(1)}, s32[512]{0:T(512)}, u32[]{:S(2)}) copy-start(s32[512]{0:T(512)} %param.9) | copy-start | bytes 6148
  0.0 3.7 %copy-start = (bf16[640,4096]{1,0:T(8,128)(2,1)S(1)}, bf16[640,4096]{1,0:T(8,128)(2,1)}, u32[]{:S(2)}) copy-start(bf16[640,4096]{1,0:T(8,128)(2,1)} %refs_0_.6) | copy-start | bytes 15728644
  0.0 3.7 %copy-start.5 = (bf16[128]{0:T(256)(128)(2,1)S(1)}, bf16[128]{0:T(256)(128)(2,1)}, u32[]{:S(2)}) copy-start(bf16[128]{0:T(256)(128)(2,1)} %param.8) | copy-start | bytes 772
  1.1 5.4 %collective-permute-start = (bf16[640,128]{1,0:T(8,128)(2,1)S(1)}, bf16[640,128]{1,0:T(8,128)(2,1)S(1)}, u32[]{:S(2)}, u32[]{:S(2)}) collective-permute-start(bf16[640,128]{1,0:T(8,128)(2,1)S(1)} %history.1.refs_5_), channel_id=1, source_target_pairs={{0,2},{2,4},{4,6},{6,8},{8,10},{10,12},{12,14},{14,16},{16,18},{18... | collective-permute-start | bytes 491528 | tf_op jit(solution)/shard_map/ppermute | solution.py:389
  8.2 9.0 %collective-permute-start.1 = (bf16[4,96,256]{2,1,0:T(8,128)(2,1)S(1)}, bf16[4,96,256]{2,1,0:T(8,128)(2,1)S(1)}, u32[]{:S(2)}, u32[]{:S(2)}) collective-permute-start(bf16[4,96,256]{2,1,0:T(8,128)(2,1)S(1)} %get-tuple-element.51.refs_2_.refs_0_), channel_id=1, source_target_pairs={{0,1},{1,0},{2,3},{3,2},{4,5},{5,4},{6,7},{7,6},{8,9},{9,8},{10,11... | collective-permute-start | bytes 589832 | tf_op jit(solution)/shard_map/ppermute | solution.py:94
  11.7 3.4 %collective-permute-start.4 = (bf16[4,64,256]{2,1,0:T(8,128)(2,1)S(1)}, bf16[4,64,256]{2,1,0:T(8,128)(2,1)S(1)}, u32[]{:S(2)}, u32[]{:S(2)}) collective-permute-start(bf16[4,64,256]{2,1,0:T(8,128)(2,1)S(1)} %get-tuple-element.61), channel_id=1, source_target_pairs={{0,2},{2,0},{4,6},{6,4},{8,10},{10,8},{12,14},{14,12},{16,18},{18,... | collective-permute-start | bytes 393224 | tf_op jit(solution)/shard_map/ppermute | solution.py:94
  13.2 1.3 %collective-permute-start.2 = (bf16[4,48,256]{2,1,0:T(8,128)(2,1)S(1)}, bf16[4,48,256]{2,1,0:T(8,128)(2,1)S(1)}, u32[]{:S(2)}, u32[]{:S(2)}) collective-permute-start(bf16[4,48,256]{2,1,0:T(8,128)(2,1)S(1)} %get-tuple-element.59), channel_id=1, source_target_pairs={{0,2},{2,0},{4,6},{6,4},{8,10},{10,8},{12,14},{14,12},{16,18},{18,... | collective-permute-start | bytes 294920 | tf_op jit(solution)/shard_map/ppermute | solution.py:94
  13.3 1.4 %collective-permute-start.3 = (bf16[4,48,256]{2,1,0:T(8,128)(2,1)S(1)}, bf16[4,48,256]{2,1,0:T(8,128)(2,1)S(1)}, u32[]{:S(2)}, u32[]{:S(2)}) collective-permute-start(bf16[4,48,256]{2,1,0:T(8,128)(2,1)S(1)} %get-tuple-element.60), channel_id=1, source_target_pairs={{0,2},{2,0},{4,6},{6,4},{8,10},{10,8},{12,14},{14,12},{16,18},{18,... | collective-permute-start | bytes 294920 | tf_op jit(solution)/shard_map/ppermute | solution.py:94
  13.8 1.3 %collective-permute-start.5 = (bf16[4,48,256]{2,1,0:T(8,128)(2,1)S(1)}, bf16[4,48,256]{2,1,0:T(8,128)(2,1)S(1)}, u32[]{:S(2)}, u32[]{:S(2)}) collective-permute-start(bf16[4,48,256]{2,1,0:T(8,128)(2,1)S(1)} %get-tuple-element.62), channel_id=1, source_target_pairs={{0,2},{2,0},{4,6},{6,4},{8,10},{10,8},{12,14},{14,12},{16,18},{18,... | collective-permute-start | bytes 294920 | tf_op jit(solution)/shard_map/ppermute | solution.py:94
  14.5 4.1 %collective-permute-start.7 = (bf16[4,640,256]{2,1,0:T(8,128)(2,1)S(1)}, bf16[4,640,256]{2,1,0:T(8,128)(2,1)S(1)}, u32[]{:S(2)}, u32[]{:S(2)}) collective-permute-start(bf16[4,640,256]{2,1,0:T(8,128)(2,1)S(1)} %get-tuple-element.53.refs_1_.refs_2_), channel_id=1, source_target_pairs={{0,2},{2,0},{4,6},{6,4},{8,10},{10,8},{12,14},{14,12},{16,18},{18,... | collective-permute-start | bytes 3932168 | tf_op jit(solution)/shard_map/ppermute | solution.py:94
  15.1 8.8 %collective-permute-start.9 = (bf16[2,4,48,256]{3,2,1,0:T(8,128)(2,1)S(1)}, bf16[2,4,48,256]{3,2,1,0:T(8,128)(2,1)S(1)}, u32[]{:S(2)}, u32[]{:S(2)}) collective-permute-start(bf16[2,4,48,256]{3,2,1,0:T(8,128)(2,1)S(1)} %get-tuple-element.63.refs_2_.refs_0_), channel_id=1, source_target_pairs={{0,1},{1,0},{2,3},{3,2},{4,5},{5,4},{6,7},{7,6},{8,9},{9,8},{10,11... | collective-permute-start | bytes 589832 | tf_op jit(solution)/shard_map/ppermute | solution.py:94
  15.7 3.0 %copy-start.2 = (f32[8,128]{1,0:T(8,128)S(1)}, f32[8,128]{1,0:T(8,128)}, u32[]{:S(2)}) copy-start(f32[8,128]{1,0:T(8,128)} %constant.7.clone.refs_4_) | copy-start | bytes 12292
  15.7 3.0 %copy-start.3 = (f32[8,128]{1,0:T(8,128)S(1)}, f32[8,128]{1,0:T(8,128)}, u32[]{:S(2)}) copy-start(f32[8,128]{1,0:T(8,128)} %constant.8.clone.refs_5_) | copy-start | bytes 12292
  15.7 13.0 %collective-permute-start.12 = (bf16[2,4,48,256]{3,2,1,0:T(8,128)(2,1)S(1)}, bf16[2,4,48,256]{3,2,1,0:T(8,128)(2,1)S(1)}, u32[]{:S(2)}, u32[]{:S(2)}) collective-permute-start(bf16[2,4,48,256]{3,2,1,0:T(8,128)(2,1)S(1)} %get-tuple-element.69.refs_0_), channel_id=1, source_target_pairs={{0,1},{1,0},{2,3},{3,2},{4,5},{5,4},{6,7},{7,6},{8,9},{9,8},{10,11... | collective-permute-start | bytes 589832 | tf_op jit(solution)/shard_map/ppermute | solution.py:94
  17.3 1.4 %collective-permute-start.6 = (bf16[4,48,256]{2,1,0:T(8,128)(2,1)S(1)}, bf16[4,48,256]{2,1,0:T(8,128)(2,1)S(1)}, u32[]{:S(2)}, u32[]{:S(2)}) collective-permute-start(bf16[4,48,256]{2,1,0:T(8,128)(2,1)S(1)} %get-tuple-element.65), channel_id=1, source_target_pairs={{0,2},{2,0},{4,6},{6,4},{8,10},{10,8},{12,14},{14,12},{16,18},{18,... | collective-permute-start | bytes 294920 | tf_op jit(solution)/shard_map/ppermute | solution.py:94
  17.3 15.4 %collective-permute-start.11 = (bf16[2,4,64,256]{3,2,1,0:T(8,128)(2,1)S(1)}, bf16[2,4,64,256]{3,2,1,0:T(8,128)(2,1)S(1)}, u32[]{:S(2)}, u32[]{:S(2)}) collective-permute-start(bf16[2,4,64,256]{3,2,1,0:T(8,128)(2,1)S(1)} %get-tuple-element.68.refs_0_), channel_id=1, source_target_pairs={{0,1},{1,0},{2,3},{3,2},{4,5},{5,4},{6,7},{7,6},{8,9},{9,8},{10,11... | collective-permute-start | bytes 786440 | tf_op jit(solution)/shard_map/ppermute | solution.py:94
  19.7 10.7 %collective-permute-start.8 = (bf16[192,640]{1,0:T(8,128)(2,1)S(1)}, bf16[192,640]{1,0:T(8,128)(2,1)S(1)}, u32[]{:S(2)}, u32[]{:S(2)}) collective-permute-start(bf16[192,640]{1,0:T(8,128)(2,1)S(1)} %send_0.1.refs_7_), channel_id=1, source_target_pairs={{0,8},{2,10},{4,12},{6,14},{8,0},{10,2},{12,4},{14,6},{16,24},{18,... | collective-permute-start | bytes 737288 | tf_op jit(solution)/shard_map/ppermute | solution.py:94
  24.9 12.3 %collective-permute-start.10 = (bf16[192,640]{1,0:T(8,128)(2,1)S(1)}, bf16[192,640]{1,0:T(8,128)(2,1)S(1)}, u32[]{:S(2)}, u32[]{:S(2)}) collective-permute-start(bf16[192,640]{1,0:T(8,128)(2,1)S(1)} %send_1.1.refs_6_), channel_id=1, source_target_pairs={{0,8},{2,10},{4,12},{6,14},{8,0},{10,2},{12,4},{14,6},{16,24},{18,... | collective-permute-start | bytes 737288 | tf_op jit(solution)/shard_map/ppermute | solution.py:94
  27.2 12.1 %collective-permute-start.15 = (bf16[2,4,48,256]{3,2,1,0:T(8,128)(2,1)S(1)}, bf16[2,4,48,256]{3,2,1,0:T(8,128)(2,1)S(1)}, u32[]{:S(2)}, u32[]{:S(2)}) collective-permute-start(bf16[2,4,48,256]{3,2,1,0:T(8,128)(2,1)S(1)} %get-tuple-element.72.refs_0_), channel_id=1, source_target_pairs={{0,1},{1,0},{2,3},{3,2},{4,5},{5,4},{6,7},{7,6},{8,9},{9,8},{10,11... | collective-permute-start | bytes 589832 | tf_op jit(solution)/shard_map/ppermute | solution.py:94
  29.7 12.1 %collective-permute-start.14 = (bf16[192,640]{1,0:T(8,128)(2,1)S(1)}, bf16[192,640]{1,0:T(8,128)(2,1)S(1)}, u32[]{:S(2)}, u32[]{:S(2)}) collective-permute-start(bf16[192,640]{1,0:T(8,128)(2,1)S(1)} %send_2.1.refs_7_), channel_id=1, source_target_pairs={{0,4},{2,6},{4,0},{6,2},{8,12},{10,14},{12,8},{14,10},{16,20},{18,... | collective-permute-start | bytes 737288 | tf_op jit(solution)/shard_map/ppermute | solution.py:94
  34.0 15.0 %collective-permute-start.17 = (bf16[256,640]{1,0:T(8,128)(2,1)S(1)}, bf16[256,640]{1,0:T(8,128)(2,1)S(1)}, u32[]{:S(2)}, u32[]{:S(2)}) collective-permute-start(bf16[256,640]{1,0:T(8,128)(2,1)S(1)} %send_3.1.refs_4_), channel_id=1, source_target_pairs={{0,8},{2,10},{4,12},{6,14},{8,0},{10,2},{12,4},{14,6},{16,24},{18,... | collective-permute-start | bytes 983048 | tf_op jit(solution)/shard_map/ppermute | solution.py:94
  37.3 9.0 %collective-permute-start.13 = (bf16[192,640]{1,0:T(8,128)(2,1)S(1)}, bf16[192,640]{1,0:T(8,128)(2,1)S(1)}, u32[]{:S(2)}, u32[]{:S(2)}) collective-permute-start(bf16[192,640]{1,0:T(8,128)(2,1)S(1)} %get-tuple-element.71), channel_id=1, source_target_pairs={{0,4},{2,6},{4,0},{6,2},{8,12},{10,14},{12,8},{14,10},{16,20},{18,... | collective-permute-start | bytes 737288 | tf_op jit(solution)/shard_map/ppermute | solution.py:94
  40.3 10.6 %collective-permute-start.18 = (bf16[192,640]{1,0:T(8,128)(2,1)S(1)}, bf16[192,640]{1,0:T(8,128)(2,1)S(1)}, u32[]{:S(2)}, u32[]{:S(2)}) collective-permute-start(bf16[192,640]{1,0:T(8,128)(2,1)S(1)} %send_4.1.refs_2_), channel_id=1, source_target_pairs={{0,4},{2,6},{4,0},{6,2},{8,12},{10,14},{12,8},{14,10},{16,20},{18,... | collective-permute-start | bytes 737288 | tf_op jit(solution)/shard_map/ppermute | solution.py:94
  41.9 8.3 %collective-permute-start.19 = (bf16[96,640]{1,0:T(8,128)(2,1)S(1)}, bf16[96,640]{1,0:T(8,128)(2,1)S(1)}, u32[]{:S(2)}, u32[]{:S(2)}) collective-permute-start(bf16[96,640]{1,0:T(8,128)(2,1)S(1)} %get-tuple-element.77), channel_id=1, source_target_pairs={{0,8},{2,10},{4,12},{6,14},{8,0},{10,2},{12,4},{14,6},{16,24},{18,... | collective-permute-start | bytes 368648 | tf_op jit(solution)/shard_map/ppermute | solution.py:94
  46.3 7.3 %collective-permute-start.16 = (bf16[96,640]{1,0:T(8,128)(2,1)S(1)}, bf16[96,640]{1,0:T(8,128)(2,1)S(1)}, u32[]{:S(2)}, u32[]{:S(2)}) collective-permute-start(bf16[96,640]{1,0:T(8,128)(2,1)S(1)} %get-tuple-element.75), channel_id=1, source_target_pairs={{0,16},{2,18},{4,20},{6,22},{8,24},{10,26},{12,28},{14,30},{16,0},... | collective-permute-start | bytes 368648 | tf_op jit(solution)/shard_map/ppermute | solution.py:94
  49.0 5.4 %collective-permute-start.21 = (bf16[128,640]{1,0:T(8,128)(2,1)S(1)}, bf16[128,640]{1,0:T(8,128)(2,1)S(1)}, u32[]{:S(2)}, u32[]{:S(2)}) collective-permute-start(bf16[128,640]{1,0:T(8,128)(2,1)S(1)} %get-tuple-element.81), channel_id=1, source_target_pairs={{0,4},{2,6},{4,0},{6,2},{8,12},{10,14},{12,8},{14,10},{16,20},{18,... | collective-permute-start | bytes 491528 | tf_op jit(solution)/shard_map/ppermute | solution.py:94
  50.1 7.1 %collective-permute-start.20 = (bf16[48,640]{1,0:T(8,128)(2,1)S(1)}, bf16[48,640]{1,0:T(8,128)(2,1)S(1)}, u32[]{:S(2)}, u32[]{:S(2)}) collective-permute-start(bf16[48,640]{1,0:T(8,128)(2,1)S(1)} %get-tuple-element.80), channel_id=1, source_target_pairs={{0,16},{2,18},{4,20},{6,22},{8,24},{10,26},{12,28},{14,30},{16,0},... | collective-permute-start | bytes 184328 | tf_op jit(solution)/shard_map/ppermute | solution.py:94
  51.0 6.3 %collective-permute-start.23 = (bf16[96,640]{1,0:T(8,128)(2,1)S(1)}, bf16[96,640]{1,0:T(8,128)(2,1)S(1)}, u32[]{:S(2)}, u32[]{:S(2)}) collective-permute-start(bf16[96,640]{1,0:T(8,128)(2,1)S(1)} %get-tuple-element.84), channel_id=1, source_target_pairs={{0,8},{2,10},{4,12},{6,14},{8,0},{10,2},{12,4},{14,6},{16,24},{18,... | collective-permute-start | bytes 368648 | tf_op jit(solution)/shard_map/ppermute | solution.py:94
  54.4 6.1 %collective-permute-start.22 = (bf16[64,640]{1,0:T(8,128)(2,1)S(1)}, bf16[64,640]{1,0:T(8,128)(2,1)S(1)}, u32[]{:S(2)}, u32[]{:S(2)}) collective-permute-start(bf16[64,640]{1,0:T(8,128)(2,1)S(1)} %get-tuple-element.83), channel_id=1, source_target_pairs={{0,16},{2,18},{4,20},{6,22},{8,24},{10,26},{12,28},{14,30},{16,0},... | collective-permute-start | bytes 245768 | tf_op jit(solution)/shard_map/ppermute | solution.py:94
  57.3 5.2 %collective-permute-start.24 = (bf16[48,640]{1,0:T(8,128)(2,1)S(1)}, bf16[48,640]{1,0:T(8,128)(2,1)S(1)}, u32[]{:S(2)}, u32[]{:S(2)}) collective-permute-start(bf16[48,640]{1,0:T(8,128)(2,1)S(1)} %get-tuple-element.86), channel_id=1, source_target_pairs={{0,16},{2,18},{4,20},{6,22},{8,24},{10,26},{12,28},{14,30},{16,0},... | collective-permute-start | bytes 184328 | tf_op jit(solution)/shard_map/ppermute | solution.py:94

commit v7 on v5

--- a/solution.py
+++ b/solution.py
@@ -21,7 +21,7 @@
 CHUNKS = (6, 6, 6, 8, 6)
 FIRST = (1, 1, 0, 1, 0)
 SECOND = ((2,), (4,), (0, 1), (3,))
-THIRD = ((2,), (0,), (3,), (1,))
+THIRD = ((2, 0), (3,), (1,))
 ACROSS = ((1,), (2,), (3,), (4,))
 PLAN = (
     ('merge', 0, (1, 2, 3), ()),
@@ -31,22 +31,20 @@
     ('send', 1, (), ()),
     ('keep', 1, (), ()),
     ('send', 2, (), (('y', 2),)),
-    ('keep', 2, (), (('first', 0),)),
-    ('send', 3, (), (('y', 3),)),
+    ('keep', 2, (), ()),
+    ('send', 3, (), (('y', 3), ('first', 0))),
     ('second', 2, (), ()),
     ('keep', 3, (), ()),
     ('send', 4, (), (('y', 4),)),
     ('second', 0, (), ()),
-    ('third', 0, (), (('first', 2),)),
     ('second', 3, (), (('first', 3),)),
     ('keep', 4, (), ()),
-    ('third', 1, (), (('second', 0),)),
+    ('third', 0, (), ()),
     ('second', 1, (), (('first', 4), ('second', 2))),
-    ('sum', 0, (), (('third', 0),)),
-    ('third', 2, (), (('second', 3),)),
-    ('sum', 1, (), (('third', 1),)),
-    ('third', 3, (), (('second', 1),)),
-    ('sum', 2, (), ()),
+    ('third', 1, (), ()),
+    ('third', 2, (), ()),
+    ('sum', 0, (), ()),
+    ('sum', 1, (), ()),
 )
 BASE_COST = 0.05
 COSTS = {
@@ -62,20 +60,19 @@
     'send_4': 0.275,
     'second_0': 0.191,
     'keep_4': 0.11,
-    'third_0': 0.286,
     'second_3': 0.191,
-    'third_1': 0.286,
     'second_1': 2,
-    'sum_0': 0.027,
-    'third_2': 0.304,
-    'sum_1': 1,
-    'third_3': 0.373,
-    'sum_2': 0.293,
     'panels': 0.05,
     'gate': 4,
     'first': 0.5,
     'send_1': 0.05,
     'keep_1': 0.05,
+    'third_0': 0.05,
+    'sum_0': 0.05,
+    'third_1': 0.05,
+    'sum_1': 0.05,
+    'third_2': 0.05,
+    'sum_2': 0.05,
 }
 
 VMEM = pl.BlockSpec(memory_space=pltpu.VMEM)

time: 63.4 us -> 63.5 us (level)
  starting transfers between devices: 30.6 us -> 31.5 us
  waiting for transfers between devices: 13.6 us -> 12.8 us
    ppermute x24 -> x23, starting transfers between devices: 28.1 us -> 29 us  [swap(): lax.ppermute(value, axis, [(i, i ^ bit) for i in range(lax.axis_size(axis...]
    ppermute x24 -> x23, waiting for transfers between devices: 13.6 us -> 12.8 us  [swap(): lax.ppermute(value, axis, [(i, i ^ bit) for i in range(lax.axis_size(axis...]
    pallas_call x29 -> x27, Pallas kernels: 18.6 us -> 18.6 us  [__call__(): pl.pallas_call(body, out_shape=[*outs, *(jax.ShapeDtypeStruct(g.shape, g....]
  transfers between devices with their start and end apart: 25 -> 24, of which waited for: 11 -> 11; matrix products, arithmetic and copies ran while one was open for 0% -> 0% of each run, Pallas kernels for 24% -> 24%
where the time goes in v7:
time: 63.5 us; the launch traced here: 63.3 us
  starting transfers between devices  31.5 us (50%)
  Pallas kernels  18.6 us (29%)
  waiting for transfers between devices  12.8 us (20%)
    ppermute x23, starting transfers between devices, swap(): lax.ppermute(value, axis, [(i, i ^ bit) for i in range(lax.axis_size(axis...  29 us
    pallas_call x27, Pallas kernels, __call__(): pl.pallas_call(body, out_shape=[*outs, *(jax.ShapeDtypeStruct(g.shape, g....  18.6 us
    ppermute x23, waiting for transfers between devices, swap(): lax.ppermute(value, axis, [(i, i ^ bit) for i in range(lax.axis_size(axis...  12.8 us
    ppermute x1, starting transfers between devices, local(): lax.ppermute(tail, 'tm', [(i, i + 1) for i in range(time_parts - 1)])  2.51 us
  transfers between devices with their start and end apart: 24, of which 11 were waited for; matrix products, arithmetic and copies ran while one was open for 0% of the time, Pallas kernels for 24%

profile of v7, /device:TPU:0, one launch (start us, length us, event | category | flops | bytes accessed | tf_op | source)
XLA Modules:
  0.0 63.3 jit_solution(5003274508890249720)
XLA Ops:
  0.0 1.1 %history.1.refs_5_ = bf16[640,128]{1,0:T(8,128)(2,1)S(1)} custom-call(bf16[640,4096]{1,0:T(8,128)(2,1)} %refs_0_.6), custom_call_target="tpu_custom_call" | custom-call | flops 50000000 | bytes 10000 | tf_op jit(solution)/shard_map/history/pallas_call | solution.py:336
  1.1 2.5 %collective-permute-start = (bf16[640,128]{1,0:T(8,128)(2,1)S(1)}, bf16[640,128]{1,0:T(8,128)(2,1)S(1)}, u32[]{:S(2)}, u32[]{:S(2)}) collective-permute-start(bf16[640,128]{1,0:T(8,128)(2,1)S(1)} %history.1.refs_5_), channel_id=1, source_target_pairs={{0,2},{2,4},{4,6},{6,8},{8,10},{10,12},{12,14},{14,16},{16,18},{18... | collective-permute-start | bytes 491528 | tf_op jit(solution)/shard_map/ppermute | solution.py:381
  3.7 3.0 %late.1 = (bf16[3,640,256]{2,1,0:T(8,128)(2,1)S(1)}, bf16[256,1152]{1,0:T(8,128)(2,1)S(1)}, f32[640,128]{1,0:T(8,128)S(1)}, bf16[256,128]{1,0:T(8,128)(2,1)S(1)}, bf16[512,640]{1,0:T(8,128)(2,1)S(1)}) custom-call(bf16[640,4096]{1,0:T(8,128)(2,1)S(1)} %copy-done, bf16[1,128]{1,0:T(2,128)(2,1)S(1)} %bitcast.4, s32[1,640]{1,0:T(1,128)S(1)} %reshape.13.refs_2_, ...), custom_call_target="tpu_custom_call" | custom-call | flops 50000000 | bytes 10000 | tf_op jit(solution)/shard_map/late/pallas_call | solution.py:336
  6.7 1.8 %first.1 = (bf16[4,96,256]{2,1,0:T(8,128)(2,1)S(1)}, bf16[4,640,256]{2,1,0:T(8,128)(2,1)S(1)}) custom-call(bf16[640,4096]{1,0:T(8,128)(2,1)S(1)} %copy-done, bf16[640,128]{1,0:T(8,128)(2,1)S(1)} %collective-permute-done.refs_1_, bf16[256,1152]{1,0:T(8,128)(2,1)S(1)} %get-tuple-element.44.refs_2_, bf16[256,256]{1,0:T(8,128)(2,1)S(1)} %copy-done.1, ...), custom_call_target="tpu_custom_call" | custom-call | flops 500000000 | bytes 10000 | tf_op jit(solution)/shard_map/first/pallas_call | solution.py:336
  8.5 2.4 %collective-permute-start.1 = (bf16[4,96,256]{2,1,0:T(8,128)(2,1)S(1)}, bf16[4,96,256]{2,1,0:T(8,128)(2,1)S(1)}, u32[]{:S(2)}, u32[]{:S(2)}) collective-permute-start(bf16[4,96,256]{2,1,0:T(8,128)(2,1)S(1)} %get-tuple-element.49.refs_2_.refs_0_), channel_id=1, source_target_pairs={{0,1},{1,0},{2,3},{3,2},{4,5},{5,4},{6,7},{7,6},{8,9},{9,8},{10,11... | collective-permute-start | bytes 589832 | tf_op jit(solution)/shard_map/ppermute | solution.py:91
  11.7 1.6 %collective-permute-start.4 = (bf16[4,64,256]{2,1,0:T(8,128)(2,1)S(1)}, bf16[4,64,256]{2,1,0:T(8,128)(2,1)S(1)}, u32[]{:S(2)}, u32[]{:S(2)}) collective-permute-start(bf16[4,64,256]{2,1,0:T(8,128)(2,1)S(1)} %get-tuple-element.59), channel_id=1, source_target_pairs={{0,2},{2,0},{4,6},{6,4},{8,10},{10,8},{12,14},{14,12},{16,18},{18,... | collective-permute-start | bytes 393224 | tf_op jit(solution)/shard_map/ppermute | solution.py:91
  15.7 1.5 %collective-permute-start.12 = (bf16[2,4,48,256]{3,2,1,0:T(8,128)(2,1)S(1)}, bf16[2,4,48,256]{3,2,1,0:T(8,128)(2,1)S(1)}, u32[]{:S(2)}, u32[]{:S(2)}) collective-permute-start(bf16[2,4,48,256]{3,2,1,0:T(8,128)(2,1)S(1)} %get-tuple-element.67.refs_0_), channel_id=1, source_target_pairs={{0,1},{1,0},{2,3},{3,2},{4,5},{5,4},{6,7},{7,6},{8,9},{9,8},{10,11... | collective-permute-start | bytes 589832 | tf_op jit(solution)/shard_map/ppermute | solution.py:91
  17.4 1.2 %collective-permute-start.11 = (bf16[2,4,64,256]{3,2,1,0:T(8,128)(2,1)S(1)}, bf16[2,4,64,256]{3,2,1,0:T(8,128)(2,1)S(1)}, u32[]{:S(2)}, u32[]{:S(2)}) collective-permute-start(bf16[2,4,64,256]{3,2,1,0:T(8,128)(2,1)S(1)} %get-tuple-element.66.refs_0_), channel_id=1, source_target_pairs={{0,1},{1,0},{2,3},{3,2},{4,5},{5,4},{6,7},{7,6},{8,9},{9,8},{10,11... | collective-permute-start | bytes 786440 | tf_op jit(solution)/shard_map/ppermute | solution.py:91
  18.7 1.0 %send_0.1.refs_7_ = bf16[192,640]{1,0:T(8,128)(2,1)S(1)} custom-call(bf16[4,48,256]{2,1,0:T(8,128)(2,1)S(1)} %get-tuple-element.62.refs_0_.refs_6_, bf16[4,48,256]{2,1,0:T(8,128)(2,1)S(1)} %collective-permute-done.6.refs_1_, bf16[4,640,256]{2,1,0:T(8,128)(2,1)S(1)} %get-tuple-element.51.refs_1_.refs_2_, ...), custom_call_target="tpu_custom_call" | custom-call | flops 500000000 | bytes 10000 | tf_op jit(solution)/shard_map/send_0/pallas_call | solution.py:336
  19.7 3.0 %collective-permute-start.8 = (bf16[192,640]{1,0:T(8,128)(2,1)S(1)}, bf16[192,640]{1,0:T(8,128)(2,1)S(1)}, u32[]{:S(2)}, u32[]{:S(2)}) collective-permute-start(bf16[192,640]{1,0:T(8,128)(2,1)S(1)} %send_0.1.refs_7_), channel_id=1, source_target_pairs={{0,8},{2,10},{4,12},{6,14},{8,0},{10,2},{12,4},{14,6},{16,24},{18,... | collective-permute-start | bytes 737288 | tf_op jit(solution)/shard_map/ppermute | solution.py:91
  22.7 1.0 %keep_0.1 = (f32[192,640]{1,0:T(8,128)S(1)}, bf16[2,4,48,256]{3,2,1,0:T(8,128)(2,1)S(1)}) custom-call(bf16[4,48,256]{2,1,0:T(8,128)(2,1)S(1)} %get-tuple-element.62.refs_0_.refs_6_, bf16[4,48,256]{2,1,0:T(8,128)(2,1)S(1)} %collective-permute-done.6.refs_1_, ...), custom_call_target="tpu_custom_call", output_to_operand_aliasing={{1}: (6, {})} | custom-call | flops 182000000 | bytes 10000 | tf_op jit(solution)/shard_map/keep_0/pallas_call | solution.py:336
  23.7 1.0 %send_1.1.refs_6_ = bf16[192,640]{1,0:T(8,128)(2,1)S(1)} custom-call(bf16[2,4,48,256]{3,2,1,0:T(8,128)(2,1)S(1)} %get-tuple-element.61.refs_2_.refs_0_, bf16[2,4,48,256]{3,2,1,0:T(8,128)(2,1)S(1)} %collective-permute-done.9.refs_1_, bf16[4,640,256]{2,1,0:T(8,128)(2,1)S(1)} %get-tuple-element.51.refs_1_.refs_2_, ...), custom_call_target="tpu_custom_call" | custom-call | flops 50000000 | bytes 10000 | tf_op jit(solution)/shard_map/send_1/pallas_call | solution.py:336
  24.7 2.3 %collective-permute-start.10 = (bf16[192,640]{1,0:T(8,128)(2,1)S(1)}, bf16[192,640]{1,0:T(8,128)(2,1)S(1)}, u32[]{:S(2)}, u32[]{:S(2)}) collective-permute-start(bf16[192,640]{1,0:T(8,128)(2,1)S(1)} %send_1.1.refs_6_), channel_id=1, source_target_pairs={{0,8},{2,10},{4,12},{6,14},{8,0},{10,2},{12,4},{14,6},{16,24},{18,... | collective-permute-start | bytes 737288 | tf_op jit(solution)/shard_map/ppermute | solution.py:91
  27.5 1.0 %keep_1.1.refs_7_.refs_2_ = f32[192,640]{1,0:T(8,128)S(1)} custom-call(bf16[2,4,48,256]{3,2,1,0:T(8,128)(2,1)S(1)} %get-tuple-element.61.refs_2_.refs_0_, bf16[2,4,48,256]{3,2,1,0:T(8,128)(2,1)S(1)} %collective-permute-done.9.refs_1_, bf16[4,640,256]{2,1,0:T(8,128)(2,1)S(1)} %get-tuple-element.51.refs_1_.refs_2_, ...), custom_call_target="tpu_custom_call" | custom-call | flops 50000000 | bytes 10000 | tf_op jit(solution)/shard_map/keep_1/pallas_call | solution.py:336
  28.5 1.0 %send_2.1.refs_6_ = bf16[192,640]{1,0:T(8,128)(2,1)S(1)} custom-call(bf16[2,4,48,256]{3,2,1,0:T(8,128)(2,1)S(1)} %get-tuple-element.67.refs_0_, bf16[2,4,48,256]{3,2,1,0:T(8,128)(2,1)S(1)} %collective-permute-done.12.refs_1_.refs_6_, bf16[4,640,256]{2,1,0:T(8,128)(2,1)S(1)} %get-tuple-element.51.refs_1_.refs_2_, ...), custom_call_target="tpu_custom_call" | custom-call | flops 15000000512 | bytes 10000 | tf_op jit(solution)/shard_map/send_2/pallas_call | solution.py:336
  30.3 1.0 %keep_2.1.refs_8_.refs_0_ = f32[192,640]{1,0:T(8,128)S(1)} custom-call(bf16[2,4,48,256]{3,2,1,0:T(8,128)(2,1)S(1)} %get-tuple-element.67.refs_0_, bf16[2,4,48,256]{3,2,1,0:T(8,128)(2,1)S(1)} %collective-permute-done.12.refs_1_.refs_6_, bf16[4,640,256]{2,1,0:T(8,128)(2,1)S(1)} %get-tuple-element.51.refs_1_.refs_2_, ...), custom_call_target="tpu_custom_call" | custom-call | flops 347000000 | bytes 10000 | tf_op jit(solution)/shard_map/keep_2/pallas_call | solution.py:336
  31.3 1.5 %collective-permute-done.11.refs_1_.refs_6_ = bf16[2,4,64,256]{3,2,1,0:T(8,128)(2,1)S(1)} collective-permute-done((bf16[2,4,64,256]{3,2,1,0:T(8,128)(2,1)S(1)}, bf16[2,4,64,256]{3,2,1,0:T(8,128)(2,1)S(1)}, u32[]{:S(2)}, u32[]{:S(2)}) %collective-permute-start.11) | collective-permute-done | bytes 262176 | tf_op jit(solution)/shard_map/ppermute | solution.py:91
  32.8 1.2 %send_3.1.refs_4_ = bf16[256,640]{1,0:T(8,128)(2,1)S(1)} custom-call(bf16[2,4,64,256]{3,2,1,0:T(8,128)(2,1)S(1)} %get-tuple-element.66.refs_0_, bf16[2,4,64,256]{3,2,1,0:T(8,128)(2,1)S(1)} %collective-permute-done.11.refs_1_.refs_6_, bf16[4,640,256]{2,1,0:T(8,128)(2,1)S(1)} %get-tuple-element.51.refs_1_.refs_2_, ...), custom_call_target="tpu_custom_call" | custom-call | flops 277000000 | bytes 10000 | tf_op jit(solution)/shard_map/send_3/pallas_call | solution.py:336
  34.0 3.0 %collective-permute-start.17 = (bf16[256,640]{1,0:T(8,128)(2,1)S(1)}, bf16[256,640]{1,0:T(8,128)(2,1)S(1)}, u32[]{:S(2)}, u32[]{:S(2)}) collective-permute-start(bf16[256,640]{1,0:T(8,128)(2,1)S(1)} %send_3.1.refs_4_), channel_id=1, source_target_pairs={{0,8},{2,10},{4,12},{6,14},{8,0},{10,2},{12,4},{14,6},{16,24},{18,... | collective-permute-start | bytes 983048 | tf_op jit(solution)/shard_map/ppermute | solution.py:91
  37.7 1.3 %keep_3.1.refs_7_.refs_0_ = f32[256,640]{1,0:T(8,128)S(1)} custom-call(bf16[2,4,64,256]{3,2,1,0:T(8,128)(2,1)S(1)} %get-tuple-element.66.refs_0_, bf16[2,4,64,256]{3,2,1,0:T(8,128)(2,1)S(1)} %collective-permute-done.11.refs_1_.refs_6_, bf16[4,640,256]{2,1,0:T(8,128)(2,1)S(1)} %get-tuple-element.51.refs_1_.refs_2_, ...), custom_call_target="tpu_custom_call" | custom-call | flops 112000000 | bytes 10000 | tf_op jit(solution)/shard_map/keep_3/pallas_call | solution.py:336
  39.1 1.0 %send_4.1.refs_2_ = bf16[192,640]{1,0:T(8,128)(2,1)S(1)} custom-call(bf16[2,4,48,256]{3,2,1,0:T(8,128)(2,1)S(1)} %get-tuple-element.70.refs_0_, bf16[2,4,48,256]{3,2,1,0:T(8,128)(2,1)S(1)} %collective-permute-done.15.refs_1_.refs_6_, bf16[4,640,256]{2,1,0:T(8,128)(2,1)S(1)} %get-tuple-element.51.refs_1_.refs_2_, ...), custom_call_target="tpu_custom_call" | custom-call | flops 275000000 | bytes 10000 | tf_op jit(solution)/shard_map/send_4/pallas_call | solution.py:336
  40.1 1.5 %collective-permute-start.19 = (bf16[192,640]{1,0:T(8,128)(2,1)S(1)}, bf16[192,640]{1,0:T(8,128)(2,1)S(1)}, u32[]{:S(2)}, u32[]{:S(2)}) collective-permute-start(bf16[192,640]{1,0:T(8,128)(2,1)S(1)} %send_4.1.refs_2_), channel_id=1, source_target_pairs={{0,4},{2,6},{4,0},{6,2},{8,12},{10,14},{12,8},{14,10},{16,20},{18,... | collective-permute-start | bytes 737288 | tf_op jit(solution)/shard_map/ppermute | solution.py:91
  41.7 3.4 %collective-permute-done.17.refs_1_.refs_2_ = bf16[256,640]{1,0:T(8,128)(2,1)S(1)} collective-permute-done((bf16[256,640]{1,0:T(8,128)(2,1)S(1)}, bf16[256,640]{1,0:T(8,128)(2,1)S(1)}, u32[]{:S(2)}, u32[]{:S(2)}) %collective-permute-start.17) | collective-permute-done | bytes 327712 | tf_op jit(solution)/shard_map/ppermute | solution.py:91
  46.0 1.0 %keep_4.1.refs_4_.refs_0_ = f32[192,640]{1,0:T(8,128)S(1)} custom-call(bf16[2,4,48,256]{3,2,1,0:T(8,128)(2,1)S(1)} %get-tuple-element.70.refs_0_, bf16[2,4,48,256]{3,2,1,0:T(8,128)(2,1)S(1)} %collective-permute-done.15.refs_1_.refs_6_, bf16[4,640,256]{2,1,0:T(8,128)(2,1)S(1)} %get-tuple-element.51.refs_1_.refs_2_, ...), custom_call_target="tpu_custom_call" | custom-call | flops 110000000 | bytes 10000 | tf_op jit(solution)/shard_map/keep_4/pallas_call | solution.py:336
  47.1 2.7 %collective-permute-start.18 = (bf16[144,640]{1,0:T(8,128)(2,1)S(1)}, bf16[144,640]{1,0:T(8,128)(2,1)S(1)}, u32[]{:S(2)}, u32[]{:S(2)}) collective-permute-start(bf16[144,640]{1,0:T(8,128)(2,1)S(1)} %get-tuple-element.75), channel_id=1, source_target_pairs={{0,16},{2,18},{4,20},{6,22},{8,24},{10,26},{12,28},{14,30},{16,0},... | collective-permute-start | bytes 552968 | tf_op jit(solution)/shard_map/ppermute | solution.py:91
  49.8 0.9 %collective-permute-done.19.refs_1_.refs_2_ = bf16[192,640]{1,0:T(8,128)(2,1)S(1)} collective-permute-done((bf16[192,640]{1,0:T(8,128)(2,1)S(1)}, bf16[192,640]{1,0:T(8,128)(2,1)S(1)}, u32[]{:S(2)}, u32[]{:S(2)}) %collective-permute-start.19) | collective-permute-done | bytes 245792 | tf_op jit(solution)/shard_map/ppermute | solution.py:91
  51.5 1.0 %collective-permute-done.21.refs_1_ = bf16[128,640]{1,0:T(8,128)(2,1)S(1)} collective-permute-done((bf16[128,640]{1,0:T(8,128)(2,1)S(1)}, bf16[128,640]{1,0:T(8,128)(2,1)S(1)}, u32[]{:S(2)}, u32[]{:S(2)}) %collective-permute-start.21) | collective-permute-done | bytes 163872 | tf_op jit(solution)/shard_map/ppermute | solution.py:91
  52.5 2.7 %collective-permute-start.22 = (bf16[64,640]{1,0:T(8,128)(2,1)S(1)}, bf16[64,640]{1,0:T(8,128)(2,1)S(1)}, u32[]{:S(2)}, u32[]{:S(2)}) collective-permute-start(bf16[64,640]{1,0:T(8,128)(2,1)S(1)} %get-tuple-element.81), channel_id=1, source_target_pairs={{0,16},{2,18},{4,20},{6,22},{8,24},{10,26},{12,28},{14,30},{16,0},... | collective-permute-start | bytes 245768 | tf_op jit(solution)/shard_map/ppermute | solution.py:91
  55.2 1.1 %collective-permute-done.20.refs_1_ = bf16[96,640]{1,0:T(8,128)(2,1)S(1)} collective-permute-done((bf16[96,640]{1,0:T(8,128)(2,1)S(1)}, bf16[96,640]{1,0:T(8,128)(2,1)S(1)}, u32[]{:S(2)}, u32[]{:S(2)}) %collective-permute-start.20) | collective-permute-done | bytes 122912 | tf_op jit(solution)/shard_map/ppermute | solution.py:91
  56.3 2.2 %collective-permute-start.23 = (bf16[48,640]{1,0:T(8,128)(2,1)S(1)}, bf16[48,640]{1,0:T(8,128)(2,1)S(1)}, u32[]{:S(2)}, u32[]{:S(2)}) collective-permute-start(bf16[48,640]{1,0:T(8,128)(2,1)S(1)} %get-tuple-element.82), channel_id=1, source_target_pairs={{0,16},{2,18},{4,20},{6,22},{8,24},{10,26},{12,28},{14,30},{16,0},... | collective-permute-start | bytes 184328 | tf_op jit(solution)/shard_map/ppermute | solution.py:91
  58.6 1.6 %collective-permute-done.18.refs_1_ = bf16[144,640]{1,0:T(8,128)(2,1)S(1)} collective-permute-done((bf16[144,640]{1,0:T(8,128)(2,1)S(1)}, bf16[144,640]{1,0:T(8,128)(2,1)S(1)}, u32[]{:S(2)}, u32[]{:S(2)}) %collective-permute-start.18) | collective-permute-done | bytes 184352 | tf_op jit(solution)/shard_map/ppermute | solution.py:91
  60.2 1.5 %collective-permute-done.22.refs_1_ = bf16[64,640]{1,0:T(8,128)(2,1)S(1)} collective-permute-done((bf16[64,640]{1,0:T(8,128)(2,1)S(1)}, bf16[64,640]{1,0:T(8,128)(2,1)S(1)}, u32[]{:S(2)}, u32[]{:S(2)}) %collective-permute-start.22) | collective-permute-done | bytes 81952 | tf_op jit(solution)/shard_map/ppermute | solution.py:91
  (58 shorter events, 9.1 us)
Async XLA Ops:
  0.0 3.6 %copy-start.1 = (bf16[256,256]{1,0:T(8,128)(2,1)S(1)}, bf16[256,256]{1,0:T(8,128)(2,1)}, u32[]{:S(2)}) copy-start(bf16[256,256]{1,0:T(8,128)(2,1)} %constant.6.clone.refs_4_.refs_3_.refs_0_) | copy-start | bytes 393220
  0.0 3.6 %copy-start.6 = (s32[640]{0:T(1024)S(1)}, s32[640]{0:T(1024)}, u32[]{:S(2)}) copy-start(s32[640]{0:T(1024)} %param.10) | copy-start | bytes 7684
  0.0 3.6 %copy-start.5 = (bf16[128]{0:T(256)(128)(2,1)S(1)}, bf16[128]{0:T(256)(128)(2,1)}, u32[]{:S(2)}) copy-start(bf16[128]{0:T(256)(128)(2,1)} %param.8) | copy-start | bytes 772
  0.0 3.7 %copy-start = (bf16[640,4096]{1,0:T(8,128)(2,1)S(1)}, bf16[640,4096]{1,0:T(8,128)(2,1)}, u32[]{:S(2)}) copy-start(bf16[640,4096]{1,0:T(8,128)(2,1)} %refs_0_.6) | copy-start | bytes 15728644
  0.0 3.7 %copy-start.4 = (s32[512]{0:T(512)S(1)}, s32[512]{0:T(512)}, u32[]{:S(2)}) copy-start(s32[512]{0:T(512)} %param.9) | copy-start | bytes 6148
  1.1 5.6 %collective-permute-start = (bf16[640,128]{1,0:T(8,128)(2,1)S(1)}, bf16[640,128]{1,0:T(8,128)(2,1)S(1)}, u32[]{:S(2)}, u32[]{:S(2)}) collective-permute-start(bf16[640,128]{1,0:T(8,128)(2,1)S(1)} %history.1.refs_5_), channel_id=1, source_target_pairs={{0,2},{2,4},{4,6},{6,8},{8,10},{10,12},{12,14},{14,16},{16,18},{18... | collective-permute-start | bytes 491528 | tf_op jit(solution)/shard_map/ppermute | solution.py:381
  8.5 8.8 %collective-permute-start.1 = (bf16[4,96,256]{2,1,0:T(8,128)(2,1)S(1)}, bf16[4,96,256]{2,1,0:T(8,128)(2,1)S(1)}, u32[]{:S(2)}, u32[]{:S(2)}) collective-permute-start(bf16[4,96,256]{2,1,0:T(8,128)(2,1)S(1)} %get-tuple-element.49.refs_2_.refs_0_), channel_id=1, source_target_pairs={{0,1},{1,0},{2,3},{3,2},{4,5},{5,4},{6,7},{7,6},{8,9},{9,8},{10,11... | collective-permute-start | bytes 589832 | tf_op jit(solution)/shard_map/ppermute | solution.py:91
  11.7 3.4 %collective-permute-start.4 = (bf16[4,64,256]{2,1,0:T(8,128)(2,1)S(1)}, bf16[4,64,256]{2,1,0:T(8,128)(2,1)S(1)}, u32[]{:S(2)}, u32[]{:S(2)}) collective-permute-start(bf16[4,64,256]{2,1,0:T(8,128)(2,1)S(1)} %get-tuple-element.59), channel_id=1, source_target_pairs={{0,2},{2,0},{4,6},{6,4},{8,10},{10,8},{12,14},{14,12},{16,18},{18,... | collective-permute-start | bytes 393224 | tf_op jit(solution)/shard_map/ppermute | solution.py:91
  13.3 1.3 %collective-permute-start.2 = (bf16[4,48,256]{2,1,0:T(8,128)(2,1)S(1)}, bf16[4,48,256]{2,1,0:T(8,128)(2,1)S(1)}, u32[]{:S(2)}, u32[]{:S(2)}) collective-permute-start(bf16[4,48,256]{2,1,0:T(8,128)(2,1)S(1)} %get-tuple-element.57), channel_id=1, source_target_pairs={{0,2},{2,0},{4,6},{6,4},{8,10},{10,8},{12,14},{14,12},{16,18},{18,... | collective-permute-start | bytes 294920 | tf_op jit(solution)/shard_map/ppermute | solution.py:91
  13.3 1.4 %collective-permute-start.3 = (bf16[4,48,256]{2,1,0:T(8,128)(2,1)S(1)}, bf16[4,48,256]{2,1,0:T(8,128)(2,1)S(1)}, u32[]{:S(2)}, u32[]{:S(2)}) collective-permute-start(bf16[4,48,256]{2,1,0:T(8,128)(2,1)S(1)} %get-tuple-element.58), channel_id=1, source_target_pairs={{0,2},{2,0},{4,6},{6,4},{8,10},{10,8},{12,14},{14,12},{16,18},{18,... | collective-permute-start | bytes 294920 | tf_op jit(solution)/shard_map/ppermute | solution.py:91
  13.8 1.3 %collective-permute-start.5 = (bf16[4,48,256]{2,1,0:T(8,128)(2,1)S(1)}, bf16[4,48,256]{2,1,0:T(8,128)(2,1)S(1)}, u32[]{:S(2)}, u32[]{:S(2)}) collective-permute-start(bf16[4,48,256]{2,1,0:T(8,128)(2,1)S(1)} %get-tuple-element.60), channel_id=1, source_target_pairs={{0,2},{2,0},{4,6},{6,4},{8,10},{10,8},{12,14},{14,12},{16,18},{18,... | collective-permute-start | bytes 294920 | tf_op jit(solution)/shard_map/ppermute | solution.py:91
  14.6 4.1 %collective-permute-start.7 = (bf16[4,640,256]{2,1,0:T(8,128)(2,1)S(1)}, bf16[4,640,256]{2,1,0:T(8,128)(2,1)S(1)}, u32[]{:S(2)}, u32[]{:S(2)}) collective-permute-start(bf16[4,640,256]{2,1,0:T(8,128)(2,1)S(1)} %get-tuple-element.51.refs_1_.refs_2_), channel_id=1, source_target_pairs={{0,2},{2,0},{4,6},{6,4},{8,10},{10,8},{12,14},{14,12},{16,18},{18,... | collective-permute-start | bytes 3932168 | tf_op jit(solution)/shard_map/ppermute | solution.py:91
  15.1 8.5 %collective-permute-start.9 = (bf16[2,4,48,256]{3,2,1,0:T(8,128)(2,1)S(1)}, bf16[2,4,48,256]{3,2,1,0:T(8,128)(2,1)S(1)}, u32[]{:S(2)}, u32[]{:S(2)}) collective-permute-start(bf16[2,4,48,256]{3,2,1,0:T(8,128)(2,1)S(1)} %get-tuple-element.61.refs_2_.refs_0_), channel_id=1, source_target_pairs={{0,1},{1,0},{2,3},{3,2},{4,5},{5,4},{6,7},{7,6},{8,9},{9,8},{10,11... | collective-permute-start | bytes 589832 | tf_op jit(solution)/shard_map/ppermute | solution.py:91
  15.7 3.0 %copy-start.2 = (f32[8,128]{1,0:T(8,128)S(1)}, f32[8,128]{1,0:T(8,128)}, u32[]{:S(2)}) copy-start(f32[8,128]{1,0:T(8,128)} %constant.7.clone.refs_4_) | copy-start | bytes 12292
  15.7 3.0 %copy-start.3 = (f32[8,128]{1,0:T(8,128)S(1)}, f32[8,128]{1,0:T(8,128)}, u32[]{:S(2)}) copy-start(f32[8,128]{1,0:T(8,128)} %constant.8.clone.refs_5_) | copy-start | bytes 12292
  15.7 12.8 %collective-permute-start.12 = (bf16[2,4,48,256]{3,2,1,0:T(8,128)(2,1)S(1)}, bf16[2,4,48,256]{3,2,1,0:T(8,128)(2,1)S(1)}, u32[]{:S(2)}, u32[]{:S(2)}) collective-permute-start(bf16[2,4,48,256]{3,2,1,0:T(8,128)(2,1)S(1)} %get-tuple-element.67.refs_0_), channel_id=1, source_target_pairs={{0,1},{1,0},{2,3},{3,2},{4,5},{5,4},{6,7},{7,6},{8,9},{9,8},{10,11... | collective-permute-start | bytes 589832 | tf_op jit(solution)/shard_map/ppermute | solution.py:91
  17.3 1.4 %collective-permute-start.6 = (bf16[4,48,256]{2,1,0:T(8,128)(2,1)S(1)}, bf16[4,48,256]{2,1,0:T(8,128)(2,1)S(1)}, u32[]{:S(2)}, u32[]{:S(2)}) collective-permute-start(bf16[4,48,256]{2,1,0:T(8,128)(2,1)S(1)} %get-tuple-element.63), channel_id=1, source_target_pairs={{0,2},{2,0},{4,6},{6,4},{8,10},{10,8},{12,14},{14,12},{16,18},{18,... | collective-permute-start | bytes 294920 | tf_op jit(solution)/shard_map/ppermute | solution.py:91
  17.4 15.4 %collective-permute-start.11 = (bf16[2,4,64,256]{3,2,1,0:T(8,128)(2,1)S(1)}, bf16[2,4,64,256]{3,2,1,0:T(8,128)(2,1)S(1)}, u32[]{:S(2)}, u32[]{:S(2)}) collective-permute-start(bf16[2,4,64,256]{3,2,1,0:T(8,128)(2,1)S(1)} %get-tuple-element.66.refs_0_), channel_id=1, source_target_pairs={{0,1},{1,0},{2,3},{3,2},{4,5},{5,4},{6,7},{7,6},{8,9},{9,8},{10,11... | collective-permute-start | bytes 786440 | tf_op jit(solution)/shard_map/ppermute | solution.py:91
  19.7 13.1 %collective-permute-start.8 = (bf16[192,640]{1,0:T(8,128)(2,1)S(1)}, bf16[192,640]{1,0:T(8,128)(2,1)S(1)}, u32[]{:S(2)}, u32[]{:S(2)}) collective-permute-start(bf16[192,640]{1,0:T(8,128)(2,1)S(1)} %send_0.1.refs_7_), channel_id=1, source_target_pairs={{0,8},{2,10},{4,12},{6,14},{8,0},{10,2},{12,4},{14,6},{16,24},{18,... | collective-permute-start | bytes 737288 | tf_op jit(solution)/shard_map/ppermute | solution.py:91
  24.7 12.3 %collective-permute-start.10 = (bf16[192,640]{1,0:T(8,128)(2,1)S(1)}, bf16[192,640]{1,0:T(8,128)(2,1)S(1)}, u32[]{:S(2)}, u32[]{:S(2)}) collective-permute-start(bf16[192,640]{1,0:T(8,128)(2,1)S(1)} %send_1.1.refs_6_), channel_id=1, source_target_pairs={{0,8},{2,10},{4,12},{6,14},{8,0},{10,2},{12,4},{14,6},{16,24},{18,... | collective-permute-start | bytes 737288 | tf_op jit(solution)/shard_map/ppermute | solution.py:91
  27.0 12.1 %collective-permute-start.15 = (bf16[2,4,48,256]{3,2,1,0:T(8,128)(2,1)S(1)}, bf16[2,4,48,256]{3,2,1,0:T(8,128)(2,1)S(1)}, u32[]{:S(2)}, u32[]{:S(2)}) collective-permute-start(bf16[2,4,48,256]{3,2,1,0:T(8,128)(2,1)S(1)} %get-tuple-element.70.refs_0_), channel_id=1, source_target_pairs={{0,1},{1,0},{2,3},{3,2},{4,5},{5,4},{6,7},{7,6},{8,9},{9,8},{10,11... | collective-permute-start | bytes 589832 | tf_op jit(solution)/shard_map/ppermute | solution.py:91
  29.5 12.1 %collective-permute-start.14 = (bf16[192,640]{1,0:T(8,128)(2,1)S(1)}, bf16[192,640]{1,0:T(8,128)(2,1)S(1)}, u32[]{:S(2)}, u32[]{:S(2)}) collective-permute-start(bf16[192,640]{1,0:T(8,128)(2,1)S(1)} %send_2.1.refs_6_), channel_id=1, source_target_pairs={{0,4},{2,6},{4,0},{6,2},{8,12},{10,14},{12,8},{14,10},{16,20},{18,... | collective-permute-start | bytes 737288 | tf_op jit(solution)/shard_map/ppermute | solution.py:91
  34.0 11.1 %collective-permute-start.17 = (bf16[256,640]{1,0:T(8,128)(2,1)S(1)}, bf16[256,640]{1,0:T(8,128)(2,1)S(1)}, u32[]{:S(2)}, u32[]{:S(2)}) collective-permute-start(bf16[256,640]{1,0:T(8,128)(2,1)S(1)} %send_3.1.refs_4_), channel_id=1, source_target_pairs={{0,8},{2,10},{4,12},{6,14},{8,0},{10,2},{12,4},{14,6},{16,24},{18,... | collective-permute-start | bytes 983048 | tf_op jit(solution)/shard_map/ppermute | solution.py:91
  37.1 10.0 %collective-permute-start.13 = (bf16[192,640]{1,0:T(8,128)(2,1)S(1)}, bf16[192,640]{1,0:T(8,128)(2,1)S(1)}, u32[]{:S(2)}, u32[]{:S(2)}) collective-permute-start(bf16[192,640]{1,0:T(8,128)(2,1)S(1)} %get-tuple-element.69), channel_id=1, source_target_pairs={{0,4},{2,6},{4,0},{6,2},{8,12},{10,14},{12,8},{14,10},{16,20},{18,... | collective-permute-start | bytes 737288 | tf_op jit(solution)/shard_map/ppermute | solution.py:91
  40.1 10.6 %collective-permute-start.19 = (bf16[192,640]{1,0:T(8,128)(2,1)S(1)}, bf16[192,640]{1,0:T(8,128)(2,1)S(1)}, u32[]{:S(2)}, u32[]{:S(2)}) collective-permute-start(bf16[192,640]{1,0:T(8,128)(2,1)S(1)} %send_4.1.refs_2_), channel_id=1, source_target_pairs={{0,4},{2,6},{4,0},{6,2},{8,12},{10,14},{12,8},{14,10},{16,20},{18,... | collective-permute-start | bytes 737288 | tf_op jit(solution)/shard_map/ppermute | solution.py:91
  41.6 5.4 %collective-permute-start.16 = (bf16[96,640]{1,0:T(8,128)(2,1)S(1)}, bf16[96,640]{1,0:T(8,128)(2,1)S(1)}, u32[]{:S(2)}, u32[]{:S(2)}) collective-permute-start(bf16[96,640]{1,0:T(8,128)(2,1)S(1)} %get-tuple-element.72), channel_id=1, source_target_pairs={{0,8},{2,10},{4,12},{6,14},{8,0},{10,2},{12,4},{14,6},{16,24},{18,... | collective-permute-start | bytes 368648 | tf_op jit(solution)/shard_map/ppermute | solution.py:91
  45.2 7.3 %collective-permute-start.21 = (bf16[128,640]{1,0:T(8,128)(2,1)S(1)}, bf16[128,640]{1,0:T(8,128)(2,1)S(1)}, u32[]{:S(2)}, u32[]{:S(2)}) collective-permute-start(bf16[128,640]{1,0:T(8,128)(2,1)S(1)} %get-tuple-element.78), channel_id=1, source_target_pairs={{0,4},{2,6},{4,0},{6,2},{8,12},{10,14},{12,8},{14,10},{16,20},{18,... | collective-permute-start | bytes 491528 | tf_op jit(solution)/shard_map/ppermute | solution.py:91
  47.1 13.0 %collective-permute-start.18 = (bf16[144,640]{1,0:T(8,128)(2,1)S(1)}, bf16[144,640]{1,0:T(8,128)(2,1)S(1)}, u32[]{:S(2)}, u32[]{:S(2)}) collective-permute-start(bf16[144,640]{1,0:T(8,128)(2,1)S(1)} %get-tuple-element.75), channel_id=1, source_target_pairs={{0,16},{2,18},{4,20},{6,22},{8,24},{10,26},{12,28},{14,30},{16,0},... | collective-permute-start | bytes 552968 | tf_op jit(solution)/shard_map/ppermute | solution.py:91
  50.8 5.5 %collective-permute-start.20 = (bf16[96,640]{1,0:T(8,128)(2,1)S(1)}, bf16[96,640]{1,0:T(8,128)(2,1)S(1)}, u32[]{:S(2)}, u32[]{:S(2)}) collective-permute-start(bf16[96,640]{1,0:T(8,128)(2,1)S(1)} %get-tuple-element.77), channel_id=1, source_target_pairs={{0,8},{2,10},{4,12},{6,14},{8,0},{10,2},{12,4},{14,6},{16,24},{18,... | collective-permute-start | bytes 368648 | tf_op jit(solution)/shard_map/ppermute | solution.py:91
  52.5 9.2 %collective-permute-start.22 = (bf16[64,640]{1,0:T(8,128)(2,1)S(1)}, bf16[64,640]{1,0:T(8,128)(2,1)S(1)}, u32[]{:S(2)}, u32[]{:S(2)}) collective-permute-start(bf16[64,640]{1,0:T(8,128)(2,1)S(1)} %get-tuple-element.81), channel_id=1, source_target_pairs={{0,16},{2,18},{4,20},{6,22},{8,24},{10,26},{12,28},{14,30},{16,0},... | collective-permute-start | bytes 245768 | tf_op jit(solution)/shard_map/ppermute | solution.py:91
  56.3 6.0 %collective-permute-start.23 = (bf16[48,640]{1,0:T(8,128)(2,1)S(1)}, bf16[48,640]{1,0:T(8,128)(2,1)S(1)}, u32[]{:S(2)}, u32[]{:S(2)}) collective-permute-start(bf16[48,640]{1,0:T(8,128)(2,1)S(1)} %get-tuple-element.82), channel_id=1, source_target_pairs={{0,16},{2,18},{4,20},{6,22},{8,24},{10,26},{12,28},{14,30},{16,0},... | collective-permute-start | bytes 184328 | tf_op jit(solution)/shard_map/ppermute | solution.py:91
